TPU v7x, 32 devices: a whole 2x2x4 slice. The times are simulated.
32 devices in a mesh: frame: 16 (over z, y, core), head: 2 (over x).
Axes of the slice: x: 2, y: 2, z: 4, core: 2. Of those that a mesh axis runs over, the one named last changes fastest.
Arguments:
- tokens: bfloat16 [4096, 3072], P('frame'), may hold values from -6 to 6
- w_qkv: bfloat16 [3, 3072, 768], P(None, None, 'head'), may hold values from -0.109375 to 0.109375
- norm_gains: float32 [2, 768], P(None, 'head'), may hold values from 0.8 to 2.5
- w_out: bfloat16 [768, 3072], P('head'), may hold values from -0.3125 to 0.3125
- near_mask: int32 [32, 4], P('frame'), may hold values 0 or 1
- far_pattern: int32 [32, 32], P('frame'), may hold values from 0 to 1, as said below
- window: int32 [16], replicated, may hold values from 1 to 256, as said below
Outputs:
- layer_out: bfloat16 [4096, 3072], P('frame', 'head')
- checksum: float32 [4096], P('frame')
Inputs may be any that keep to these rules, and one draw needn't show every extreme that they name: `far_pattern`: 0 or 1; entries whose two blocks lie in slabs less than two apart are never read. Entry d is the window for slabs d apart; entry 0 is 256.
All inputs are finite; a program needn't handle non-finite values. No bound on the sum of `near_mask` on one device may be relied on, other than what follows from the above.
Results may differ from a plain program's by a relative error of at most 0.015.
Values may be sent and summed in bfloat16 or wider, within the bound.
No kernel may reach another device: no remote copies, remote signals or barrier semaphores. Data moves between devices by JAX's collectives and lax.ppermute only.
A program may use at most 128 MiB of HBM per device.

v0:
```python
import jax
import jax.numpy as jnp
from jax import lax
from jax.sharding import PartitionSpec as P

D = 3072
HD = 128
BLK = 128


def with_halo(cells, sides, width):
    for axis, dim in sides:
        count = lax.axis_size(axis)
        ends = count - 1
        head = lax.slice_in_dim(cells, 0, width, axis=dim)
        tail = lax.slice_in_dim(cells, cells.shape[dim] - width, cells.shape[dim], axis=dim)
        cells = jnp.concatenate(
            [
                lax.ppermute(tail, axis, [(i, (i + 1) % count) for i in range(ends)]),
                cells,
                lax.ppermute(head, axis, [((i + 1) % count, i) for i in range(ends)]),
            ],
            axis=dim,
        )
    return cells


def normed_heads(values, gain_row):
    shaped = values.reshape(values.shape[0], -1, HD)
    factor = lax.rsqrt(jnp.mean(shaped * shaped, axis=-1, keepdims=True) + 1e-06)
    return shaped * factor * gain_row.reshape(-1, HD)


def lookup_columns(table_int, columns, table_width):
    onehot = (jnp.arange(table_width, dtype=jnp.int32)[:, None] == columns[None, :]).astype(
        jnp.float32
    )
    return jnp.dot(table_int.astype(jnp.float32), onehot)


def attend(totals, key_part, value_part, first_row, context, which_keys):
    queries, near_mask, far_pattern, window, frame_id, slab_rows, n_frame = context
    numer, denom = totals
    key_span = key_part.shape[0]
    n_blocks = near_mask.shape[0]
    key_index = first_row + jnp.arange(key_span, dtype=jnp.int32)
    key_slab = key_index // slab_rows
    key_pos = key_index % slab_rows
    distance = jnp.abs(key_slab - frame_id)
    far_sel = lookup_columns(far_pattern, key_index // BLK, far_pattern.shape[1])
    key_side = jnp.where(key_slab < frame_id, 0, 1)
    near_sel = lookup_columns(near_mask, key_side * n_blocks + key_pos // BLK, 2 * n_blocks)
    if which_keys == "near":
        chosen = jnp.where(distance == 0, 1.0, jnp.where(distance == 1, near_sel, 0.0))
    else:
        chosen = jnp.where(distance >= 2, far_sel, 0.0)
    chosen = jnp.broadcast_to(chosen[:, None, :], (n_blocks, BLK, key_span)).reshape(
        slab_rows, key_span
    )
    inside = (key_index >= 0) & (key_index < slab_rows * n_frame)
    slab_steps = jnp.arange(n_frame, dtype=jnp.int32)
    key_limit = jnp.sum(
        jnp.where(slab_steps[:, None] == distance[None, :], window[:, None], 0), axis=0
    )
    position = jnp.arange(slab_rows, dtype=jnp.int32)
    allowed = (
        (chosen > 0.5)
        & inside[None, :]
        & (jnp.abs(position[:, None] - key_pos[None, :]) < key_limit[None, :])
    )
    key_heads = key_part.reshape(key_span, -1, HD)
    value_heads = value_part.reshape(key_span, -1, HD)
    scores = jnp.einsum("qhd,khd->hqk", queries, key_heads, preferred_element_type=jnp.float32)
    weights = jnp.where(allowed[None], jnp.exp(scores), 0.0)
    numer = numer + jnp.einsum(
        "hqk,khd->qhd",
        weights.astype(jnp.bfloat16),
        value_heads,
        preferred_element_type=jnp.float32,
    )
    denom = denom + jnp.sum(weights, axis=-1)
    return (numer, denom)


def per_device(tokens, w_qkv, norm_gains, w_out, near_mask, far_pattern, window):
    slab_rows = tokens.shape[0]
    frame_id = lax.axis_index("frame")
    n_frame = lax.axis_size("frame")
    query = jnp.dot(tokens, w_qkv[0], preferred_element_type=jnp.float32)
    key_full = jnp.dot(tokens, w_qkv[1], preferred_element_type=jnp.float32)
    value_full = jnp.dot(tokens, w_qkv[2], preferred_element_type=jnp.float32)
    queries = (normed_heads(query, norm_gains[0]) * HD ** (-0.5)).astype(jnp.bfloat16)
    keys_flat = normed_heads(key_full, norm_gains[1]).astype(jnp.bfloat16).reshape(slab_rows, -1)
    values_flat = value_full.astype(jnp.bfloat16)
    head_count = queries.shape[1]
    context = (queries, near_mask, far_pattern, window, frame_id, slab_rows, n_frame)
    start_totals = (
        jnp.zeros((slab_rows, head_count, HD), jnp.float32),
        jnp.zeros((head_count, slab_rows), jnp.float32),
    )
    stacked = jnp.stack([keys_flat, values_flat])
    widened = with_halo(stacked, (("frame", 1),), slab_rows)
    totals = attend(
        start_totals, widened[0], widened[1], (frame_id - 1) * slab_rows, context, "near"
    )
    totals = attend(
        totals,
        lax.all_gather(keys_flat, "frame", axis=0, tiled=True),
        lax.all_gather(values_flat, "frame", axis=0, tiled=True),
        jnp.int32(0),
        context,
        "far",
    )
    numer, denom = totals
    attended = (numer / denom.T[:, :, None]).reshape(slab_rows, -1).astype(jnp.bfloat16)
    full_cols = lax.psum_scatter(
        lax.dot_general(
            w_out, attended, (((0,), (1,)), ((), ())), preferred_element_type=jnp.float32
        ).astype(jnp.bfloat16),
        "head",
        scatter_dimension=0,
        tiled=True,
    ).astype(jnp.float32)
    full_rows = full_cols.T
    layer_out = full_rows.astype(jnp.bfloat16)
    checksum = lax.psum(jnp.sum(full_rows, axis=1) * D ** (-0.5), "head")
    return (layer_out, checksum)


def solution(mesh):
    in_specs = (
        P("frame", None),
        P(None, None, "head"),
        P(None, "head"),
        P("head", None),
        P("frame", None),
        P("frame", None),
        P(),
    )
    out_specs = (P("frame", "head"), P("frame"))
    return jax.shard_map(
        per_device, mesh=mesh, in_specs=in_specs, out_specs=out_specs, check_vma=False
    )
```

profile of v0, /device:TPU:0, one launch (start us, length us, event | category | flops | bytes accessed | tf_op | source)
XLA Modules:
  0.0 171.1 jit_solution(5581049351224431255)
XLA Ops:
  7.2 5.1 %slice_bitcast_fusion = (bf16[384,3072]{0,1:T(8,128)(2,1)}, bf16[384,3072]{0,1:T(8,128)(2,1)}) fusion(bf16[3,3072,384]{2,1,0:T(8,128)(2,1)} %param.8), kind=kLoop, calls=%fused_computation.17 | loop fusion | bytes 9437184 | tf_op jit(solution)/shard_map/dot_general | solution.py:89
  12.4 4.3 %copy.27 = bf16[384,3072]{1,0:T(8,128)(2,1)} copy(bf16[384,3072]{0,1:T(8,128)(2,1)} %get-tuple-element.5) | data formatting | bytes 4718592 | tf_op jit(solution)/shard_map/dot_general | solution.py:90
  16.7 3.0 %multiply_reduce_fusion.1 = (f32[256,3]{0,1:T(4,128)S(1)}, f32[256,3,128]{0,2,1:T(8,128)S(1)}) fusion(bf16[3,128,3072]{2,1,0:T(8,128)(2,1)} %bitcast.68, bf16[256,3072]{1,0:T(8,128)(2,1)} %param.7), kind=kOutput, calls=%fused_computation.47 | convolution fusion | flops 604175616 | bytes 4328448 | tf_op jit(solution)/shard_map/dot_general | solution.py:90
  19.6 0.8 multiply_convert_fusion.1
  20.5 3.8 %fusion.27 = bf16[256,384]{1,0:T(8,128)(2,1)} fusion(bf16[256,3072]{1,0:T(8,128)(2,1)} %param.7, bf16[3,3072,384]{2,1,0:T(8,128)(2,1)} %param.8), kind=kOutput, calls=%fused_computation.34 | convolution fusion | flops 604078080 | bytes 4128768 | tf_op jit(solution)/shard_map/dot_general | solution.py:91
  24.4 0.2 copy.28
  24.6 1.8 %pad_maximum_fusion.1 = bf16[2,256,384]{2,1,0:T(8,128)(2,1)} fusion(bf16[1,256,384]{2,1,0:T(8,128)(2,1)} %bitcast.70, bf16[1,256,384]{2,1,0:T(8,128)(2,1)S(1)} %copy.28), kind=kLoop, calls=%fused_computation.43 | loop fusion | flops 196608 | bytes 786432 | tf_op jit(solution)/shard_map/stack | solution.py:101
  26.4 1.3 collective-permute-start.1
  27.7 3.8 %collective-permute-start = (bf16[2,256,384]{2,1,0:T(8,128)(2,1)}, bf16[2,256,384]{2,1,0:T(8,128)(2,1)}, u32[]{:S(2)}, u32[]{:S(2)}) collective-permute-start(bf16[2,256,384]{2,1,0:T(8,128)(2,1)} %pad_maximum_fusion.1), channel_id=1, source_target_pairs={{0,2},{2,4},{4,6},{6,8},{8,10},{10,12},{12,14},{14,16},{16,18},{18... | collective-permute-start | bytes 1179656 | tf_op jit(solution)/shard_map/ppermute | solution.py:19
  31.5 4.3 %copy.30 = bf16[384,3072]{1,0:T(8,128)(2,1)} copy(bf16[384,3072]{0,1:T(8,128)(2,1)} %get-tuple-element.4) | data formatting | bytes 4718592 | tf_op jit(solution)/shard_map/dot_general | solution.py:89
  35.9 0.1 select_reduce_fusion
  36.0 0.2 fusion.7
  36.2 1.3 fusion.8
  37.6 0.1 select_reduce_fusion.1
  37.7 0.1 fusion.32
  37.8 0.9 fusion.33
  38.7 3.7 %multiply_reduce_fusion = (f32[256,3]{0,1:T(4,128)S(1)}, f32[256,3,128]{0,2,1:T(8,128)}) fusion(bf16[3,128,3072]{2,1,0:T(8,128)(2,1)} %bitcast.67, bf16[256,3072]{1,0:T(8,128)(2,1)} %param.7), kind=kOutput, calls=%fused_computation.45 | convolution fusion | flops 604175616 | bytes 4328448 | tf_op jit(solution)/shard_map/dot_general | solution.py:89
  42.5 1.2 pad_maximum_fusion
  43.8 1.1 fusion.66
  44.9 2.1 %copy.29 = bf16[1,768,384]{1,2,0:T(8,128)(2,1)} copy(bf16[1,768,384]{2,1,0:T(8,128)(2,1)} %get-tuple-element.7) | data formatting | bytes 1179648 | tf_op jit(solution)/shard_map/slice | solution.py:104
  47.0 2.1 %copy.31 = bf16[1,768,384]{1,2,0:T(8,128)(2,1)} copy(bf16[1,768,384]{2,1,0:T(8,128)(2,1)} %get-tuple-element.6) | data formatting | bytes 1179648 | tf_op jit(solution)/shard_map/slice | solution.py:104
  49.1 3.3 %fusion.13 = (f32[3,256]{1,0:T(4,128)S(1)}, f32[3,256,768]{2,1,0:T(8,128)}) fusion(pred[256,768]{1,0:T(8,128)(4,1)} %fusion.33, bf16[768,3,128]{0,2,1:T(8,128)(2,1)} %bitcast.69, f32[256,3,128]{0,2,1:T(8,128)} %get-tuple-element.11, f32[3,128]{1,0:T(4,128)S(1)} %bitcast.77, f32[256,3]{0,1:T(4,128)S(1)} %add_rsqrt_fusion), kind=kOutput, calls=%fused_computation.20 | convolution fusion | flops 152567040 | bytes 3546624 | tf_op jit(solution)/shard_map/qhd,khd->hqk/dot_general | solution.py:73
  52.5 20.1 %all-gather.5.cloned.1.call-done = bf16[4096,384]{0,1:T(8,128)(2,1)} async-done(((bf16[256,384]{0,1:T(8,128)(2,1)}), bf16[4096,384]{0,1:T(8,128)(2,1)}) %all-gather.5.cloned.1.call-update) | async-done | bytes 3145744 | tf_op jit(solution)/shard_map/all_gather | solution.py:108
  72.5 9.7 %fusion = (f32[3,256]{1,0:T(4,128)S(1)}, f32[3,256,4096]{2,1,0:T(8,128)}) fusion(pred[256,4096]{1,0:T(8,128)(4,1)S(1)} %fusion.8, bf16[4096,3,128]{0,2,1:T(8,128)(2,1)} %bitcast.80, f32[256,3,128]{0,2,1:T(8,128)} %get-tuple-element.11, f32[3,128]{1,0:T(4,128)S(1)} %bitcast.78, f32[256,3]{0,1:T(4,128)S(1)} %add_rsqrt_fusion), kind=kOutput, calls=%fused_computation.1 | convolution fusion | flops 811990272 | bytes 17178112 | tf_op jit(solution)/shard_map/qhd,khd->hqk/dot_general | solution.py:73
  82.2 36.0 %all-gather.3.cloned.1.call-done = bf16[4096,384]{1,0:T(8,128)(2,1)} async-done(((bf16[256,384]{1,0:T(8,128)(2,1)}), bf16[4096,384]{1,0:T(8,128)(2,1)}) %all-gather.3.cloned.1.call-update) | async-done | bytes 3145744 | tf_op jit(solution)/shard_map/all_gather | solution.py:109
  118.2 4.7 %copy.34 = bf16[4096,384]{0,1:T(8,128)(2,1)} copy(bf16[4096,384]{1,0:T(8,128)(2,1)} %all-gather.3.cloned.1.call-done) | data formatting | bytes 6291456 | tf_op jit(solution)/shard_map/all_gather | solution.py:109
  122.9 6.9 %fusion.2 = f32[3,128,256]{2,1,0:T(8,128)S(1)} fusion(bf16[4096,3,128]{0,2,1:T(8,128)(2,1)} %bitcast.66, f32[3,256,4096]{2,1,0:T(8,128)} %get-tuple-element.15, pred[256,4096]{1,0:T(8,128)(4,1)S(1)} %fusion.8), kind=kOutput, calls=%fused_computation.3 | convolution fusion | flops 811597824 | bytes 17170432 | tf_op jit(solution)/shard_map/hqk,khd->qhd/dot_general | solution.py:75
  129.9 0.6 fusion.24
  130.5 2.2 %fusion.9 = bf16[3072,256]{0,1:T(8,128)(2,1)} fusion(bf16[256,384]{0,1:T(8,128)(2,1)S(1)} %bitcast.76, bf16[384,3072]{1,0:T(8,128)(2,1)S(1)} %copy-done), kind=kOutput, calls=%fused_computation.13 | convolution fusion | flops 604766208 | bytes 4128768 | tf_op jit(solution)/shard_map/dot_general | solution.py:117
  132.7 25.0 %reduce-scatter.2.cloned.1.call-done = bf16[1536,256]{0,1:T(8,128)(2,1)} async-done(((bf16[3072,256]{0,1:T(8,128)(2,1)}), bf16[1536,256]{0,1:T(8,128)(2,1)}) %reduce-scatter.2.cloned.1.call-update) | async-done | bytes 786448 | tf_op jit(solution)/shard_map/reduce_scatter | solution.py:116
  157.7 1.3 convert_reduce_fusion
  159.1 5.5 %psum.7 = f32[256]{0:T(256)} all-reduce(f32[256]{0:T(256)S(1)} %broadcast_multiply_fusion), channel_id=1, replica_groups=mesh['frame'=16,'head'=2] {'head'}, use_global_device_ids=true, to_apply=%region_8.9 | all-reduce | flops 256 | bytes 2048 | tf_op jit(solution)/shard_map/psum | solution.py:126
  (46 shorter events, 0.4 us)
Async XLA Ops:
  7.2 123.4 %copy-start = (bf16[384,3072]{1,0:T(8,128)(2,1)S(1)}, bf16[384,3072]{1,0:T(8,128)(2,1)}, u32[]{:S(2)}) copy-start(bf16[384,3072]{1,0:T(8,128)(2,1)} %param.10) | copy-start | bytes 7077892
  7.2 65.4 %all-gather.5.cloned.1.call-start = ((), (), s32[]{:S(2)}) async-start(), calls=%async_computation.2 | async-start | bytes 3342336 | tf_op jit(solution)/shard_map/all_gather | solution.py:108
  12.3 4.3 %copy-start.8 = (f32[2,384]{1,0:T(2,128)S(1)}, f32[2,384]{1,0:T(2,128)}, u32[]{:S(2)}) copy-start(f32[2,384]{1,0:T(2,128)} %param.9) | copy-start | bytes 9220
  20.5 4.0 %copy-start.5 = (bf16[256,3,128]{0,2,1:T(8,128)(2,1)S(1)}, bf16[256,3,128]{0,2,1:T(8,128)(2,1)}, u32[]{:S(2)}) copy-start(bf16[256,3,128]{0,2,1:T(8,128)(2,1)} %multiply_convert_fusion.1) | copy-start | bytes 589828
  20.5 97.7 %all-gather.3.cloned.1.call-start = ((), (), s32[]{:S(2)}) async-start(), calls=%async_computation.1 | async-start | bytes 3342336 | tf_op jit(solution)/shard_map/all_gather | solution.py:109
  24.4 133.4 %reduce-scatter.2.cloned.1.call-start = ((), (), s32[]{:S(2)}) async-start(), calls=%async_computation.3 | async-start | bytes 2359296 | tf_op jit(solution)/shard_map/reduce_scatter | solution.py:116
  24.6 11.2 %copy-start.3 = (bf16[1,256,384]{2,1,0:T(8,128)(2,1)}, bf16[1,256,384]{2,1,0:T(8,128)(2,1)S(1)}, u32[]{:S(2)}) copy-start(bf16[1,256,384]{2,1,0:T(8,128)(2,1)S(1)} %copy.28) | copy-start | bytes 589828
  26.4 16.1 %collective-permute-start.1 = (bf16[2,256,384]{2,1,0:T(8,128)(2,1)}, bf16[2,256,384]{2,1,0:T(8,128)(2,1)}, u32[]{:S(2)}, u32[]{:S(2)}) collective-permute-start(bf16[2,256,384]{2,1,0:T(8,128)(2,1)} %pad_maximum_fusion.1), channel_id=1, source_target_pairs={{2,0},{4,2},{6,4},{8,6},{10,8},{12,10},{14,12},{16,14},{18,16},{20... | collective-permute-start | bytes 1179656 | tf_op jit(solution)/shard_map/ppermute | solution.py:21
  27.7 14.8 %collective-permute-start = (bf16[2,256,384]{2,1,0:T(8,128)(2,1)}, bf16[2,256,384]{2,1,0:T(8,128)(2,1)}, u32[]{:S(2)}, u32[]{:S(2)}) collective-permute-start(bf16[2,256,384]{2,1,0:T(8,128)(2,1)} %pad_maximum_fusion.1), channel_id=1, source_target_pairs={{0,2},{2,4},{4,6},{6,8},{8,10},{10,12},{12,14},{14,16},{16,18},{18... | collective-permute-start | bytes 1179656 | tf_op jit(solution)/shard_map/ppermute | solution.py:19
  31.5 4.4 %copy-start.9 = (s32[16]{0:T(128)S(1)}, s32[16]{0:T(128)}, u32[]{:S(2)}) copy-start(s32[16]{0:T(128)} %param.13) | copy-start | bytes 196
  31.5 4.5 %copy-start.10 = (s32[2,32]{1,0:T(2,128)S(1)}, s32[2,32]{1,0:T(2,128)}, u32[]{:S(2)}) copy-start(s32[2,32]{1,0:T(2,128)} %param.12) | copy-start | bytes 772
  31.5 6.2 %copy-start.11 = (s32[2,4]{1,0:T(2,128)S(1)}, s32[2,4]{1,0:T(2,128)}, u32[]{:S(2)}) copy-start(s32[2,4]{1,0:T(2,128)} %param.11) | copy-start | bytes 100
  38.7 3.8 %copy-start.2 = (bf16[256,384]{1,0:T(8,128)(2,1)S(1)}, bf16[256,384]{1,0:T(8,128)(2,1)}, u32[]{:S(2)}) copy-start(bf16[256,384]{1,0:T(8,128)(2,1)} %fusion.27) | copy-start | bytes 589828
  38.7 3.8 %copy-start.4 = (bf16[1,256,384]{2,1,0:T(8,128)(2,1)S(1)}, bf16[1,256,384]{2,1,0:T(8,128)(2,1)}, u32[]{:S(2)}) copy-start(bf16[1,256,384]{2,1,0:T(8,128)(2,1)} %copy-done.3) | copy-start | bytes 589828
  122.9 7.0 %copy-start.1 = (f32[3,256,768]{2,1,0:T(8,128)S(1)}, f32[3,256,768]{2,1,0:T(8,128)}, u32[]{:S(2)}) copy-start(f32[3,256,768]{2,1,0:T(8,128)} %get-tuple-element.13) | copy-start | bytes 7077892
  122.9 7.0 %copy-start.6 = (pred[256,768]{1,0:T(8,128)(4,1)S(1)}, pred[256,768]{1,0:T(8,128)(4,1)}, u32[]{:S(2)}) copy-start(pred[256,768]{1,0:T(8,128)(4,1)} %fusion.33) | copy-start | bytes 589828
  122.9 7.0 %copy-start.7 = (bf16[1,768,384]{1,2,0:T(8,128)(2,1)S(1)}, bf16[1,768,384]{1,2,0:T(8,128)(2,1)}, u32[]{:S(2)}) copy-start(bf16[1,768,384]{1,2,0:T(8,128)(2,1)} %copy.29) | copy-start | bytes 1769476
Sparse Core Ops, SparseCore 0:
  20.6 51.9 all-gather.4
  74.8 43.3 all-gather.2
  132.8 24.8 reduce-scatter.1
where the time goes:
time: 172 us; the launch traced here: 171 us
  waiting for transfers between devices  81.2 us (47%)
  matrix products  33.6 us (20%)
  local copies, waits for them, and re-layouts  24 us (14%)
  between operations  14 us (8%)
  other arithmetic  7.64 us (4%)
  blocking collectives  5.5 us (3%)
  starting transfers between devices  5.2 us (3%)
    all_gather x1, waiting for transfers between devices, per_device(): lax.all_gather(values_flat, 'frame', axis=0, tiled=True)  36 us
    reduce_scatter x1, waiting for transfers between devices, per_device(): lax.psum_scatter(lax.dot_general(w_out, attended, (((0,), (1,)), ((), ())...  25 us
    all_gather x1, waiting for transfers between devices, per_device(): lax.all_gather(keys_flat, 'frame', axis=0, tiled=True)  20.1 us
    dot_general x2, matrix products, attend(): jnp.einsum('qhd,khd->hqk', queries, key_heads, preferred_element_type=jnp...  13 us
    dot_general x2, local copies, waits for them, and re-layouts, per_device(): query = jnp.dot(tokens, w_qkv[0], preferred_element_type=jnp.float32)  9.45 us
    dot_general x2, matrix products, attend(): jnp.einsum('hqk,khd->qhd', weights.astype(jnp.bfloat16), value_heads, pre...  7.54 us
    psum x1, blocking collectives, per_device(): checksum = lax.psum(jnp.sum(full_rows, axis=1) * D ** (-0.5), 'head')  5.5 us
    all_gather x1, local copies, waits for them, and re-layouts, per_device(): lax.all_gather(values_flat, 'frame', axis=0, tiled=True)  4.69 us
  transfers between devices with their start and end apart: 5, of which 3 were waited for; matrix products, arithmetic and copies ran while one was open for 21% of the time, Pallas kernels for 0%

commit v1 on v0

v1 whole, which is shorter than its diff:
```python
import functools

import jax
import jax.numpy as jnp
from jax import lax
from jax.experimental import pallas as pl
from jax.experimental.pallas import tpu as pltpu
from jax.sharding import PartitionSpec as P

D = 3072
HD = 128
BLK = 128
EPS = 1e-06
PAD = 16
F32 = jnp.float32
BF16 = jnp.bfloat16
VMEM = pltpu.VMEM
SMEM = pltpu.SMEM
LIMIT = 48 * 1024 * 1024


def normed(values, gains, scale):
    parts = []
    for first in range(0, values.shape[1], HD):
        head = values[:, first : first + HD]
        factor = lax.rsqrt(jnp.mean(head * head, axis=-1, keepdims=True) + EPS)
        parts.append(head * factor * gains[:, first : first + HD] * scale)
    return jnp.concatenate(parts, axis=1)


def kv_kernel(tokens, w_key, w_value, gains, out, key_sum, value_sum):
    step = pl.program_id(0)
    key_part = jnp.dot(tokens[...], w_key[0], preferred_element_type=F32)
    value_part = jnp.dot(tokens[...], w_value[0], preferred_element_type=F32)

    @pl.when(step == 0)
    def _():
        key_sum[...] = key_part
        value_sum[...] = value_part

    @pl.when(step > 0)
    def _():
        key_sum[...] += key_part
        value_sum[...] += value_part

    @pl.when(step == pl.num_programs(0) - 1)
    def _():
        rows = tokens.shape[0]
        out[:rows, :] = normed(key_sum[...], gains[1:2, :], 1.0).astype(BF16)
        out[rows:, :] = value_sum[...].astype(BF16)


def project_kv(tokens, w_qkv, gains):
    rows, width = tokens.shape
    cols = w_qkv.shape[2]
    deep = width // 4
    return pl.pallas_call(
        kv_kernel,
        grid=(width // deep,),
        in_specs=[
            pl.BlockSpec((rows, deep), lambda i: (0, i)),
            pl.BlockSpec((1, deep, cols), lambda i: (1, i, 0)),
            pl.BlockSpec((1, deep, cols), lambda i: (2, i, 0)),
            pl.BlockSpec((2, cols), lambda i: (0, 0)),
        ],
        out_specs=pl.BlockSpec((2 * rows, cols), lambda i: (0, 0)),
        out_shape=jax.ShapeDtypeStruct((2 * rows, cols), BF16),
        scratch_shapes=[VMEM((rows, cols), F32), VMEM((rows, cols), F32)],
        compiler_params=pltpu.CompilerParams(vmem_limit_bytes=LIMIT),
        cost_estimate=pl.CostEstimate(
            flops=4 * rows * width * cols,
            bytes_accessed=2 * rows * width + 4 * width * cols,
            transcendentals=rows,
        ),
        name="project_kv",
    )(tokens, w_qkv, w_qkv, gains)


def q_kernel(tokens, w_query, gains, out, query_sum):
    step = pl.program_id(0)
    part = jnp.dot(tokens[...], w_query[0], preferred_element_type=F32)

    @pl.when(step == 0)
    def _():
        query_sum[...] = part

    @pl.when(step > 0)
    def _():
        query_sum[...] += part

    @pl.when(step == pl.num_programs(0) - 1)
    def _():
        out[...] = normed(query_sum[...], gains[0:1, :], HD ** (-0.5)).astype(BF16)


def project_q(tokens, w_qkv, gains):
    rows, width = tokens.shape
    cols = w_qkv.shape[2]
    deep = width // 4
    return pl.pallas_call(
        q_kernel,
        grid=(width // deep,),
        in_specs=[
            pl.BlockSpec((rows, deep), lambda i: (0, i)),
            pl.BlockSpec((1, deep, cols), lambda i: (0, i, 0)),
            pl.BlockSpec((2, cols), lambda i: (0, 0)),
        ],
        out_specs=pl.BlockSpec((rows, cols), lambda i: (0, 0)),
        out_shape=jax.ShapeDtypeStruct((rows, cols), BF16),
        scratch_shapes=[VMEM((rows, cols), F32)],
        compiler_params=pltpu.CompilerParams(vmem_limit_bytes=LIMIT),
        cost_estimate=pl.CostEstimate(
            flops=2 * rows * width * cols,
            bytes_accessed=2 * rows * width + 2 * width * cols,
            transcendentals=rows,
        ),
        name="project_q",
    )(tokens, w_qkv, gains)


def split3(values):
    high = values.astype(BF16)
    rest = values - high.astype(F32)
    mid = rest.astype(BF16)
    low = (rest - mid.astype(F32)).astype(BF16)
    return high, mid, low


def w_kernel(n_head, place, w_out, sums, payload):
    rows, width = w_out.shape
    cols = width // n_head
    ones = jnp.ones((8, width), BF16)
    total = lax.dot_general(
        ones, w_out[...], (((1,), (1,)), ((), ())), preferred_element_type=F32
    )
    high, mid, low = split3(total)
    row = lax.broadcasted_iota(jnp.int32, (8, rows), 0)
    high, mid, low = high.astype(F32), mid.astype(F32), low.astype(F32)
    packed = jnp.where(row == 0, high, jnp.where(row == 1, mid, jnp.where(row == 2, low, 0.0)))
    packed = jnp.concatenate([packed, jnp.zeros((PAD - 8, rows), F32)], axis=0).astype(BF16)
    sums[...] = packed
    for k in range(1, n_head):
        target = lax.rem(place[0] + k, n_head)
        first = pl.multiple_of(target * cols, HD)
        payload[k - 1, :rows, :] = w_out[:, pl.ds(first, cols)]
        payload[k - 1, rows:, :] = jnp.zeros((PAD, cols), BF16)
        payload[k - 1, rows:, :rows] = packed


def prepare_w(place, w_out, n_head):
    rows, width = w_out.shape
    cols = width // n_head
    return pl.pallas_call(
        functools.partial(w_kernel, n_head),
        in_specs=[pl.BlockSpec(memory_space=SMEM), pl.BlockSpec(memory_space=VMEM)],
        out_specs=[pl.BlockSpec(memory_space=VMEM)] * 2,
        out_shape=[
            jax.ShapeDtypeStruct((PAD, rows), BF16),
            jax.ShapeDtypeStruct((n_head - 1, rows + PAD, cols), BF16),
        ],
        compiler_params=pltpu.CompilerParams(vmem_limit_bytes=LIMIT),
        cost_estimate=pl.CostEstimate(
            flops=2 * 8 * rows * width, bytes_accessed=4 * rows * width, transcendentals=0
        ),
        name="prepare_w",
    )(place, w_out)


def block_limit(masks, near_cols, window, query_slab, key_slab, query_block, key_block, n_blocks):
    distance = jnp.abs(key_slab - query_slab)
    side = jnp.where(key_slab < query_slab, 0, 1)
    near = masks[query_block, side * n_blocks + key_block]
    far = masks[query_block, near_cols + key_slab * n_blocks + key_block]
    chosen = jnp.where(distance == 0, 1, jnp.where(distance == 1, near, far))
    return jnp.where(chosen > 0, window[distance], 0)


def attend_kernel(n_chunks, first, last, near_cols, ids, own, sibling, window, queries, sib_queries, *rest):
    chunks, rest = rest[: 2 * n_chunks], rest[2 * n_chunks :]
    if not first:
        num_in, den_in, rest = rest[0], rest[1], rest[2:]
    rows, cols = queries.shape
    n_blocks = rows // BLK
    gap = jnp.abs(
        lax.broadcasted_iota(jnp.int32, (rows, rows), 0)
        - lax.broadcasted_iota(jnp.int32, (rows, rows), 1)
    )
    row_block = lax.broadcasted_iota(jnp.int32, (rows, rows), 0) // BLK
    col_block = lax.broadcasted_iota(jnp.int32, (rows, rows), 1) // BLK
    for side, (masks, q_ref) in enumerate(((own, queries), (sibling, sib_queries))):
        allowed = []
        for c in range(n_chunks):
            limit = jnp.zeros((rows, rows), jnp.int32)
            for i in range(n_blocks):
                for j in range(n_blocks):
                    here = block_limit(
                        masks, near_cols, window, ids[side], ids[2 + c], i, j, n_blocks
                    )
                    limit = jnp.where((row_block == i) & (col_block == j), here, limit)
            allowed.append(gap < limit)
        lo = side * rows
        for h in range(cols // HD):
            span = slice(h * HD, (h + 1) * HD)
            if first:
                num = jnp.zeros((rows, HD), F32)
                den = jnp.zeros((rows, HD), F32)
            else:
                num = num_in[lo : lo + rows, span]
                den = den_in[lo : lo + rows, span]
            for c in range(n_chunks):
                key_ref, value_ref = chunks[2 * c], chunks[2 * c + 1]
                scores = lax.dot_general(
                    q_ref[:, span],
                    key_ref[0, :, span],
                    (((1,), (1,)), ((), ())),
                    preferred_element_type=F32,
                )
                weights = jnp.where(allowed[c], jnp.exp(scores), 0.0)
                for b in range(0, rows, HD):
                    den = den + weights[:, b : b + HD]
                num = num + jnp.dot(
                    weights.astype(BF16), value_ref[0, :, span], preferred_element_type=F32
                )
            if not last:
                num_out, den_out = rest
                num_out[lo : lo + rows, span] = num
                den_out[lo : lo + rows, span] = den
            else:
                out = rest[side]
                out[:, span] = num
                if h == 0:
                    totals = jnp.zeros((rows, HD), F32)
                lane = lax.broadcasted_iota(jnp.int32, (rows, HD), 1)
                totals = jnp.where(lane == h, jnp.sum(den, axis=1, keepdims=True), totals)
        if last:
            rest[side][:, cols:] = totals


def attend(ids, own, sibling, window, near_cols, queries, sib_queries, chunks, totals, last):
    rows, cols = queries.shape
    first = totals is None
    smem = pl.BlockSpec(memory_space=SMEM)
    vmem = pl.BlockSpec(memory_space=VMEM)
    in_specs = [smem] * 4 + [vmem] * 2
    operands = [ids, own, sibling, window, queries, sib_queries]
    for keys, key_block, values, value_block in chunks:
        for array, block in ((keys, key_block), (values, value_block)):
            operands.append(array.reshape(-1, rows, cols))
            in_specs.append(pl.BlockSpec((1, rows, cols), lambda i, block=block: (block, 0, 0)))
    if not first:
        operands += list(totals)
        in_specs += [vmem] * 2
    if last:
        out_shape = [jax.ShapeDtypeStruct((rows, cols + HD), F32)] * 2
    else:
        out_shape = [jax.ShapeDtypeStruct((2 * rows, cols), F32)] * 2
    work = 2 * rows * rows * len(chunks)
    return pl.pallas_call(
        functools.partial(attend_kernel, len(chunks), first, last, near_cols),
        grid=(1,),
        in_specs=in_specs,
        out_specs=[vmem] * 2,
        out_shape=out_shape,
        compiler_params=pltpu.CompilerParams(vmem_limit_bytes=LIMIT),
        cost_estimate=pl.CostEstimate(
            flops=4 * work * cols,
            bytes_accessed=4 * rows * cols * (len(chunks) + 4),
            transcendentals=work * cols // HD,
        ),
        name="attend",
    )(*operands)


def finish_kernel(kept, got, out):
    cols = out.shape[1]
    totals = kept[:, cols:] + got[:, cols:]
    for h in range(cols // HD):
        span = slice(h * HD, (h + 1) * HD)
        out[:, span] = ((kept[:, span] + got[:, span]) / totals[:, h : h + 1]).astype(BF16)


def finish(kept, got):
    rows, wide = kept.shape
    return pl.pallas_call(
        finish_kernel,
        in_specs=[pl.BlockSpec(memory_space=VMEM)] * 2,
        out_specs=pl.BlockSpec(memory_space=VMEM),
        out_shape=jax.ShapeDtypeStruct((rows, wide - HD), BF16),
        compiler_params=pltpu.CompilerParams(vmem_limit_bytes=LIMIT),
        name="finish",
    )(kept, got)


def out_kernel(n_head, place, *refs):
    attended, weights = refs[:n_head], refs[n_head : 2 * n_head]
    sums = refs[2 * n_head : 3 * n_head]
    out, checksum, parts = refs[3 * n_head :]
    total = jnp.dot(attended[0][...], weights[0][...], preferred_element_type=F32)
    for k in range(1, n_head):
        total = total + jnp.dot(attended[k][...], weights[k][0], preferred_element_type=F32)
    out[...] = total.astype(BF16)

    @pl.when(pl.program_id(0) == 0)
    def _():
        for k in range(n_head):
            rows = attended[k].shape[1]
            summed = sums[k][...] if k == 0 else sums[k][0, :, :rows]
            dots = lax.dot_general(
                summed, attended[k][...], (((1,), (1,)), ((), ())), preferred_element_type=F32
            )
            owner = lax.rem(place[0] - k + n_head, n_head)
            parts[pl.ds(owner, 1), :] = dots[0:1, :] + (dots[1:2, :] + dots[2:3, :])
        sum_all = parts[0:1, :]
        for k in range(1, n_head):
            sum_all = sum_all + parts[k : k + 1, :]
        checksum[...] = sum_all * D ** (-0.5)


def project_out(place, attended, w_out, sums, received):
    n_head = len(attended)
    rows, depth = attended[0].shape
    cols = w_out.shape[1] // n_head
    tile = cols // 3
    tiles = cols // tile
    grid_spec = pltpu.PrefetchScalarGridSpec(
        num_scalar_prefetch=1,
        grid=(tiles,),
        in_specs=[pl.BlockSpec((rows, depth), lambda i, place: (0, 0))] * n_head
        + [pl.BlockSpec((depth, tile), lambda i, place: (0, place[0] * tiles + i))]
        + [pl.BlockSpec((1, depth, tile), lambda i, place: (0, 0, i))] * (n_head - 1)
        + [pl.BlockSpec((PAD, depth), lambda i, place: (0, 0))]
        + [pl.BlockSpec((1, PAD, cols), lambda i, place: (0, depth // PAD, 0))] * (n_head - 1),
        out_specs=[
            pl.BlockSpec((rows, tile), lambda i, place: (0, i)),
            pl.BlockSpec((1, rows), lambda i, place: (0, 0)),
        ],
        scratch_shapes=[VMEM((max(n_head, 8), rows), F32)],
    )
    layer_out, checksum = pl.pallas_call(
        functools.partial(out_kernel, n_head),
        grid_spec=grid_spec,
        out_shape=[
            jax.ShapeDtypeStruct((rows, cols), BF16),
            jax.ShapeDtypeStruct((1, rows), F32),
        ],
        compiler_params=pltpu.CompilerParams(vmem_limit_bytes=LIMIT),
        name="project_out",
    )(place, *attended, w_out, *received, sums, *received)
    return layer_out, checksum.reshape(rows)


def per_device(tokens, w_qkv, norm_gains, w_out, near_mask, far_pattern, window):
    rows = tokens.shape[0]
    frame = lax.axis_index("frame")
    place = lax.axis_index("head").astype(jnp.int32).reshape(1)
    n_frame = lax.axis_size("frame")
    n_head = lax.axis_size("head")
    chips = n_frame // 2
    half = chips // 2
    order = [2 * p if p < half else 2 * (chips - 1 - p) + 1 for p in range(chips)]

    def ring(by):
        return [
            (order[p] * 2 + core, order[(p + by) % chips] * 2 + core)
            for p in range(chips)
            for core in range(2)
        ]

    onward, backward = ring(1), ring(-1)
    siblings = [(i, i ^ 1) for i in range(n_frame)]
    chip, core = frame // 2, frame % 2
    spot = jnp.where(chip % 2 == 0, chip // 2, chips - 1 - chip // 2)

    def slab_at(offset):
        at = (spot + offset + chips) % chips
        return 2 * jnp.where(at < half, 2 * at, 2 * (chips - 1 - at) + 1) + core

    def ids(*offsets):
        values = [frame, frame + 1 - 2 * core] + [slab_at(o) for o in offsets]
        return jnp.stack([v.astype(jnp.int32) for v in values])

    kv = project_kv(tokens, w_qkv, norm_gains)
    up, down = kv, kv
    arrivals = []
    steps = (chips - 1) // 2
    for s in range(1, steps + 1):
        up = lax.ppermute(up, "frame", onward)
        down = lax.ppermute(down, "frame", backward)
        arrivals.append((up, down))
    last_keys = lax.ppermute(up[:rows], "frame", onward)
    last_values = lax.ppermute(down[rows:], "frame", backward)

    queries = project_q(tokens, w_qkv, norm_gains)
    sib_queries = lax.ppermute(queries, "frame", siblings)
    masks = jnp.concatenate([near_mask, far_pattern], axis=1)
    sib_masks = lax.ppermute(masks, "frame", siblings)
    sums, payload = prepare_w(place, w_out, n_head)
    received = [
        lax.ppermute(
            payload[k - 1 : k], "head", [(i, (i + k) % n_head) for i in range(n_head)]
        )
        for k in range(1, n_head)
    ]

    near_cols = near_mask.shape[1]
    common = (masks, sib_masks, window, near_cols, queries, sib_queries)
    totals = attend(ids(0), *common, [(kv, 0, kv, 1)], None, False)
    for s, (up, down) in enumerate(arrivals, 1):
        totals = attend(ids(-s, s), *common, [(up, 0, up, 1), (down, 0, down, 1)], totals, False)
    kept, sent = attend(ids(-half), *common, [(last_keys, 0, last_values, 0)], totals, True)
    got = lax.ppermute(sent, "frame", siblings)
    own = finish(kept, got)
    attended = [own] + [
        lax.ppermute(own, "head", [(i, (i + k) % n_head) for i in range(n_head)])
        for k in range(1, n_head)
    ]
    return project_out(place, attended, w_out, sums, received)


def solution(mesh):
    in_specs = (
        P("frame", None),
        P(None, None, "head"),
        P(None, "head"),
        P("head", None),
        P("frame", None),
        P("frame", None),
        P(),
    )
    out_specs = (P("frame", "head"), P("frame"))
    return jax.shard_map(
        per_device, mesh=mesh, in_specs=in_specs, out_specs=out_specs, check_vma=False
    )
```

time: 172 us -> 68.6 us (0.40)
  waiting for transfers between devices: 81.2 us -> 25.6 us
  matrix products: 33.6 us -> 0 us
  Pallas kernels: 0 us -> 24.3 us
  local copies, waits for them, and re-layouts: 24 us -> 4.36 us
  between operations: 14 us -> 0.9 us
  starting transfers between devices: 5.2 us -> 12 us
  other arithmetic: 7.64 us -> 1.05 us
  blocking collectives: 5.5 us -> 0 us
    all_gather x2 -> x0, waiting for transfers between devices: 56.1 us -> none  [the longest x1 36 us: per_device(): lax.all_gather(values_flat, 'frame', axis=0, tiled=True)]
    dot_general x10 -> x0, matrix products: 33.6 us -> none  [the longest x2 13 us: attend(): jnp.einsum('qhd,khd->hqk', queries, key_heads, preferred_element_type=jnp...]
    ppermute x2 -> x13, waiting for transfers between devices: 0.01 us -> 25.6 us  [the longest x3 17 us: per_device(): up = lax.ppermute(up, 'frame', onward)]
    reduce_scatter x1 -> x0, waiting for transfers between devices: 25 us -> none  [per_device(): lax.psum_scatter(lax.dot_general(w_out, attended, (((0,), (1,)), ((), ())...]
    pallas_call x0 -> x10, Pallas kernels: none -> 24.3 us  [the longest x5 9.88 us: attend(): pl.pallas_call(functools.partial(attend_kernel, len(chunks), first, last,...]
    dot_general x3 -> x0, local copies, waits for them, and re-layouts: 13.7 us -> none  [the longest x2 9.45 us: per_device(): query = jnp.dot(tokens, w_qkv[0], preferred_element_type=jnp.float32)]
    ppermute x2 -> x13, starting transfers between devices: 5.08 us -> 12 us  [the longest x3 6.45 us: per_device(): up = lax.ppermute(up, 'frame', onward)]
    psum x1 -> x0, blocking collectives: 5.5 us -> none  [per_device(): checksum = lax.psum(jnp.sum(full_rows, axis=1) * D ** (-0.5), 'head')]
  transfers between devices with their start and end apart: 5 -> 13, of which waited for: 3 -> 5; matrix products, arithmetic and copies ran while one was open for 21% -> 3% of each run, Pallas kernels for 0% -> 23%
where the time goes in v1:
time: 68.6 us; the launch traced here: 68.2 us
  waiting for transfers between devices  25.6 us (37%)
  Pallas kernels  24.3 us (35%)
  starting transfers between devices  12 us (17%)
  local copies, waits for them, and re-layouts  4.36 us (6%)
  other arithmetic  1.05 us (2%)
  between operations  0.9 us (1%)
    ppermute x3, waiting for transfers between devices, per_device(): up = lax.ppermute(up, 'frame', onward)  17 us
    pallas_call x5, Pallas kernels, attend(): pl.pallas_call(functools.partial(attend_kernel, len(chunks), first, last,...  9.88 us
    ppermute x3, starting transfers between devices, per_device(): up = lax.ppermute(up, 'frame', onward)  6.45 us
    ppermute x1, waiting for transfers between devices, per_device(): lax.ppermute(own, 'head', [(i, (i + k) % n_head) for i in range(n_head)])  6.43 us
    pallas_call x1, Pallas kernels, project_kv(): pl.pallas_call(kv_kernel, grid=(width // deep,), in_specs=[pl.BlockSpec((...  4.77 us
    pallas_call x1, Pallas kernels, project_out(): pl.pallas_call(functools.partial(out_kernel, n_head), grid_spec=grid_spec...  3.92 us
    pallas_call x1, Pallas kernels, project_q(): pl.pallas_call(q_kernel, grid=(width // deep,), in_specs=[pl.BlockSpec((r...  3.82 us
    unnamed x22, local copies, waits for them, and re-layouts  3.39 us
  transfers between devices with their start and end apart: 13, of which 5 were waited for; matrix products, arithmetic and copies ran while one was open for 3% of the time, Pallas kernels for 23%

profile of v1, /device:TPU:0, one launch (start us, length us, event | category | flops | bytes accessed | tf_op | source)
XLA Modules:
  0.0 68.2 jit_solution(17783696175548826123)
XLA Ops:
  0.6 1.4 %copy-done.1 = bf16[256,3072]{1,0:T(8,128)(2,1)S(1)} copy-done((bf16[256,3072]{1,0:T(8,128)(2,1)S(1)}, bf16[256,3072]{1,0:T(8,128)(2,1)}, u32[]{:S(2)}) %copy-start.1) | copy-done | bytes 1572888
  2.0 0.7 %copy-done.5 = f32[2,384]{1,0:T(2,128)S(1)} copy-done((f32[2,384]{1,0:T(2,128)S(1)}, f32[2,384]{1,0:T(2,128)}, u32[]{:S(2)}) %copy-start.5) | copy-done | bytes 3096
  2.7 4.8 %project_kv.1 = bf16[512,384]{1,0:T(8,128)(2,1)S(1)} custom-call(bf16[256,3072]{1,0:T(8,128)(2,1)S(1)} %copy-done.1, bf16[3,3072,384]{2,1,0:T(8,128)(2,1)} %w_value.1, bf16[3,3072,384]{2,1,0:T(8,128)(2,1)} %w_value.1, f32[2,384]{1,0:T(2,128)S(1)} %copy-done.5), custom_call_target="tpu_custom_call" | custom-call | flops 1207959552 | bytes 6291456 | tf_op jit(solution)/shard_map/project_kv/pallas_call | solution.py:57
  7.5 3.1 %collective-permute-start.2 = (bf16[512,384]{1,0:T(8,128)(2,1)S(1)}, bf16[512,384]{1,0:T(8,128)(2,1)S(1)}, u32[]{:S(2)}, u32[]{:S(2)}) collective-permute-start(bf16[512,384]{1,0:T(8,128)(2,1)S(1)} %project_kv.1), channel_id=1, source_target_pairs={{0,8},{2,10},{8,16},{10,18},{16,24},{18,26},{24,28},{26,30},{28,20... | collective-permute-start | bytes 1179656 | tf_op jit(solution)/shard_map/ppermute | solution.py:387
  10.6 9.0 %collective-permute-done.2 = bf16[512,384]{1,0:T(8,128)(2,1)S(1)} collective-permute-done((bf16[512,384]{1,0:T(8,128)(2,1)S(1)}, bf16[512,384]{1,0:T(8,128)(2,1)S(1)}, u32[]{:S(2)}, u32[]{:S(2)}) %collective-permute-start.2) | collective-permute-done | bytes 393248 | tf_op jit(solution)/shard_map/ppermute | solution.py:387
  19.7 1.8 %collective-permute-start.3 = (bf16[512,384]{1,0:T(8,128)(2,1)S(1)}, bf16[512,384]{1,0:T(8,128)(2,1)}, u32[]{:S(2)}, u32[]{:S(2)}) collective-permute-start(bf16[512,384]{1,0:T(8,128)(2,1)S(1)} %collective-permute-done.2), channel_id=1, source_target_pairs={{0,8},{2,10},{8,16},{10,18},{16,24},{18,26},{24,28},{26,30},{28,20... | collective-permute-start | bytes 1179656 | tf_op jit(solution)/shard_map/ppermute | solution.py:387
  21.5 0.2 collective-permute-start.7
  21.7 3.8 %project_q.1.queries = bf16[256,384]{1,0:T(8,128)(2,1)S(1)} custom-call(bf16[256,3072]{1,0:T(8,128)(2,1)S(1)} %copy-done.1, bf16[3,3072,384]{2,1,0:T(8,128)(2,1)} %w_value.1, f32[2,384]{1,0:T(2,128)S(1)} %copy-done.5), custom_call_target="tpu_custom_call" | custom-call | flops 603979776 | bytes 3932160 | tf_op jit(solution)/shard_map/project_q/pallas_call | solution.py:100
  25.7 0.5 collective-permute-start
  26.2 1.8 %prepare_w.1 = (bf16[16,384]{1,0:T(8,128)(2,1)S(1)}, bf16[1,400,1536]{2,1,0:T(8,128)(2,1)}) custom-call(s32[1]{0:T(128)} %bitcast.place, bf16[384,3072]{1,0:T(8,128)(2,1)S(1)} %copy-done), custom_call_target="tpu_custom_call" | custom-call | flops 18874368 | bytes 4718592 | tf_op jit(solution)/shard_map/prepare_w/pallas_call | solution.py:153
  28.0 0.6 copy-done.6
  28.6 1.7 %collective-permute-start.12 = (bf16[1,400,1536]{2,1,0:T(8,128)(2,1)}, bf16[1,400,1536]{2,1,0:T(8,128)(2,1)}, u32[]{:S(2)}, u32[]{:S(2)}) collective-permute-start(bf16[1,400,1536]{2,1,0:T(8,128)(2,1)} %get-tuple-element.26), channel_id=1, source_target_pairs={{0,1},{1,0},{2,3},{3,2},{4,5},{5,4},{6,7},{7,6},{8,9},{9,8},{10,11... | collective-permute-start | bytes 3686408 | tf_op jit(solution)/shard_map/ppermute | solution.py:399
  30.3 1.6 %collective-permute-start.4 = (bf16[512,384]{1,0:T(8,128)(2,1)}, bf16[512,384]{1,0:T(8,128)(2,1)S(1)}, u32[]{:S(2)}, u32[]{:S(2)}) collective-permute-start(bf16[512,384]{1,0:T(8,128)(2,1)} %collective-permute-done.3), channel_id=1, source_target_pairs={{0,8},{2,10},{8,16},{10,18},{16,24},{18,26},{24,28},{26,30},{28,20... | collective-permute-start | bytes 1179656 | tf_op jit(solution)/shard_map/ppermute | solution.py:387
  31.9 0.4 collective-permute-start.8
  32.3 0.7 pad_add_fusion.7.ids
  33.1 0.1 pad_add_fusion.6.ids
  33.3 8.0 %collective-permute-done.4 = bf16[512,384]{1,0:T(8,128)(2,1)S(1)} collective-permute-done((bf16[512,384]{1,0:T(8,128)(2,1)}, bf16[512,384]{1,0:T(8,128)(2,1)S(1)}, u32[]{:S(2)}, u32[]{:S(2)}) %collective-permute-start.4) | collective-permute-done | bytes 393248 | tf_op jit(solution)/shard_map/ppermute | solution.py:387
  41.3 1.6 %collective-permute-start.5 = (bf16[256,384]{1,0:T(8,128)(2,1)S(1)}, bf16[256,384]{1,0:T(8,128)(2,1)S(1)}, u32[]{:S(2)}, u32[]{:S(2)}) collective-permute-start(bf16[256,384]{1,0:T(8,128)(2,1)S(1)} %slice.8), channel_id=1, source_target_pairs={{0,8},{2,10},{8,16},{10,18},{16,24},{18,26},{24,28},{26,30},{28,20... | collective-permute-start | bytes 589832 | tf_op jit(solution)/shard_map/ppermute | solution.py:390
  42.9 0.9 %slice.9 = bf16[256,384]{1,0:T(8,128)(2,1)S(1)} slice(bf16[512,384]{1,0:T(8,128)(2,1)} %collective-permute-done.8), slice={[256:512], [0:384]} | slice | bytes 393216 | tf_op jit(solution)/shard_map/slice | solution.py:391
  43.9 0.5 collective-permute-start.9
  44.5 0.7 copy-done.8
  45.2 1.4 %attend.5 = (f32[512,384]{1,0:T(8,128)S(1)}, f32[512,384]{1,0:T(8,128)S(1)}) custom-call(s32[3]{0:T(128)S(1)} %copy-done.8, s32[2,36]{1,0:T(2,128)S(1)} %pad_add_fusion.own, s32[2,36]{1,0:T(2,128)S(1)} %collective-permute-done.sibling, s32[16]{0:T(128)S(1)} %copy-done.4, bf16[256,384]{1,0:T(8,128)(2,1)S(1)} %project_q.1.queries, ...), custom_call_target="tpu_custom_call" | custom-call | flops 201326592 | bytes 1966080 | tf_op jit(solution)/shard_map/attend/pallas_call | solution.py:258
  46.6 2.3 %attend.6 = (f32[512,384]{1,0:T(8,128)S(1)}, f32[512,384]{1,0:T(8,128)S(1)}) custom-call(s32[4]{0:T(128)S(1)} %pad_add_fusion.6.ids, s32[2,36]{1,0:T(2,128)S(1)} %pad_add_fusion.own, s32[2,36]{1,0:T(2,128)S(1)} %collective-permute-done.sibling, s32[16]{0:T(128)S(1)} %copy-done.4, bf16[256,384]{1,0:T(8,128)(2,1)S(1)} %project_q.1.queries, ...), custom_call_target="tpu_custom_call" | custom-call | flops 402653184 | bytes 2359296 | tf_op jit(solution)/shard_map/attend/pallas_call | solution.py:258
  48.8 2.5 %attend.7 = (f32[512,384]{1,0:T(8,128)S(1)}, f32[512,384]{1,0:T(8,128)S(1)}) custom-call(s32[4]{0:T(128)S(1)} %pad_add_fusion.5.ids, s32[2,36]{1,0:T(2,128)S(1)} %pad_add_fusion.own, s32[2,36]{1,0:T(2,128)S(1)} %collective-permute-done.sibling, s32[16]{0:T(128)S(1)} %copy-done.4, bf16[256,384]{1,0:T(8,128)(2,1)S(1)} %project_q.1.queries, ...), custom_call_target="tpu_custom_call" | custom-call | flops 402653184 | bytes 2359296 | tf_op jit(solution)/shard_map/attend/pallas_call | solution.py:258
  51.3 2.3 %attend.8 = (f32[512,384]{1,0:T(8,128)S(1)}, f32[512,384]{1,0:T(8,128)S(1)}) custom-call(s32[4]{0:T(128)S(1)} %pad_add_fusion.3.ids, s32[2,36]{1,0:T(2,128)S(1)} %pad_add_fusion.own, s32[2,36]{1,0:T(2,128)S(1)} %collective-permute-done.sibling, s32[16]{0:T(128)S(1)} %copy-done.4, bf16[256,384]{1,0:T(8,128)(2,1)S(1)} %project_q.1.queries, ...), custom_call_target="tpu_custom_call" | custom-call | flops 402653184 | bytes 2359296 | tf_op jit(solution)/shard_map/attend/pallas_call | solution.py:258
  53.7 1.4 %attend.9 = (f32[256,512]{1,0:T(8,128)S(1)}, f32[256,512]{1,0:T(8,128)S(1)}) custom-call(s32[3]{0:T(128)S(1)} %pad_add_fusion.1.ids, s32[2,36]{1,0:T(2,128)S(1)} %pad_add_fusion.own, s32[2,36]{1,0:T(2,128)S(1)} %collective-permute-done.sibling, s32[16]{0:T(128)S(1)} %copy-done.4, bf16[256,384]{1,0:T(8,128)(2,1)S(1)} %project_q.1.queries, ...), custom_call_target="tpu_custom_call" | custom-call | flops 201326592 | bytes 1966080 | tf_op jit(solution)/shard_map/attend/pallas_call | solution.py:258
  55.2 1.9 %collective-permute-done.10.got = f32[256,512]{1,0:T(8,128)S(1)} collective-permute-done((f32[256,512]{1,0:T(8,128)S(1)}, f32[256,512]{1,0:T(8,128)S(1)}, u32[]{:S(2)}, u32[]{:S(2)}) %collective-permute-start.10) | collective-permute-done | bytes 524320 | tf_op jit(solution)/shard_map/ppermute | solution.py:411
  57.1 0.2 finish.1.refs_0_
  57.3 0.4 collective-permute-start.11
  57.7 0.2 collective-permute-done.12.refs_3_.refs_5_
  57.9 6.4 %collective-permute-done.11.refs_1_ = bf16[256,384]{1,0:T(8,128)(2,1)S(1)} collective-permute-done((bf16[256,384]{1,0:T(8,128)(2,1)S(1)}, bf16[256,384]{1,0:T(8,128)(2,1)S(1)}, u32[]{:S(2)}, u32[]{:S(2)}) %collective-permute-start.11) | collective-permute-done | bytes 196640 | tf_op jit(solution)/shard_map/ppermute | solution.py:414
  64.3 3.9 %project_out.1 = (bf16[256,1536]{1,0:T(8,128)(2,1)}, f32[1,256]{1,0:T(1,128)}) custom-call(s32[1]{0:T(128)} %bitcast.place, bf16[256,384]{1,0:T(8,128)(2,1)S(1)} %finish.1.refs_0_, bf16[256,384]{1,0:T(8,128)(2,1)S(1)} %collective-permute-done.11.refs_1_, bf16[384,3072]{1,0:T(8,128)(2,1)S(1)} %copy-done, ...), custom_call_target="tpu_custom_call" | custom-call | tf_op jit(solution)/shard_map/project_out/pallas_call | solution.py:339
  (34 shorter events, 0.5 us)
Async XLA Ops:
  0.6 1.4 %copy-start.1 = (bf16[256,3072]{1,0:T(8,128)(2,1)S(1)}, bf16[256,3072]{1,0:T(8,128)(2,1)}, u32[]{:S(2)}) copy-start(bf16[256,3072]{1,0:T(8,128)(2,1)} %tokens.3) | copy-start | bytes 4718596
  2.0 0.7 %copy-start.5 = (f32[2,384]{1,0:T(2,128)S(1)}, f32[2,384]{1,0:T(2,128)}, u32[]{:S(2)}) copy-start(f32[2,384]{1,0:T(2,128)} %gains.3) | copy-start | bytes 9220
  7.5 18.1 %copy-start.9 = (s32[2,32]{1,0:T(2,128)S(1)}, s32[2,32]{1,0:T(2,128)}, u32[]{:S(2)}) copy-start(s32[2,32]{1,0:T(2,128)} %param.12) | copy-start | bytes 772
  7.5 18.1 %copy-start.10 = (s32[2,4]{1,0:T(2,128)S(1)}, s32[2,4]{1,0:T(2,128)}, u32[]{:S(2)}) copy-start(s32[2,4]{1,0:T(2,128)} %param.11) | copy-start | bytes 100
  7.5 12.1 %collective-permute-start.2 = (bf16[512,384]{1,0:T(8,128)(2,1)S(1)}, bf16[512,384]{1,0:T(8,128)(2,1)S(1)}, u32[]{:S(2)}, u32[]{:S(2)}) collective-permute-start(bf16[512,384]{1,0:T(8,128)(2,1)S(1)} %project_kv.1), channel_id=1, source_target_pairs={{0,8},{2,10},{8,16},{10,18},{16,24},{18,26},{24,28},{26,30},{28,20... | collective-permute-start | bytes 1179656 | tf_op jit(solution)/shard_map/ppermute | solution.py:387
  10.6 10.9 %collective-permute-start.6 = (bf16[512,384]{1,0:T(8,128)(2,1)S(1)}, bf16[512,384]{1,0:T(8,128)(2,1)}, u32[]{:S(2)}, u32[]{:S(2)}) collective-permute-start(bf16[512,384]{1,0:T(8,128)(2,1)S(1)} %project_kv.1), channel_id=1, source_target_pairs={{0,4},{2,6},{8,0},{10,2},{16,8},{18,10},{24,16},{26,18},{28,24},{3... | collective-permute-start | bytes 1179656 | tf_op jit(solution)/shard_map/ppermute | solution.py:388
  19.7 5.9 %copy-start.2 = (bf16[512,384]{1,0:T(8,128)(2,1)}, bf16[512,384]{1,0:T(8,128)(2,1)S(1)}, u32[]{:S(2)}) copy-start(bf16[512,384]{1,0:T(8,128)(2,1)S(1)} %collective-permute-done.2) | copy-start | bytes 1179652
  19.7 10.6 %collective-permute-start.3 = (bf16[512,384]{1,0:T(8,128)(2,1)S(1)}, bf16[512,384]{1,0:T(8,128)(2,1)}, u32[]{:S(2)}, u32[]{:S(2)}) collective-permute-start(bf16[512,384]{1,0:T(8,128)(2,1)S(1)} %collective-permute-done.2), channel_id=1, source_target_pairs={{0,8},{2,10},{8,16},{10,18},{16,24},{18,26},{24,28},{26,30},{28,20... | collective-permute-start | bytes 1179656 | tf_op jit(solution)/shard_map/ppermute | solution.py:387
  21.5 10.4 %collective-permute-start.7 = (bf16[512,384]{1,0:T(8,128)(2,1)}, bf16[512,384]{1,0:T(8,128)(2,1)}, u32[]{:S(2)}, u32[]{:S(2)}) collective-permute-start(bf16[512,384]{1,0:T(8,128)(2,1)} %collective-permute-done.6), channel_id=1, source_target_pairs={{0,4},{2,6},{8,0},{10,2},{16,8},{18,10},{24,16},{26,18},{28,24},{3... | collective-permute-start | bytes 1179656 | tf_op jit(solution)/shard_map/ppermute | solution.py:388
  21.7 4.5 %copy-start = (bf16[384,3072]{1,0:T(8,128)(2,1)S(1)}, bf16[384,3072]{1,0:T(8,128)(2,1)}, u32[]{:S(2)}) copy-start(bf16[384,3072]{1,0:T(8,128)(2,1)} %refs_2_.1) | copy-start | bytes 7077892
  25.5 18.9 %collective-permute-start.1 = (bf16[256,384]{1,0:T(8,128)(2,1)S(1)}, bf16[256,384]{1,0:T(8,128)(2,1)S(1)}, u32[]{:S(2)}, u32[]{:S(2)}) collective-permute-start(bf16[256,384]{1,0:T(8,128)(2,1)S(1)} %project_q.1.queries), channel_id=1, source_target_pairs={{0,2},{2,0},{4,6},{6,4},{8,10},{10,8},{12,14},{14,12},{16,18},{18,... | collective-permute-start | bytes 589832 | tf_op jit(solution)/shard_map/ppermute | solution.py:394
  25.7 18.7 %collective-permute-start = (s32[2,36]{1,0:T(2,128)S(1)}, s32[2,36]{1,0:T(2,128)S(1)}, u32[]{:S(2)}, u32[]{:S(2)}) collective-permute-start(s32[2,36]{1,0:T(2,128)S(1)} %pad_add_fusion.own), channel_id=1, source_target_pairs={{0,2},{2,0},{4,6},{6,4},{8,10},{10,8},{12,14},{14,12},{16,18},{18,... | collective-permute-start | bytes 872 | tf_op jit(solution)/shard_map/ppermute | solution.py:396
  26.2 18.3 %copy-start.4 = (s32[16]{0:T(128)S(1)}, s32[16]{0:T(128)}, u32[]{:S(2)}) copy-start(s32[16]{0:T(128)} %window.9) | copy-start | bytes 196
  28.0 0.6 copy-start.6
  28.6 29.3 %collective-permute-start.12 = (bf16[1,400,1536]{2,1,0:T(8,128)(2,1)}, bf16[1,400,1536]{2,1,0:T(8,128)(2,1)}, u32[]{:S(2)}, u32[]{:S(2)}) collective-permute-start(bf16[1,400,1536]{2,1,0:T(8,128)(2,1)} %get-tuple-element.26), channel_id=1, source_target_pairs={{0,1},{1,0},{2,3},{3,2},{4,5},{5,4},{6,7},{7,6},{8,9},{9,8},{10,11... | collective-permute-start | bytes 3686408 | tf_op jit(solution)/shard_map/ppermute | solution.py:399
  30.3 11.0 %collective-permute-start.4 = (bf16[512,384]{1,0:T(8,128)(2,1)}, bf16[512,384]{1,0:T(8,128)(2,1)S(1)}, u32[]{:S(2)}, u32[]{:S(2)}) collective-permute-start(bf16[512,384]{1,0:T(8,128)(2,1)} %collective-permute-done.3), channel_id=1, source_target_pairs={{0,8},{2,10},{8,16},{10,18},{16,24},{18,26},{24,28},{26,30},{28,20... | collective-permute-start | bytes 1179656 | tf_op jit(solution)/shard_map/ppermute | solution.py:387
  31.9 11.1 %collective-permute-start.8 = (bf16[512,384]{1,0:T(8,128)(2,1)}, bf16[512,384]{1,0:T(8,128)(2,1)}, u32[]{:S(2)}, u32[]{:S(2)}) collective-permute-start(bf16[512,384]{1,0:T(8,128)(2,1)} %collective-permute-done.7), channel_id=1, source_target_pairs={{0,4},{2,6},{8,0},{10,2},{16,8},{18,10},{24,16},{26,18},{28,24},{3... | collective-permute-start | bytes 1179656 | tf_op jit(solution)/shard_map/ppermute | solution.py:388
  33.1 13.4 %copy-start.3 = (bf16[512,384]{1,0:T(8,128)(2,1)S(1)}, bf16[512,384]{1,0:T(8,128)(2,1)}, u32[]{:S(2)}) copy-start(bf16[512,384]{1,0:T(8,128)(2,1)} %copy-done.2) | copy-start | bytes 1179652
  41.3 12.4 %collective-permute-start.5 = (bf16[256,384]{1,0:T(8,128)(2,1)S(1)}, bf16[256,384]{1,0:T(8,128)(2,1)S(1)}, u32[]{:S(2)}, u32[]{:S(2)}) collective-permute-start(bf16[256,384]{1,0:T(8,128)(2,1)S(1)} %slice.8), channel_id=1, source_target_pairs={{0,8},{2,10},{8,16},{10,18},{16,24},{18,26},{24,28},{26,30},{28,20... | collective-permute-start | bytes 589832 | tf_op jit(solution)/shard_map/ppermute | solution.py:390
  43.9 9.8 %collective-permute-start.9 = (bf16[256,384]{1,0:T(8,128)(2,1)S(1)}, bf16[256,384]{1,0:T(8,128)(2,1)S(1)}, u32[]{:S(2)}, u32[]{:S(2)}) collective-permute-start(bf16[256,384]{1,0:T(8,128)(2,1)S(1)} %slice.9), channel_id=1, source_target_pairs={{0,4},{2,6},{8,0},{10,2},{16,8},{18,10},{24,16},{26,18},{28,24},{3... | collective-permute-start | bytes 589832 | tf_op jit(solution)/shard_map/ppermute | solution.py:391
  44.5 0.7 %copy-start.8 = (s32[3]{0:T(128)S(1)}, s32[3]{0:T(128)}, u32[]{:S(2)}) copy-start(s32[3]{0:T(128)} %pad_add_fusion.7.ids) | copy-start | bytes 40
  53.7 10.6 %copy-start.7 = (bf16[16,384]{1,0:T(8,128)(2,1)S(1)}, bf16[16,384]{1,0:T(8,128)(2,1)}, u32[]{:S(2)}) copy-start(bf16[16,384]{1,0:T(8,128)(2,1)} %copy-done.6) | copy-start | bytes 36868
  55.1 2.0 %collective-permute-start.10 = (f32[256,512]{1,0:T(8,128)S(1)}, f32[256,512]{1,0:T(8,128)S(1)}, u32[]{:S(2)}, u32[]{:S(2)}) collective-permute-start(f32[256,512]{1,0:T(8,128)S(1)} %get-tuple-element.25), channel_id=1, source_target_pairs={{0,2},{2,0},{4,6},{6,4},{8,10},{10,8},{12,14},{14,12},{16,18},{18,... | collective-permute-start | bytes 1572872 | tf_op jit(solution)/shard_map/ppermute | solution.py:411
  57.3 7.0 %collective-permute-start.11 = (bf16[256,384]{1,0:T(8,128)(2,1)S(1)}, bf16[256,384]{1,0:T(8,128)(2,1)S(1)}, u32[]{:S(2)}, u32[]{:S(2)}) collective-permute-start(bf16[256,384]{1,0:T(8,128)(2,1)S(1)} %finish.1.refs_0_), channel_id=1, source_target_pairs={{0,1},{1,0},{2,3},{3,2},{4,5},{5,4},{6,7},{7,6},{8,9},{9,8},{10,11... | collective-permute-start | bytes 589832 | tf_op jit(solution)/shard_map/ppermute | solution.py:414

commit v2 on v0

v2 whole, which is shorter than its diff:
```python
import functools

import jax
import jax.numpy as jnp
from jax import lax
from jax.experimental import pallas as pl
from jax.experimental.pallas import tpu as pltpu
from jax.sharding import PartitionSpec as P

D = 3072
HD = 128
BLK = 128
EPS = 1e-06
PAD = 16
BARRED = -1e30
F32 = jnp.float32
BF16 = jnp.bfloat16
VMEM = pltpu.VMEM
SMEM = pltpu.SMEM
MIB = 1024 * 1024
IN_VMEM = pl.BlockSpec(memory_space=VMEM)
IN_SMEM = pl.BlockSpec(memory_space=SMEM)
IN_HBM = pl.BlockSpec(memory_space=pltpu.HBM)
ANYWHERE = pl.BlockSpec(memory_space=pl.ANY)


def params(mib):
    return pltpu.CompilerParams(vmem_limit_bytes=mib * MIB)


def cost(microseconds):
    return pl.CostEstimate(
        flops=int(microseconds * 0), bytes_accessed=int(microseconds * 0), transcendentals=0
    )


def normed(values, gains, scale):
    parts = []
    for first in range(0, values.shape[1], HD):
        head = values[:, first : first + HD]
        factor = lax.rsqrt(jnp.mean(head * head, axis=-1, keepdims=True) + EPS)
        parts.append(head * factor * gains[:, first : first + HD] * scale)
    return jnp.concatenate(parts, axis=1)


def project_kernel(steps, tokens, w_qkv, gains, near_mask, far_pattern, kv, queries, *scratch):
    token_buf, w_buf, gain_buf, near_buf, far_buf, total, sems, small_sems = scratch
    rows, width = tokens.shape
    count, _, cols = w_qkv.shape
    deep = width // steps
    copies = []
    for s in range(steps):
        span = pl.ds(s * deep, deep)
        group = [pltpu.make_async_copy(tokens.at[:, span], token_buf.at[:, span], sems.at[0, s])]
        for j in range(count):
            group.append(
                pltpu.make_async_copy(
                    w_qkv.at[j, span], w_buf.at[span, pl.ds(j * cols, cols)], sems.at[1 + j, s]
                )
            )
        for copy in group:
            copy.start()
        copies.append(group)
    small = [
        pltpu.make_async_copy(source, target, small_sems.at[i])
        for i, (source, target) in enumerate(
            ((gains, gain_buf), (near_mask, near_buf), (far_pattern, far_buf))
        )
    ]
    for copy in small:
        copy.start()
    for s in range(steps):
        for copy in copies[s]:
            copy.wait()
        span = slice(s * deep, (s + 1) * deep)
        part = jnp.dot(token_buf[:, span], w_buf[span, :], preferred_element_type=F32)
        if s == 0:
            total[...] = part
        elif s < steps - 1:
            total[...] += part
    part = total[...] + part
    for copy in small:
        copy.wait()
    query, key, value = (part[:, j * cols : (j + 1) * cols] for j in range(count))
    kv[:rows, :] = normed(key, gain_buf[1:2, :], 1.0).astype(BF16)
    kv[rows:, :] = value.astype(BF16)
    queries[:rows, :] = normed(query, gain_buf[0:1, :], HD ** (-0.5)).astype(BF16)
    n_blocks, n_near = near_mask.shape
    queries[rows:, :] = jnp.zeros((PAD, cols), BF16)
    queries[rows : rows + n_blocks, :n_near] = near_buf[...].astype(F32).astype(BF16)
    queries[rows : rows + n_blocks, HD : HD + far_pattern.shape[1]] = (
        far_buf[...].astype(F32).astype(BF16)
    )


def project(tokens, w_qkv, gains, near_mask, far_pattern):
    rows, width = tokens.shape
    count, _, cols = w_qkv.shape
    steps = 4
    return pl.pallas_call(
        functools.partial(project_kernel, steps),
        in_specs=[ANYWHERE] * 5,
        out_specs=[IN_VMEM] * 2,
        out_shape=[
            jax.ShapeDtypeStruct((2 * rows, cols), BF16),
            jax.ShapeDtypeStruct((rows + PAD, cols), BF16),
        ],
        scratch_shapes=[
            VMEM((rows, width), BF16),
            VMEM((width, count * cols), BF16),
            VMEM(gains.shape, F32),
            VMEM(near_mask.shape, jnp.int32),
            VMEM(far_pattern.shape, jnp.int32),
            VMEM((rows, count * cols), F32),
            pltpu.SemaphoreType.DMA((1 + count, steps)),
            pltpu.SemaphoreType.DMA((3,)),
        ],
        compiler_params=params(56),
        cost_estimate=cost(5.0),
        name="project",
    )(tokens, w_qkv, gains, near_mask, far_pattern)


def split_sum(values):
    high = values.astype(BF16).astype(F32)
    mid = (values - high).astype(BF16).astype(F32)
    return high, mid, values - high - mid


def w_kernel(n_head, place, w_out, _, sums, payload):
    rows, width = w_out.shape
    cols = width // n_head
    total = lax.dot_general(
        jnp.ones((8, width), BF16), w_out[...], (((1,), (1,)), ((), ())), preferred_element_type=F32
    )
    high, mid, low = split_sum(total)
    row = lax.broadcasted_iota(jnp.int32, (8, rows), 0)
    packed = jnp.where(row == 0, high, jnp.where(row == 1, mid, jnp.where(row == 2, low, 0.0)))
    packed = jnp.concatenate([packed, jnp.zeros((PAD - 8, rows), F32)], axis=0).astype(BF16)
    sums[...] = packed
    share = payload.shape[1]
    for k in range(1, n_head):
        target = lax.rem(place[0] + k, n_head)
        first = pl.multiple_of(target * cols, HD)

        @pl.when(place[1] == 0)
        def _():
            payload[k - 1] = w_out[:share, pl.ds(first, cols)]

        @pl.when(place[1] == 1)
        def _():
            payload[k - 1, : rows - share, :] = w_out[share:, pl.ds(first, cols)]
            payload[k - 1, rows - share :, :] = jnp.zeros((2 * share - rows, cols), BF16)
            payload[k - 1, rows - share : rows - share + PAD, :rows] = packed


def prepare_w(place, w_out, n_head, before):
    rows, width = w_out.shape
    cols = width // n_head
    share = (rows + 2 * PAD) // 2
    return pl.pallas_call(
        functools.partial(w_kernel, n_head),
        in_specs=[IN_SMEM, IN_VMEM, IN_VMEM],
        out_specs=[IN_VMEM] * 2,
        out_shape=[
            jax.ShapeDtypeStruct((PAD, rows), BF16),
            jax.ShapeDtypeStruct((n_head - 1, share, cols), BF16),
        ],
        compiler_params=params(16),
        cost_estimate=cost(1.2),
        name="prepare_w",
    )(place, w_out, before)


def merge_kernel(place, mine, sibling, out):
    share = mine.shape[1]

    @pl.when(place[1] == 0)
    def _():
        out[:, :share, :] = mine[...]
        out[:, share:, :] = sibling[...]

    @pl.when(place[1] == 1)
    def _():
        out[:, :share, :] = sibling[...]
        out[:, share:, :] = mine[...]


def merge_w(place, mine, sibling):
    n, share, cols = mine.shape
    return pl.pallas_call(
        merge_kernel,
        in_specs=[IN_SMEM, IN_VMEM, IN_VMEM],
        out_specs=IN_VMEM,
        out_shape=jax.ShapeDtypeStruct((n, 2 * share, cols), BF16),
        compiler_params=params(16),
        cost_estimate=cost(0.4),
        name="merge_w",
    )(place, mine, sibling)


def bias_kernel(side, n_slabs, n_blocks, ids, window, queries, _, out):
    rows = n_blocks * BLK
    shifted = lax.broadcasted_iota(jnp.int32, (BLK, BLK), 0) - lax.broadcasted_iota(
        jnp.int32, (BLK, BLK), 1
    )
    gaps = {
        by: jnp.abs(shifted + by * BLK).astype(F32) for by in range(1 - n_blocks, n_blocks)
    }
    lane = lax.broadcasted_iota(jnp.int32, (PAD, queries.shape[1]), 1)
    masks = queries[rows : rows + PAD, :].astype(F32)
    query_slab = ids[side]
    for c in range(n_slabs):
        key_slab = ids[2 + c]
        distance = jnp.abs(key_slab - query_slab)
        before = jnp.where(key_slab < query_slab, 0, 1)
        first = jnp.where(distance == 1, before * n_blocks, HD + key_slab * n_blocks)
        whole = jnp.where(distance == 0, 1.0, 0.0)
        reach = window[distance].astype(F32)
        for j in range(n_blocks):
            picked = jnp.sum(jnp.where(lane == first + j, masks, 0.0), axis=1, keepdims=True)
            limit = jnp.where(jnp.maximum(picked, whole) > 0.5, reach, 0.0)
            for i in range(n_blocks):
                here = jnp.broadcast_to(limit[i : i + 1, :], (BLK, BLK))
                out[c, i * BLK : (i + 1) * BLK, j * BLK : (j + 1) * BLK] = jnp.where(
                    gaps[i - j] < here, 0.0, BARRED
                )


def biases(side, ids, window, queries, n_blocks, before):
    n_slabs = ids.shape[0] - 2
    rows = n_blocks * BLK
    return pl.pallas_call(
        functools.partial(bias_kernel, side, n_slabs, n_blocks),
        in_specs=[IN_SMEM] * 2 + [IN_VMEM] * 2,
        out_specs=IN_VMEM,
        out_shape=jax.ShapeDtypeStruct((n_slabs, rows, rows), F32),
        compiler_params=params(16),
        cost_estimate=cost(0.5),
        name="biases",
    )(ids, window, queries, before)


def attend_kernel(slabs, lone, has_totals, packed, heads, bias, queries, _, *refs):
    rows = bias.shape[1]
    chunks, refs = [], list(refs)
    for apart in lone:
        if apart:
            chunks.append((refs.pop(0), refs.pop(0)))
        else:
            both = refs.pop(0)
            chunks.append((both.at[:rows], both.at[rows:]))
    before, out = (refs[0], refs[1]) if has_totals else (None, refs[0])
    ones = jnp.ones((rows, HD), BF16)
    if packed:
        out[rows:, :] = jnp.zeros((PAD, out.shape[1]), BF16)
    for h in range(*heads):
        span = slice(h * HD, (h + 1) * HD)
        keys = jnp.concatenate([key[:, span] for key, _ in chunks], axis=0)
        scores = lax.dot_general(
            queries[:rows, span], keys, (((1,), (1,)), ((), ())), preferred_element_type=F32
        )
        weights = [
            jnp.exp(scores[:, n * rows : (n + 1) * rows] + bias[slab]).astype(BF16)
            for n, slab in enumerate(slabs)
        ]
        values = jnp.concatenate(
            [jnp.concatenate([value[:, span], ones], axis=1) for _, value in chunks], axis=0
        )
        sums = jnp.dot(jnp.concatenate(weights, axis=1), values, preferred_element_type=F32)
        if has_totals:
            sums = sums + before[h]
        if not packed:
            out[h] = sums
            continue
        span = slice((h - heads[0]) * HD, (h - heads[0] + 1) * HD)
        out[:rows, span] = sums[:, :HD].astype(BF16)
        for b in range(rows // HD):
            row = sums[b * HD : (b + 1) * HD, HD:].T[0:1, :]
            high = row.astype(BF16)
            out[rows + 2 * b : rows + 2 * b + 1, span] = high
            out[rows + 2 * b + 1 : rows + 2 * b + 2, span] = (row - high.astype(F32)).astype(BF16)


def attend(bias, queries, before, parts, totals, heads, packed, name):
    rows = bias.shape[1]
    operands = [bias, queries, before] + [array for chunk, _ in parts for array in chunk]
    if totals is not None:
        operands.append(totals)
    count = heads[1] - heads[0]
    if packed:
        shape = jax.ShapeDtypeStruct((rows + PAD, count * HD), BF16)
    else:
        shape = jax.ShapeDtypeStruct((count, rows, 2 * HD), F32)
    slabs = [slab for _, slab in parts]
    return pl.pallas_call(
        functools.partial(
            attend_kernel, slabs, [len(c) > 1 for c, _ in parts], totals is not None, packed, heads
        ),
        in_specs=[IN_VMEM] * len(operands),
        out_specs=IN_VMEM,
        out_shape=shape,
        compiler_params=params(24),
        cost_estimate=cost(0.08 * len(parts) * count + 0.15),
        name=name,
    )(*operands)


def finish_kernel(heads, kept, got, _, out):
    rows = kept.shape[1]
    for h in range(*heads):
        span = slice((h - heads[0]) * HD, (h - heads[0] + 1) * HD)
        for b in range(rows // HD):
            here = slice(b * HD, (b + 1) * HD)
            pair = got[rows : rows + PAD, span].astype(F32)
            row = pair[2 * b : 2 * b + 1, :] + pair[2 * b + 1 : 2 * b + 2, :]
            other = jnp.broadcast_to(row, (HD, HD)).T
            num = kept[h, here, :HD] + got[here, span].astype(F32)
            out[here, span] = (num / (kept[h, here, HD:] + other)).astype(BF16)


def finish(kept, got, heads, before):
    rows = kept.shape[1]
    return pl.pallas_call(
        functools.partial(finish_kernel, heads),
        in_specs=[IN_VMEM] * 3,
        out_specs=IN_VMEM,
        out_shape=jax.ShapeDtypeStruct((rows, (heads[1] - heads[0]) * HD), BF16),
        compiler_params=params(16),
        cost_estimate=cost(0.15),
        name="finish",
    )(kept, got, before)


def gate_kernel(array, _, out):
    pass


def gate(array, before):
    return pl.pallas_call(
        gate_kernel,
        in_specs=[IN_VMEM] * 2,
        out_specs=IN_VMEM,
        out_shape=jax.ShapeDtypeStruct(array.shape, array.dtype),
        input_output_aliases={0: 0},
        compiler_params=params(16),
        cost_estimate=cost(0.1),
        name="gate",
    )(array, before)


def row_dot(summed, values):
    dots = lax.dot_general(
        summed, values, (((1,), (1,)), ((), ())), preferred_element_type=F32
    )
    return dots[0:1, :] + (dots[1:2, :] + dots[2:3, :])


def early_kernel(n_head, place, own, w_out, sums, partial, parts, owners):
    cols = partial.shape[1]
    first = pl.multiple_of(place[0] * cols, HD)
    partial[...] = jnp.dot(own[...], w_out[:, pl.ds(first, cols)], preferred_element_type=F32)
    parts[...] = jnp.zeros(parts.shape, F32)
    parts[pl.ds(place[0], 1), :] = row_dot(sums[...], own[...])
    row = lax.broadcasted_iota(jnp.int32, parts.shape, 0)
    for k in range(1, n_head):
        owner = lax.rem(place[0] - k + n_head, n_head)
        owners[k - 1] = jnp.where(row == owner, 1.0, 0.0)


def project_early(place, own, w_out, sums, n_head):
    rows = own.shape[0]
    cols = w_out.shape[1] // n_head
    places = -(-n_head // 8) * 8
    return pl.pallas_call(
        functools.partial(early_kernel, n_head),
        in_specs=[IN_SMEM] + [IN_VMEM] * 3,
        out_specs=[IN_VMEM] * 3,
        out_shape=[
            jax.ShapeDtypeStruct((rows, cols), F32),
            jax.ShapeDtypeStruct((places, rows), F32),
            jax.ShapeDtypeStruct((n_head - 1, places, rows), F32),
        ],
        compiler_params=params(24),
        cost_estimate=cost(1.4),
        name="project_early",
    )(place, own, w_out, sums)


def last_kernel(n_head, depth, *refs):
    late, refs = refs[: n_head - 1], refs[n_head - 1 :]
    received, partial, parts, owners, layer_out, checksum, staged, sems = refs
    rows, cols = partial.shape
    tiles = sems.shape[0]
    tile = cols // tiles
    stores = []
    for t in range(tiles):
        here = slice(t * tile, (t + 1) * tile)
        total = partial[:, here]
        for k in range(1, n_head):
            total = total + jnp.dot(
                late[k - 1][...], received[k - 1, :depth, here], preferred_element_type=F32
            )
        staged[:, here] = total.astype(BF16)
        there = pl.ds(t * tile, tile)
        store = pltpu.make_async_copy(staged.at[:, there], layer_out.at[:, there], sems.at[t])
        store.start()
        stores.append(store)
    every = parts[...]
    for k in range(1, n_head):
        dot = row_dot(received[k - 1, depth : depth + PAD, :depth], late[k - 1][...])
        every = every + owners[k - 1] * dot
    sum_all = every[0:1, :]
    for k in range(1, n_head):
        sum_all = sum_all + every[k : k + 1, :]
    checksum[...] = sum_all * D ** (-0.5)
    for store in stores:
        store.wait()


def project_last(late, received, partial, parts, owners):
    n_head = len(late) + 1
    depth = late[0].shape[1]
    rows, cols = partial.shape
    tiles = next(t for t in (3, 2, 1) if cols % (t * HD) == 0)
    operands = [*late, received, partial, parts, owners]
    layer_out, checksum = pl.pallas_call(
        functools.partial(last_kernel, n_head, depth),
        in_specs=[IN_VMEM] * len(operands),
        out_specs=[ANYWHERE, IN_VMEM],
        out_shape=[
            jax.ShapeDtypeStruct((rows, cols), BF16),
            jax.ShapeDtypeStruct((1, rows), F32),
        ],
        scratch_shapes=[VMEM((rows, cols), BF16), pltpu.SemaphoreType.DMA((tiles,))],
        compiler_params=params(24),
        name="project_last",
    )(*operands)
    return layer_out, checksum.reshape(rows)


def per_device(tokens, w_qkv, norm_gains, w_out, near_mask, far_pattern, window):
    rows = tokens.shape[0]
    heads = w_qkv.shape[2] // HD
    n_blocks = rows // BLK
    frame = lax.axis_index("frame").astype(jnp.int32)
    place = jnp.stack([lax.axis_index("head").astype(jnp.int32), frame % 2])
    n_frame = lax.axis_size("frame")
    n_head = lax.axis_size("head")
    half = n_frame // 2
    every = (0, heads)

    def swapped(array, by):
        return lax.ppermute(array, "frame", [(i, i ^ by) for i in range(n_frame)])

    def from_head(array, k):
        return lax.ppermute(array, "head", [(i, (i + k) % n_head) for i in range(n_head)])

    spans = []
    by = half // 2
    while by > 1:
        spans.append(by)
        by //= 2
    far = sorted((o for o in range(2, half, 2) if o not in spans), key=lambda o: bin(o).count("1"))
    straight = [0] + spans + far
    slabs = straight + [o ^ 1 for o in straight]

    kv, queries = project(tokens, w_qkv, norm_gains, near_mask, far_pattern)
    other_queries = swapped(queries, half)
    chunks = {0: (kv,)}
    near = {by: swapped(kv, by) for by in spans}
    chunks[1] = (swapped(kv, 1),)
    ids = jnp.stack([frame, frame ^ half] + [frame ^ s for s in slabs])

    def some(offsets):
        return [(chunks[o], slabs.index(o)) for o in offsets]

    bias = biases(0, ids, window, queries, n_blocks, queries)
    own = attend(bias, queries, bias, some([0, 1]), None, every, False, "attend_first")
    sums, payload = prepare_w(place, w_out, n_head, own)
    mine = [from_head(payload[k - 1 : k], k) for k in range(1, n_head)]
    mine = mine[0] if len(mine) == 1 else jnp.concatenate(mine)

    low = spans[-1]
    near[low] = gate(near[low], own)
    other_bias = biases(1, ids, window, other_queries, n_blocks, near[low])
    for by in spans[:-1]:
        near[by] = gate(near[by], other_bias)
    for by in spans:
        chunks[by] = (near[by],)
        chunks[by ^ 1] = (swapped(near[by], 1),)
    keys = {by: near[by][:rows] for by in spans}
    values = {by: near[by][rows:] for by in spans}
    for o in far:
        bits = [by for by in spans if o & by]
        values[o] = swapped(values[o ^ bits[0]], bits[0])
        keys[o] = swapped(keys[o ^ bits[-1]], bits[-1])
    other = attend(
        other_bias, other_queries, own, some([0, 1] + spans), None, every, False, "other_first"
    )
    for o in far:
        keys[o], values[o] = gate(keys[o], other), gate(values[o], other)
        chunks[o] = (keys[o], values[o])
        chunks[o ^ 1] = (swapped(keys[o], 1), swapped(values[o], 1))
    middle = [by ^ 1 for by in spans] + far
    other = attend(other_bias, other_queries, other, some(middle), other, every, False, "other_middle")
    late = [o ^ 1 for o in far]
    sent = attend(other_bias, other_queries, other, some(late), other, every, True, "other_last")
    rest = spans + middle + late
    own = attend(bias, queries, sent, some(rest), own, every, False, "attend_rest")
    done = finish(own, swapped(sent, half), every, own)
    late = [from_head(done, k) for k in range(1, n_head)]
    mine = gate(mine, done)
    received = merge_w(place, mine, swapped(mine, 1))
    partial, sum_parts, owners = project_early(place, done, w_out, sums, n_head)
    return project_last(late, received, partial, sum_parts, owners)


def solution(mesh):
    in_specs = (
        P("frame", None),
        P(None, None, "head"),
        P(None, "head"),
        P("head", None),
        P("frame", None),
        P("frame", None),
        P(),
    )
    out_specs = (P("frame", "head"), P("frame"))
    return jax.shard_map(
        per_device, mesh=mesh, in_specs=in_specs, out_specs=out_specs, check_vma=False
    )
```

time: 172 us -> 58.5 us (0.34)
  waiting for transfers between devices: 81.2 us -> 20.7 us
  matrix products: 33.6 us -> 0 us
  local copies, waits for them, and re-layouts: 24 us -> 2.26 us
  Pallas kernels: 0 us -> 19.1 us
  between operations: 14 us -> 0.83 us
  starting transfers between devices: 5.2 us -> 15.4 us
  other arithmetic: 7.64 us -> 0.08 us
  blocking collectives: 5.5 us -> 0 us
    all_gather x2 -> x0, waiting for transfers between devices: 56.1 us -> none  [the longest x1 36 us: per_device(): lax.all_gather(values_flat, 'frame', axis=0, tiled=True)]
    dot_general x10 -> x0, matrix products: 33.6 us -> none  [the longest x2 13 us: attend(): jnp.einsum('qhd,khd->hqk', queries, key_heads, preferred_element_type=jnp...]
    reduce_scatter x1 -> x0, waiting for transfers between devices: 25 us -> none  [per_device(): lax.psum_scatter(lax.dot_general(w_out, attended, (((0,), (1,)), ((), ())...]
    ppermute x2 -> x14, waiting for transfers between devices: 0.01 us -> 20.7 us  [the longest x12 16.7 us: swapped(): return lax.ppermute(array, 'frame', [(i, i ^ by) for i in range(n_frame)])]
    pallas_call x0 -> x18, Pallas kernels: none -> 19.1 us  [the longest x5 6.72 us: attend(): pl.pallas_call(functools.partial(attend_kernel, slabs, [len(c) > 1 for c,...]
    dot_general x3 -> x0, local copies, waits for them, and re-layouts: 13.7 us -> none  [the longest x2 9.45 us: per_device(): query = jnp.dot(tokens, w_qkv[0], preferred_element_type=jnp.float32)]
    ppermute x2 -> x14, starting transfers between devices: 5.08 us -> 15.4 us  [the longest x12 12.3 us: swapped(): return lax.ppermute(array, 'frame', [(i, i ^ by) for i in range(n_frame)])]
    psum x1 -> x0, blocking collectives: 5.5 us -> none  [per_device(): checksum = lax.psum(jnp.sum(full_rows, axis=1) * D ** (-0.5), 'head')]
  transfers between devices with their start and end apart: 5 -> 14, of which waited for: 3 -> 6; matrix products, arithmetic and copies ran while one was open for 21% -> 0% of each run, Pallas kernels for 0% -> 20%
where the time goes in v2:
time: 58.5 us; the launch traced here: 58.3 us
  waiting for transfers between devices  20.7 us (35%)
  Pallas kernels  19.1 us (33%)
  starting transfers between devices  15.4 us (26%)
  local copies, waits for them, and re-layouts  2.26 us (4%)
  between operations  0.83 us (1%)
    ppermute x12, waiting for transfers between devices, swapped(): return lax.ppermute(array, 'frame', [(i, i ^ by) for i in range(n_frame)])  16.7 us
    ppermute x12, starting transfers between devices, swapped(): return lax.ppermute(array, 'frame', [(i, i ^ by) for i in range(n_frame)])  12.3 us
    pallas_call x5, Pallas kernels, attend(): pl.pallas_call(functools.partial(attend_kernel, slabs, [len(c) > 1 for c,...  6.72 us
    pallas_call x1, Pallas kernels, project(): pl.pallas_call(functools.partial(project_kernel, steps), in_specs=[ANYWHE...  5.68 us
    ppermute x2, waiting for transfers between devices, from_head(): lax.ppermute(array, 'head', [(i, (i + k) % n_head) for i in range(n_head)])  3.97 us
    ppermute x2, starting transfers between devices, from_head(): lax.ppermute(array, 'head', [(i, (i + k) % n_head) for i in range(n_head)])  3.11 us
    unnamed x10, local copies, waits for them, and re-layouts  2.13 us
    pallas_call x1, Pallas kernels, project_last(): pl.pallas_call(functools.partial(last_kernel, n_head, depth), in_specs=[I...  1.86 us
  transfers between devices with their start and end apart: 14, of which 6 were waited for; matrix products, arithmetic and copies ran while one was open for 0% of the time, Pallas kernels for 20%

profile of v2, /device:TPU:0, one launch (start us, length us, event | category | flops | bytes accessed | tf_op | source)
XLA Modules:
  0.0 58.3 jit_solution(6271596332240674342)
XLA Ops:
  0.6 5.7 %project.1 = (bf16[512,384]{1,0:T(8,128)(2,1)}, bf16[272,384]{1,0:T(8,128)(2,1)}) custom-call(bf16[256,3072]{1,0:T(8,128)(2,1)} %tokens.1, bf16[3,3072,384]{2,1,0:T(8,128)(2,1)} %w_qkv.1, f32[2,384]{1,0:T(2,128)} %gains.1, s32[2,4]{1,0:T(2,128)} %near_mask.1, s32[2,32]{1,0:T(2,128)} %far_pattern.1), custom_call_target="tpu_custom_call" | custom-call | tf_op jit(solution)/shard_map/project/pallas_call | solution.py:100
  6.3 0.5 collective-permute-start.2
  6.9 2.6 %collective-permute-start.1 = (bf16[512,384]{1,0:T(8,128)(2,1)}, bf16[512,384]{1,0:T(8,128)(2,1)S(1)}, u32[]{:S(2)}, u32[]{:S(2)}) collective-permute-start(bf16[512,384]{1,0:T(8,128)(2,1)} %get-tuple-element.12.refs_0_), channel_id=1, source_target_pairs={{0,4},{2,6},{4,0},{6,2},{8,12},{10,14},{12,8},{14,10},{16,20},{18,... | collective-permute-start | bytes 1179656 | tf_op jit(solution)/shard_map/ppermute | solution.py:454
  9.4 1.6 %collective-permute-start.3 = (bf16[512,384]{1,0:T(8,128)(2,1)}, bf16[512,384]{1,0:T(8,128)(2,1)S(1)}, u32[]{:S(2)}, u32[]{:S(2)}) collective-permute-start(bf16[512,384]{1,0:T(8,128)(2,1)} %get-tuple-element.12.refs_0_), channel_id=1, source_target_pairs={{0,8},{2,10},{4,12},{6,14},{8,0},{10,2},{12,4},{14,6},{16,24},{18,... | collective-permute-start | bytes 1179656 | tf_op jit(solution)/shard_map/ppermute | solution.py:454
  11.0 2.6 %collective-permute-start = (bf16[272,384]{1,0:T(8,128)(2,1)}, bf16[272,384]{1,0:T(8,128)(2,1)S(1)}, u32[]{:S(2)}, u32[]{:S(2)}) collective-permute-start(bf16[272,384]{1,0:T(8,128)(2,1)} %get-tuple-element.11.queries._), channel_id=1, source_target_pairs={{0,16},{2,18},{4,20},{6,22},{8,24},{10,26},{12,28},{14,30},{16,0},... | collective-permute-start | bytes 626696 | tf_op jit(solution)/shard_map/ppermute | solution.py:454
  13.6 0.1 stack.49.ids
  13.7 0.9 %copy-done.1 = bf16[272,384]{1,0:T(8,128)(2,1)S(1)} copy-done((bf16[272,384]{1,0:T(8,128)(2,1)S(1)}, bf16[272,384]{1,0:T(8,128)(2,1)}, u32[]{:S(2)}) %copy-start.1) | copy-done | bytes 208920
  14.6 0.8 %biases.2.bias._ = f32[8,256,256]{2,1,0:T(8,128)S(1)} custom-call(s32[10]{0:T(128)S(1)} %stack.49.ids, s32[16]{0:T(128)S(1)} %copy-done.4, bf16[272,384]{1,0:T(8,128)(2,1)S(1)} %copy-done.1, bf16[272,384]{1,0:T(8,128)(2,1)S(1)} %copy-done.1), custom_call_target="tpu_custom_call" | custom-call | tf_op jit(solution)/shard_map/biases/pallas_call | solution.py:233
  15.6 1.1 %copy-done.3 = bf16[512,384]{1,0:T(8,128)(2,1)S(1)} copy-done((bf16[512,384]{1,0:T(8,128)(2,1)S(1)}, bf16[512,384]{1,0:T(8,128)(2,1)}, u32[]{:S(2)}) %copy-start.3) | copy-done | bytes 393240
  16.7 1.7 %attend_first.1._.refs_8_ = f32[3,256,256]{2,1,0:T(8,128)S(1)} custom-call(f32[8,256,256]{2,1,0:T(8,128)S(1)} %biases.2.bias._, bf16[272,384]{1,0:T(8,128)(2,1)S(1)} %copy-done.2, f32[8,256,256]{2,1,0:T(8,128)S(1)} %biases.2.bias._, bf16[512,384]{1,0:T(8,128)(2,1)S(1)} %copy-done.3, bf16[512,384]{1,0:T(8,128)(2,1)} %collective-permute-done.2.refs_1_), custom_call_target="tpu_custom_call" | custom-call | tf_op jit(solution)/shard_map/attend_first/pallas_call | solution.py:296
  18.4 1.3 %prepare_w.1 = (bf16[16,384]{1,0:T(8,128)(2,1)S(1)}, bf16[1,208,1536]{2,1,0:T(8,128)(2,1)S(1)}) custom-call(s32[2]{0:T(128)S(1)} %pad_add_fusion.place, bf16[384,3072]{1,0:T(8,128)(2,1)S(1)} %copy-done, f32[3,256,256]{2,1,0:T(8,128)S(1)} %attend_first.1._.refs_8_), custom_call_target="tpu_custom_call" | custom-call | tf_op jit(solution)/shard_map/prepare_w/pallas_call | solution.py:161
  19.7 1.6 %collective-permute-start.12 = (bf16[1,208,1536]{2,1,0:T(8,128)(2,1)S(1)}, bf16[1,208,1536]{2,1,0:T(8,128)(2,1)S(1)}, u32[]{:S(2)}, u32[]{:S(2)}) collective-permute-start(bf16[1,208,1536]{2,1,0:T(8,128)(2,1)S(1)} %get-tuple-element.13), channel_id=1, source_target_pairs={{0,1},{1,0},{2,3},{3,2},{4,5},{5,4},{6,7},{7,6},{8,9},{9,8},{10,11... | collective-permute-start | bytes 1916936 | tf_op jit(solution)/shard_map/ppermute | solution.py:457
  21.3 0.5 collective-permute-start.7
  21.8 3.5 %collective-permute-done.queries = bf16[272,384]{1,0:T(8,128)(2,1)S(1)} collective-permute-done((bf16[272,384]{1,0:T(8,128)(2,1)}, bf16[272,384]{1,0:T(8,128)(2,1)S(1)}, u32[]{:S(2)}, u32[]{:S(2)}) %collective-permute-start) | collective-permute-done | bytes 208928 | tf_op jit(solution)/shard_map/ppermute | solution.py:454
  25.3 0.8 %biases.3._.bias = f32[8,256,256]{2,1,0:T(8,128)S(1)} custom-call(s32[10]{0:T(128)S(1)} %stack.49.ids, s32[16]{0:T(128)S(1)} %copy-done.4, bf16[272,384]{1,0:T(8,128)(2,1)S(1)} %collective-permute-done.queries, bf16[512,384]{1,0:T(8,128)(2,1)S(1)} %gate.5._.refs_3_.refs_1_), custom_call_target="tpu_custom_call" | custom-call | tf_op jit(solution)/shard_map/biases/pallas_call | solution.py:233
  26.2 0.5 collective-permute-start.5
  26.7 0.5 collective-permute-start.6
  27.2 2.1 %other_first.1._.refs_4_ = f32[3,256,256]{2,1,0:T(8,128)S(1)} custom-call(f32[8,256,256]{2,1,0:T(8,128)S(1)} %biases.3._.bias, bf16[272,384]{1,0:T(8,128)(2,1)S(1)} %collective-permute-done.queries, f32[3,256,256]{2,1,0:T(8,128)S(1)} %attend_first.1._.refs_8_, bf16[512,384]{1,0:T(8,128)(2,1)S(1)} %copy-done.3, ...), custom_call_target="tpu_custom_call" | custom-call | tf_op jit(solution)/shard_map/other_first/pallas_call | solution.py:296
  29.3 0.2 collective-permute-done.7.array
  29.5 4.1 %collective-permute-done.6.array = bf16[256,384]{1,0:T(8,128)(2,1)S(1)} collective-permute-done((bf16[256,384]{1,0:T(8,128)(2,1)S(1)}, bf16[256,384]{1,0:T(8,128)(2,1)S(1)}, u32[]{:S(2)}, u32[]{:S(2)}) %collective-permute-start.6) | collective-permute-done | bytes 196640 | tf_op jit(solution)/shard_map/ppermute | solution.py:454
  33.6 0.9 %other_middle.1._.refs_2_ = f32[3,256,256]{2,1,0:T(8,128)S(1)} custom-call(f32[8,256,256]{2,1,0:T(8,128)S(1)} %biases.3._.bias, bf16[272,384]{1,0:T(8,128)(2,1)S(1)} %collective-permute-done.queries, f32[3,256,256]{2,1,0:T(8,128)S(1)} %other_first.1._.refs_4_, bf16[512,384]{1,0:T(8,128)(2,1)S(1)} %collective-permute-done.4.refs_0_.refs_2_, ...), custom_call_target="tpu_custom_call" | custom-call | tf_op jit(solution)/shard_map/other_middle/pallas_call | solution.py:296
  34.5 0.5 collective-permute-done.8.refs_0_.refs_6_
  35.0 0.5 other_last.1._
  35.6 3.3 %collective-permute-start.10 = (bf16[272,384]{1,0:T(8,128)(2,1)S(1)}, bf16[272,384]{1,0:T(8,128)(2,1)S(1)}, u32[]{:S(2)}, u32[]{:S(2)}) collective-permute-start(bf16[272,384]{1,0:T(8,128)(2,1)S(1)} %other_last.1._), channel_id=1, source_target_pairs={{0,16},{2,18},{4,20},{6,22},{8,24},{10,26},{12,28},{14,30},{16,0},... | collective-permute-start | bytes 626696 | tf_op jit(solution)/shard_map/ppermute | solution.py:454
  38.9 1.5 %attend_rest.1.kept._ = f32[3,256,256]{2,1,0:T(8,128)S(1)} custom-call(f32[8,256,256]{2,1,0:T(8,128)S(1)} %biases.2.bias._, bf16[272,384]{1,0:T(8,128)(2,1)S(1)} %copy-done.2, bf16[272,384]{1,0:T(8,128)(2,1)S(1)} %other_last.1._, bf16[512,384]{1,0:T(8,128)(2,1)S(1)} %gate.6.refs_2_.refs_0_, bf16[512,384]{1,0:T(8,128)(2,1)S(1)} %gate.5._.refs_3_.refs_1_, ...), custom_call_target="tpu_custom_call" | custom-call | tf_op jit(solution)/shard_map/attend_rest/pallas_call | solution.py:296
  40.4 8.4 %collective-permute-done.10.got = bf16[272,384]{1,0:T(8,128)(2,1)S(1)} collective-permute-done((bf16[272,384]{1,0:T(8,128)(2,1)S(1)}, bf16[272,384]{1,0:T(8,128)(2,1)S(1)}, u32[]{:S(2)}, u32[]{:S(2)}) %collective-permute-start.10) | collective-permute-done | bytes 208928 | tf_op jit(solution)/shard_map/ppermute | solution.py:454
  48.8 0.2 finish.1._.own
  49.1 1.6 %collective-permute-start.11 = (bf16[256,384]{1,0:T(8,128)(2,1)S(1)}, bf16[256,384]{1,0:T(8,128)(2,1)S(1)}, u32[]{:S(2)}, u32[]{:S(2)}) collective-permute-start(bf16[256,384]{1,0:T(8,128)(2,1)S(1)} %finish.1._.own), channel_id=1, source_target_pairs={{0,1},{1,0},{2,3},{3,2},{4,5},{5,4},{6,7},{7,6},{8,9},{9,8},{10,11... | collective-permute-start | bytes 589832 | tf_op jit(solution)/shard_map/ppermute | solution.py:457
  50.7 1.1 %project_early.1 = (f32[256,1536]{1,0:T(8,128)S(1)}, f32[8,256]{1,0:T(8,128)S(1)}, f32[1,8,256]{2,1,0:T(8,128)S(1)}) custom-call(s32[2]{0:T(128)S(1)} %pad_add_fusion.place, bf16[256,384]{1,0:T(8,128)(2,1)S(1)} %finish.1._.own, bf16[384,3072]{1,0:T(8,128)(2,1)S(1)} %copy-done, bf16[16,384]{1,0:T(8,128)(2,1)S(1)} %get-tuple-element.14.sums), custom_call_target="tpu_custom_call" | custom-call | tf_op jit(solution)/shard_map/project_early/pallas_call | solution.py:375
  51.8 0.6 %merge_w.1.refs_1_ = bf16[1,416,1536]{2,1,0:T(8,128)(2,1)S(1)} custom-call(s32[2]{0:T(128)S(1)} %pad_add_fusion.place, bf16[1,208,1536]{2,1,0:T(8,128)(2,1)S(1)} %gate.9.mine, bf16[1,208,1536]{2,1,0:T(8,128)(2,1)S(1)} %collective-permute-done.13.sibling), custom_call_target="tpu_custom_call" | custom-call | tf_op jit(solution)/shard_map/merge_w/pallas_call | solution.py:191
  52.5 4.0 %collective-permute-done.11.refs_0_ = bf16[256,384]{1,0:T(8,128)(2,1)S(1)} collective-permute-done((bf16[256,384]{1,0:T(8,128)(2,1)S(1)}, bf16[256,384]{1,0:T(8,128)(2,1)S(1)}, u32[]{:S(2)}, u32[]{:S(2)}) %collective-permute-start.11) | collective-permute-done | bytes 196640 | tf_op jit(solution)/shard_map/ppermute | solution.py:457
  56.4 1.9 %project_last.1 = (bf16[256,1536]{1,0:T(8,128)(2,1)}, f32[1,256]{1,0:T(1,128)}) custom-call(bf16[256,384]{1,0:T(8,128)(2,1)S(1)} %collective-permute-done.11.refs_0_, bf16[1,416,1536]{2,1,0:T(8,128)(2,1)S(1)} %merge_w.1.refs_1_, f32[256,1536]{1,0:T(8,128)S(1)} %get-tuple-element.15.refs_2_, f32[8,256]{1,0:T(8,128)S(1)} %get-tuple-element.16.refs_3_, ...), custom_call_target="tpu_custom_call" | custom-call | tf_op jit(solution)/shard_map/project_last/pallas_call | solution.py:427
  (28 shorter events, 0.4 us)
Async XLA Ops:
  0.6 13.1 %copy-start.4 = (s32[16]{0:T(128)S(1)}, s32[16]{0:T(128)}, u32[]{:S(2)}) copy-start(s32[16]{0:T(128)} %window.3) | copy-start | bytes 196
  6.3 9.2 %collective-permute-start.2 = (bf16[512,384]{1,0:T(8,128)(2,1)}, bf16[512,384]{1,0:T(8,128)(2,1)}, u32[]{:S(2)}, u32[]{:S(2)}) collective-permute-start(bf16[512,384]{1,0:T(8,128)(2,1)} %get-tuple-element.12.refs_0_), channel_id=1, source_target_pairs={{0,2},{2,0},{4,6},{6,4},{8,10},{10,8},{12,14},{14,12},{16,18},{18,... | collective-permute-start | bytes 1179656 | tf_op jit(solution)/shard_map/ppermute | solution.py:454
  6.9 14.4 %collective-permute-start.1 = (bf16[512,384]{1,0:T(8,128)(2,1)}, bf16[512,384]{1,0:T(8,128)(2,1)S(1)}, u32[]{:S(2)}, u32[]{:S(2)}) collective-permute-start(bf16[512,384]{1,0:T(8,128)(2,1)} %get-tuple-element.12.refs_0_), channel_id=1, source_target_pairs={{0,4},{2,6},{4,0},{6,2},{8,12},{10,14},{12,8},{14,10},{16,20},{18,... | collective-permute-start | bytes 1179656 | tf_op jit(solution)/shard_map/ppermute | solution.py:454
  9.4 16.6 %collective-permute-start.3 = (bf16[512,384]{1,0:T(8,128)(2,1)}, bf16[512,384]{1,0:T(8,128)(2,1)S(1)}, u32[]{:S(2)}, u32[]{:S(2)}) collective-permute-start(bf16[512,384]{1,0:T(8,128)(2,1)} %get-tuple-element.12.refs_0_), channel_id=1, source_target_pairs={{0,8},{2,10},{4,12},{6,14},{8,0},{10,2},{12,4},{14,6},{16,24},{18,... | collective-permute-start | bytes 1179656 | tf_op jit(solution)/shard_map/ppermute | solution.py:454
  11.0 14.3 %collective-permute-start = (bf16[272,384]{1,0:T(8,128)(2,1)}, bf16[272,384]{1,0:T(8,128)(2,1)S(1)}, u32[]{:S(2)}, u32[]{:S(2)}) collective-permute-start(bf16[272,384]{1,0:T(8,128)(2,1)} %get-tuple-element.11.queries._), channel_id=1, source_target_pairs={{0,16},{2,18},{4,20},{6,22},{8,24},{10,26},{12,28},{14,30},{16,0},... | collective-permute-start | bytes 626696 | tf_op jit(solution)/shard_map/ppermute | solution.py:454
  13.7 0.9 %copy-start.1 = (bf16[272,384]{1,0:T(8,128)(2,1)S(1)}, bf16[272,384]{1,0:T(8,128)(2,1)}, u32[]{:S(2)}) copy-start(bf16[272,384]{1,0:T(8,128)(2,1)} %get-tuple-element.11.queries._) | copy-start | bytes 626692
  14.6 0.9 %copy-start.2 = (bf16[272,384]{1,0:T(8,128)(2,1)S(1)}, bf16[272,384]{1,0:T(8,128)(2,1)}, u32[]{:S(2)}) copy-start(bf16[272,384]{1,0:T(8,128)(2,1)} %get-tuple-element.11.queries._) | copy-start | bytes 626692
  15.5 2.9 %copy-start = (bf16[384,3072]{1,0:T(8,128)(2,1)S(1)}, bf16[384,3072]{1,0:T(8,128)(2,1)}, u32[]{:S(2)}) copy-start(bf16[384,3072]{1,0:T(8,128)(2,1)} %w_out.3) | copy-start | bytes 7077892
  15.6 1.1 %copy-start.3 = (bf16[512,384]{1,0:T(8,128)(2,1)S(1)}, bf16[512,384]{1,0:T(8,128)(2,1)}, u32[]{:S(2)}) copy-start(bf16[512,384]{1,0:T(8,128)(2,1)} %get-tuple-element.12.refs_0_) | copy-start | bytes 1179652
  19.7 29.3 %collective-permute-start.12 = (bf16[1,208,1536]{2,1,0:T(8,128)(2,1)S(1)}, bf16[1,208,1536]{2,1,0:T(8,128)(2,1)S(1)}, u32[]{:S(2)}, u32[]{:S(2)}) collective-permute-start(bf16[1,208,1536]{2,1,0:T(8,128)(2,1)S(1)} %get-tuple-element.13), channel_id=1, source_target_pairs={{0,1},{1,0},{2,3},{3,2},{4,5},{5,4},{6,7},{7,6},{8,9},{9,8},{10,11... | collective-permute-start | bytes 1916936 | tf_op jit(solution)/shard_map/ppermute | solution.py:457
  21.3 8.2 %collective-permute-start.7 = (bf16[256,384]{1,0:T(8,128)(2,1)S(1)}, bf16[256,384]{1,0:T(8,128)(2,1)S(1)}, u32[]{:S(2)}, u32[]{:S(2)}) collective-permute-start(bf16[256,384]{1,0:T(8,128)(2,1)S(1)} %slice.9), channel_id=1, source_target_pairs={{0,8},{2,10},{4,12},{6,14},{8,0},{10,2},{12,4},{14,6},{16,24},{18,... | collective-permute-start | bytes 589832 | tf_op jit(solution)/shard_map/ppermute | solution.py:454
  26.1 7.5 %collective-permute-start.4 = (bf16[512,384]{1,0:T(8,128)(2,1)S(1)}, bf16[512,384]{1,0:T(8,128)(2,1)S(1)}, u32[]{:S(2)}, u32[]{:S(2)}) collective-permute-start(bf16[512,384]{1,0:T(8,128)(2,1)S(1)} %gate.6.refs_2_.refs_0_), channel_id=1, source_target_pairs={{0,2},{2,0},{4,6},{6,4},{8,10},{10,8},{12,14},{14,12},{16,18},{18,... | collective-permute-start | bytes 1179656 | tf_op jit(solution)/shard_map/ppermute | solution.py:454
  26.2 7.4 %collective-permute-start.5 = (bf16[512,384]{1,0:T(8,128)(2,1)S(1)}, bf16[512,384]{1,0:T(8,128)(2,1)S(1)}, u32[]{:S(2)}, u32[]{:S(2)}) collective-permute-start(bf16[512,384]{1,0:T(8,128)(2,1)S(1)} %gate.5._.refs_3_.refs_1_), channel_id=1, source_target_pairs={{0,2},{2,0},{4,6},{6,4},{8,10},{10,8},{12,14},{14,12},{16,18},{18,... | collective-permute-start | bytes 1179656 | tf_op jit(solution)/shard_map/ppermute | solution.py:454
  26.7 6.9 %collective-permute-start.6 = (bf16[256,384]{1,0:T(8,128)(2,1)S(1)}, bf16[256,384]{1,0:T(8,128)(2,1)S(1)}, u32[]{:S(2)}, u32[]{:S(2)}) collective-permute-start(bf16[256,384]{1,0:T(8,128)(2,1)S(1)} %slice.8), channel_id=1, source_target_pairs={{0,4},{2,6},{4,0},{6,2},{8,12},{10,14},{12,8},{14,10},{16,20},{18,... | collective-permute-start | bytes 589832 | tf_op jit(solution)/shard_map/ppermute | solution.py:454
  29.5 5.0 %collective-permute-start.9 = (bf16[256,384]{1,0:T(8,128)(2,1)S(1)}, bf16[256,384]{1,0:T(8,128)(2,1)S(1)}, u32[]{:S(2)}, u32[]{:S(2)}) collective-permute-start(bf16[256,384]{1,0:T(8,128)(2,1)S(1)} %gate.8.refs_3_.refs_5_), channel_id=1, source_target_pairs={{0,2},{2,0},{4,6},{6,4},{8,10},{10,8},{12,14},{14,12},{16,18},{18,... | collective-permute-start | bytes 589832 | tf_op jit(solution)/shard_map/ppermute | solution.py:454
  33.6 1.4 %collective-permute-start.8 = (bf16[256,384]{1,0:T(8,128)(2,1)S(1)}, bf16[256,384]{1,0:T(8,128)(2,1)S(1)}, u32[]{:S(2)}, u32[]{:S(2)}) collective-permute-start(bf16[256,384]{1,0:T(8,128)(2,1)S(1)} %gate.7.refs_2_.refs_4_), channel_id=1, source_target_pairs={{0,2},{2,0},{4,6},{6,4},{8,10},{10,8},{12,14},{14,12},{16,18},{18,... | collective-permute-start | bytes 589832 | tf_op jit(solution)/shard_map/ppermute | solution.py:454
  35.6 13.3 %collective-permute-start.10 = (bf16[272,384]{1,0:T(8,128)(2,1)S(1)}, bf16[272,384]{1,0:T(8,128)(2,1)S(1)}, u32[]{:S(2)}, u32[]{:S(2)}) collective-permute-start(bf16[272,384]{1,0:T(8,128)(2,1)S(1)} %other_last.1._), channel_id=1, source_target_pairs={{0,16},{2,18},{4,20},{6,22},{8,24},{10,26},{12,28},{14,30},{16,0},... | collective-permute-start | bytes 626696 | tf_op jit(solution)/shard_map/ppermute | solution.py:454
  49.0 2.8 %collective-permute-start.13 = (bf16[1,208,1536]{2,1,0:T(8,128)(2,1)S(1)}, bf16[1,208,1536]{2,1,0:T(8,128)(2,1)S(1)}, u32[]{:S(2)}, u32[]{:S(2)}) collective-permute-start(bf16[1,208,1536]{2,1,0:T(8,128)(2,1)S(1)} %gate.9.mine), channel_id=1, source_target_pairs={{0,2},{2,0},{4,6},{6,4},{8,10},{10,8},{12,14},{14,12},{16,18},{18,... | collective-permute-start | bytes 1916936 | tf_op jit(solution)/shard_map/ppermute | solution.py:454
  49.1 7.3 %collective-permute-start.11 = (bf16[256,384]{1,0:T(8,128)(2,1)S(1)}, bf16[256,384]{1,0:T(8,128)(2,1)S(1)}, u32[]{:S(2)}, u32[]{:S(2)}) collective-permute-start(bf16[256,384]{1,0:T(8,128)(2,1)S(1)} %finish.1._.own), channel_id=1, source_target_pairs={{0,1},{1,0},{2,3},{3,2},{4,5},{5,4},{6,7},{7,6},{8,9},{9,8},{10,11... | collective-permute-start | bytes 589832 | tf_op jit(solution)/shard_map/ppermute | solution.py:457

commit v3 on v2

v3 whole, which is shorter than its diff:
```python
import functools

import jax
import jax.numpy as jnp
from jax import lax
from jax.experimental import pallas as pl
from jax.experimental.pallas import tpu as pltpu
from jax.sharding import PartitionSpec as P

D = 3072
HD = 128
BLK = 128
EPS = 1e-06
PAD = 16
BARRED = -1e30
F32 = jnp.float32
BF16 = jnp.bfloat16
VMEM = pltpu.VMEM
SMEM = pltpu.SMEM
MIB = 1024 * 1024
IN_VMEM = pl.BlockSpec(memory_space=VMEM)
IN_SMEM = pl.BlockSpec(memory_space=SMEM)
IN_HBM = pl.BlockSpec(memory_space=pltpu.HBM)
ANYWHERE = pl.BlockSpec(memory_space=pl.ANY)


def params(mib):
    return pltpu.CompilerParams(vmem_limit_bytes=mib * MIB)


def cost(microseconds):
    return pl.CostEstimate(
        flops=int(microseconds * 0), bytes_accessed=int(microseconds * 0), transcendentals=0
    )


def normed(values, gains, scale):
    parts = []
    for first in range(0, values.shape[1], HD):
        head = values[:, first : first + HD]
        factor = lax.rsqrt(jnp.mean(head * head, axis=-1, keepdims=True) + EPS)
        parts.append(head * factor * gains[:, first : first + HD] * scale)
    return jnp.concatenate(parts, axis=1)


def project_kernel(steps, n_head, tokens, w_qkv, gains, near_mask, far_pattern, w_out, *refs):
    kv, queries, payload = refs[:3]
    token_buf, w_buf, gain_buf, near_buf, far_buf, total, out_buf, sems, small_sems, out_sems = refs[3:]
    rows, width = tokens.shape
    count, _, cols = w_qkv.shape
    deep = width // steps
    copies = []
    for s in range(steps):
        span = pl.ds(s * deep, deep)
        group = [pltpu.make_async_copy(tokens.at[:, span], token_buf.at[:, span], sems.at[0, s])]
        for j in range(count):
            group.append(
                pltpu.make_async_copy(
                    w_qkv.at[j, span], w_buf.at[span, pl.ds(j * cols, cols)], sems.at[1 + j, s]
                )
            )
        for copy in group:
            copy.start()
        copies.append(group)
    small = [
        pltpu.make_async_copy(source, target, small_sems.at[i])
        for i, (source, target) in enumerate(
            ((gains, gain_buf), (near_mask, near_buf), (far_pattern, far_buf))
        )
    ]
    for copy in small:
        copy.start()
    out_cols = payload.shape[2]
    place = lax.axis_index("head")
    columns = []
    for k in range(1, n_head):
        first = pl.multiple_of(lax.rem(place + k, n_head) * out_cols, HD)
        columns.append(
            (
                pltpu.make_async_copy(
                    w_out.at[:, pl.ds(first, out_cols)], out_buf.at[k - 1], out_sems.at[0, k - 1]
                ),
                pltpu.make_async_copy(out_buf.at[k - 1], payload.at[k - 1], out_sems.at[1, k - 1]),
            )
        )
    for load, _ in columns:
        load.start()
    for s in range(steps):
        for copy in copies[s]:
            copy.wait()
        span = slice(s * deep, (s + 1) * deep)
        part = jnp.dot(token_buf[:, span], w_buf[span, :], preferred_element_type=F32)
        if s == 0:
            total[...] = part
        elif s < steps - 1:
            total[...] += part
    part = total[...] + part
    for load, store in columns:
        load.wait()
        store.start()
    for copy in small:
        copy.wait()
    query, key, value = (part[:, j * cols : (j + 1) * cols] for j in range(count))
    kv[:rows, :] = normed(key, gain_buf[1:2, :], 1.0).astype(BF16)
    kv[rows:, :] = value.astype(BF16)
    queries[:rows, :] = normed(query, gain_buf[0:1, :], HD ** (-0.5)).astype(BF16)
    n_blocks, n_near = near_mask.shape
    queries[rows:, :] = jnp.zeros((PAD, cols), BF16)
    queries[rows : rows + n_blocks, :n_near] = near_buf[...].astype(F32).astype(BF16)
    queries[rows : rows + n_blocks, HD : HD + far_pattern.shape[1]] = (
        far_buf[...].astype(F32).astype(BF16)
    )
    for _, store in columns:
        store.wait()


def project(tokens, w_qkv, gains, near_mask, far_pattern, w_out, n_head):
    rows, width = tokens.shape
    count, _, cols = w_qkv.shape
    steps = 4
    return pl.pallas_call(
        functools.partial(project_kernel, steps, n_head),
        in_specs=[ANYWHERE] * 6,
        out_specs=[IN_VMEM] * 2 + [ANYWHERE],
        out_shape=[
            jax.ShapeDtypeStruct((2 * rows, cols), BF16),
            jax.ShapeDtypeStruct((rows + PAD, cols), BF16),
            jax.ShapeDtypeStruct((n_head - 1, w_out.shape[0], w_out.shape[1] // n_head), BF16),
        ],
        scratch_shapes=[
            VMEM((rows, width), BF16),
            VMEM((width, count * cols), BF16),
            VMEM(gains.shape, F32),
            VMEM(near_mask.shape, jnp.int32),
            VMEM(far_pattern.shape, jnp.int32),
            VMEM((rows, count * cols), F32),
            VMEM((n_head - 1, w_out.shape[0], w_out.shape[1] // n_head), BF16),
            pltpu.SemaphoreType.DMA((1 + count, steps)),
            pltpu.SemaphoreType.DMA((3,)),
            pltpu.SemaphoreType.DMA((2, n_head - 1)),
        ],
        compiler_params=params(56),
        cost_estimate=cost(5.0),
        name="project",
    )(tokens, w_qkv, gains, near_mask, far_pattern, w_out)


def split_sum(values):
    high = values.astype(BF16).astype(F32)
    mid = (values - high).astype(BF16).astype(F32)
    return high, mid, values - high - mid


def sums_kernel(w_out, _, sums):
    rows, width = w_out.shape
    total = lax.dot_general(
        jnp.ones((8, width), BF16), w_out[...], (((1,), (1,)), ((), ())), preferred_element_type=F32
    )
    high, mid, low = split_sum(total)
    row = lax.broadcasted_iota(jnp.int32, (8, rows), 0)
    packed = jnp.where(row == 0, high, jnp.where(row == 1, mid, jnp.where(row == 2, low, 0.0)))
    sums[...] = jnp.concatenate([packed, jnp.zeros((PAD - 8, rows), F32)], axis=0).astype(BF16)


def row_sums(w_out, before):
    return pl.pallas_call(
        sums_kernel,
        in_specs=[IN_VMEM] * 2,
        out_specs=IN_VMEM,
        out_shape=jax.ShapeDtypeStruct((PAD, w_out.shape[0]), BF16),
        compiler_params=params(16),
        cost_estimate=cost(0.8),
        name="row_sums",
    )(w_out, before)


def bias_kernel(side, n_slabs, n_blocks, ids, window, queries, _, out):
    rows = n_blocks * BLK
    shifted = lax.broadcasted_iota(jnp.int32, (BLK, BLK), 0) - lax.broadcasted_iota(
        jnp.int32, (BLK, BLK), 1
    )
    gaps = {
        by: jnp.abs(shifted + by * BLK).astype(F32) for by in range(1 - n_blocks, n_blocks)
    }
    lane = lax.broadcasted_iota(jnp.int32, (PAD, queries.shape[1]), 1)
    masks = queries[rows : rows + PAD, :].astype(F32)
    query_slab = ids[side]
    for c in range(n_slabs):
        key_slab = ids[4 + c]
        distance = jnp.abs(key_slab - query_slab)
        before = jnp.where(key_slab < query_slab, 0, 1)
        first = jnp.where(distance == 1, before * n_blocks, HD + key_slab * n_blocks)
        whole = jnp.where(distance == 0, 1.0, 0.0)
        reach = window[distance].astype(F32)
        for j in range(n_blocks):
            picked = jnp.sum(jnp.where(lane == first + j, masks, 0.0), axis=1, keepdims=True)
            limit = jnp.where(jnp.maximum(picked, whole) > 0.5, reach, 0.0)
            for i in range(n_blocks):
                here = jnp.broadcast_to(limit[i : i + 1, :], (BLK, BLK))
                out[c, i * BLK : (i + 1) * BLK, j * BLK : (j + 1) * BLK] = jnp.where(
                    gaps[i - j] < here, 0.0, BARRED
                )


def biases(side, ids, window, queries, n_blocks, before):
    n_slabs = ids.shape[0] - 4
    rows = n_blocks * BLK
    return pl.pallas_call(
        functools.partial(bias_kernel, side, n_slabs, n_blocks),
        in_specs=[IN_SMEM] * 2 + [IN_VMEM] * 2,
        out_specs=IN_VMEM,
        out_shape=jax.ShapeDtypeStruct((n_slabs, rows, rows), F32),
        compiler_params=params(16),
        cost_estimate=cost(0.5),
        name="biases",
    )(ids, window, queries, before)


def attend_body(slabs, packed, heads, bias, queries, chunks, before, out):
    rows = bias.shape[1]
    ones = jnp.ones((rows, HD), BF16)
    if packed:
        out[rows:, :] = jnp.zeros((PAD, out.shape[1]), BF16)
    for h in range(*heads):
        span = slice(h * HD, (h + 1) * HD)
        keys = jnp.concatenate([key[:, span] for key, _ in chunks], axis=0)
        scores = lax.dot_general(
            queries[:rows, span], keys, (((1,), (1,)), ((), ())), preferred_element_type=F32
        )
        weights = [
            jnp.exp(scores[:, n * rows : (n + 1) * rows] + bias[slab]).astype(BF16)
            for n, slab in enumerate(slabs)
        ]
        values = jnp.concatenate(
            [jnp.concatenate([value[:, span], ones], axis=1) for _, value in chunks], axis=0
        )
        sums = jnp.dot(jnp.concatenate(weights, axis=1), values, preferred_element_type=F32)
        if before is not None:
            sums = sums + before[h]
        if not packed:
            out[h] = sums
            continue
        span = slice((h - heads[0]) * HD, (h - heads[0] + 1) * HD)
        out[:rows, span] = sums[:, :HD].astype(BF16)
        for b in range(rows // HD):
            pack_denominator(out, rows, b, span, sums[b * HD : (b + 1) * HD, HD:])


def taken_chunks(lone, rows, refs):
    chunks = []
    for apart in lone:
        if apart:
            keys, values = refs.pop(0), refs.pop(0)
            chunks.append((keys.at[:rows], values.at[values.shape[0] - rows :]))
        else:
            both = refs.pop(0)
            chunks.append((both.at[:rows], both.at[rows:]))
    return chunks


def attend_kernel(slabs, lone, has_totals, heads, bias, queries, _, *refs):
    refs = list(refs)
    chunks = taken_chunks(lone, bias.shape[1], refs)
    before, out = (refs[0], refs[1]) if has_totals else (None, refs[0])
    attend_body(slabs, False, heads, bias, queries, chunks, before, out)


def pair_kernel(slabs, lone, heads, first_bias, first, second_bias, second, *refs):
    refs = list(refs)
    rows = first_bias.shape[1]
    chunks = taken_chunks(lone, rows, refs)
    first_totals, second_totals, out = refs
    held = rows + PAD
    attend_body(slabs, True, heads, first_bias, first, chunks, first_totals, out.at[:held])
    attend_body(slabs, True, heads, second_bias, second, chunks, second_totals, out.at[held:])


def attend_pair(first, second, parts, heads, name):
    rows = first[0].shape[1]
    operands = [first[0], first[1], second[0], second[1]]
    operands += [array for chunk, _ in parts for array in chunk] + [first[2], second[2]]
    return pl.pallas_call(
        functools.partial(
            pair_kernel, [slab for _, slab in parts], [len(c) > 1 for c, _ in parts], heads
        ),
        in_specs=[IN_VMEM] * len(operands),
        out_specs=IN_VMEM,
        out_shape=jax.ShapeDtypeStruct((2 * (rows + PAD), (heads[1] - heads[0]) * HD), BF16),
        compiler_params=params(24),
        cost_estimate=cost(0.6),
        name=name,
    )(*operands)


def attend(bias, queries, before, parts, totals, heads, name):
    rows = bias.shape[1]
    operands = [bias, queries, before] + [array for chunk, _ in parts for array in chunk]
    if totals is not None:
        operands.append(totals)
    count = heads[1] - heads[0]
    shape = jax.ShapeDtypeStruct((count, rows, 2 * HD), F32)
    slabs = [slab for _, slab in parts]
    return pl.pallas_call(
        functools.partial(
            attend_kernel, slabs, [len(c) > 1 for c, _ in parts], totals is not None, heads
        ),
        in_specs=[IN_VMEM] * len(operands),
        out_specs=IN_VMEM,
        out_shape=shape,
        compiler_params=params(24),
        cost_estimate=cost(0.08 * len(parts) * count + 0.15),
        name=name,
    )(*operands)


def packed_sums(packed, first, rows, block, span):
    here = slice(first + block * HD, first + (block + 1) * HD)
    pair = packed[first + rows : first + rows + PAD, span].astype(F32)
    row = pair[2 * block : 2 * block + 1, :] + pair[2 * block + 1 : 2 * block + 2, :]
    return packed[here, span].astype(F32), jnp.broadcast_to(row, (HD, HD)).T


def pack_denominator(out, rows, block, span, denominator):
    row = denominator.T[0:1, :]
    high = row.astype(BF16)
    out[rows + 2 * block : rows + 2 * block + 1, span] = high
    out[rows + 2 * block + 1 : rows + 2 * block + 2, span] = (row - high.astype(F32)).astype(BF16)


def join_kernel(last, firsts, kept, *refs):
    got, out = refs[:-2], refs[-1]
    heads, rows, _ = kept.shape
    if not last:
        out[rows:, :] = jnp.zeros((PAD, out.shape[1]), BF16)
    for h in range(heads):
        span = slice(h * HD, (h + 1) * HD)
        for b in range(rows // HD):
            here = slice(b * HD, (b + 1) * HD)
            num, den = kept[h, here, :HD], kept[h, here, HD:]
            for first, packed in zip(firsts, got):
                more_num, more_den = packed_sums(packed, first, rows, b, span)
                num, den = num + more_num, den + more_den
            if last:
                out[here, span] = (num / den).astype(BF16)
            else:
                out[here, span] = num.astype(BF16)
                pack_denominator(out, rows, b, span, den)


def join(kept, got, last, before):
    heads, rows, _ = kept.shape
    return pl.pallas_call(
        functools.partial(join_kernel, last, [first for _, first in got]),
        in_specs=[IN_VMEM] * (2 + len(got)),
        out_specs=IN_VMEM,
        out_shape=jax.ShapeDtypeStruct((rows + (0 if last else PAD), heads * HD), BF16),
        compiler_params=params(16),
        cost_estimate=cost(0.15),
        name="finish" if last else "join",
    )(kept, *[array for array, _ in got], before)


def gate_kernel(array, _, out):
    pass


def gate(array, before):
    return pl.pallas_call(
        gate_kernel,
        in_specs=[ANYWHERE, IN_VMEM],
        out_specs=ANYWHERE,
        out_shape=jax.ShapeDtypeStruct(array.shape, array.dtype),
        input_output_aliases={0: 0},
        compiler_params=params(16),
        cost_estimate=cost(0.1),
        name="gate",
    )(array, before)


def row_dot(summed, values):
    dots = lax.dot_general(
        summed, values, (((1,), (1,)), ((), ())), preferred_element_type=F32
    )
    return dots[0:1, :] + (dots[1:2, :] + dots[2:3, :])


def early_kernel(n_head, place, own, w_out, sums, received, partial, parts, owners, held):
    cols = partial.shape[1]
    first = pl.multiple_of(place[0] * cols, HD)
    partial[...] = jnp.dot(own[...], w_out[:, pl.ds(first, cols)], preferred_element_type=F32)
    held[...] = received[...]
    parts[...] = jnp.zeros(parts.shape, F32)
    parts[pl.ds(place[0], 1), :] = row_dot(sums[...], own[...])
    row = lax.broadcasted_iota(jnp.int32, parts.shape, 0)
    for k in range(1, n_head):
        owner = lax.rem(place[0] - k + n_head, n_head)
        owners[k - 1] = jnp.where(row == owner, 1.0, 0.0)


def project_early(place, own, w_out, sums, received, n_head):
    rows = own.shape[0]
    cols = w_out.shape[1] // n_head
    places = -(-n_head // 8) * 8
    return pl.pallas_call(
        functools.partial(early_kernel, n_head),
        in_specs=[IN_SMEM] + [IN_VMEM] * 4,
        out_specs=[IN_VMEM] * 4,
        out_shape=[
            jax.ShapeDtypeStruct((rows, cols), F32),
            jax.ShapeDtypeStruct((places, rows), F32),
            jax.ShapeDtypeStruct((n_head - 1, places, rows), F32),
            jax.ShapeDtypeStruct(received.shape, BF16),
        ],
        compiler_params=params(24),
        cost_estimate=cost(1.4),
        name="project_early",
    )(place, own, w_out, sums, received)


def last_kernel(n_head, *refs):
    late, refs = refs[: n_head - 1], refs[n_head - 1 :]
    received, sums, partial, parts, owners, layer_out, checksum, staged, sems = refs
    rows, cols = partial.shape
    tiles = sems.shape[0]
    tile = cols // tiles
    stores = []
    for t in range(tiles):
        here = slice(t * tile, (t + 1) * tile)
        total = partial[:, here]
        for k in range(1, n_head):
            total = total + jnp.dot(
                late[k - 1][...], received[k - 1, :, here], preferred_element_type=F32
            )
        staged[:, here] = total.astype(BF16)
        there = pl.ds(t * tile, tile)
        store = pltpu.make_async_copy(staged.at[:, there], layer_out.at[:, there], sems.at[t])
        store.start()
        stores.append(store)
    every = parts[...]
    for k in range(1, n_head):
        dot = row_dot(sums[(k - 1) * PAD : k * PAD, :], late[k - 1][...])
        every = every + owners[k - 1] * dot
    sum_all = every[0:1, :]
    for k in range(1, n_head):
        sum_all = sum_all + every[k : k + 1, :]
    checksum[...] = sum_all * D ** (-0.5)
    for store in stores:
        store.wait()


def project_last(late, received, sums, partial, parts, owners):
    n_head = len(late) + 1
    rows, cols = partial.shape
    tiles = next(t for t in (3, 2, 1) if cols % (t * HD) == 0)
    operands = [*late, received, sums, partial, parts, owners]
    layer_out, checksum = pl.pallas_call(
        functools.partial(last_kernel, n_head),
        in_specs=[IN_VMEM] * len(operands),
        out_specs=[ANYWHERE, IN_VMEM],
        out_shape=[
            jax.ShapeDtypeStruct((rows, cols), BF16),
            jax.ShapeDtypeStruct((1, rows), F32),
        ],
        scratch_shapes=[VMEM((rows, cols), BF16), pltpu.SemaphoreType.DMA((tiles,))],
        compiler_params=params(24),
        name="project_last",
    )(*operands)
    return layer_out, checksum.reshape(rows)


def per_device(tokens, w_qkv, norm_gains, w_out, near_mask, far_pattern, window):
    rows = tokens.shape[0]
    heads = w_qkv.shape[2] // HD
    n_blocks = rows // BLK
    frame = lax.axis_index("frame").astype(jnp.int32)
    place = lax.axis_index("head").astype(jnp.int32).reshape(1)
    n_frame = lax.axis_size("frame")
    n_head = lax.axis_size("head")
    half = n_frame // 2
    every = (0, heads)

    def swapped(array, by):
        return lax.ppermute(array, "frame", [(i, i ^ by) for i in range(n_frame)])

    def from_head(array, k):
        return lax.ppermute(array, "head", [(i, (i + k) % n_head) for i in range(n_head)])

    def from_heads(arrays):
        got = [from_head(array, k) for k, array in enumerate(arrays, 1)]
        return got[0] if len(got) == 1 else jnp.concatenate(got)

    spans = []
    by = half // 2
    while by > 1:
        spans.append(by)
        by //= 2
    far = sorted((o for o in range(2, half, 2) if o not in spans), key=lambda o: bin(o).count("1"))
    slabs = [0] + spans + far
    n_near = 1 + len(spans)

    kv, queries, payload = project(
        tokens, w_qkv, norm_gains, near_mask, far_pattern, w_out, n_head
    )
    near = {by: swapped(kv, by) for by in spans}
    sib_queries = swapped(queries, 1)
    ids = jnp.stack([frame ^ o for o in [0, 1, half, half ^ 1] + slabs])

    def bias_of(side, array, before):
        return biases(side, ids, window, array, n_blocks, before)

    mine = [((kv,), 0)]
    own_bias = bias_of(0, queries, queries)
    own = attend(own_bias, queries, own_bias, mine, None, every, "attend_first")
    other_queries = swapped(gate(queries, own), half)
    payload = gate(payload, own)
    received = from_heads([payload[k - 1 : k] for k in range(1, n_head)])
    sib_bias = bias_of(1, sib_queries, own)
    sib = attend(sib_bias, sib_queries, sib_bias, mine, None, every, "sibling_first")

    low = spans[-1]
    near[low] = gate(near[low], sib)
    for by in spans[:-1]:
        near[by] = gate(near[by], near[low])
    margin = 2 * PAD
    keys = {by: near[by][: rows + margin] for by in spans}
    values = {by: near[by][rows - margin :] for by in spans}
    for o in far:
        bits = [by for by in spans if o & by]
        values[o] = swapped(values[o ^ bits[0]], bits[0])
        keys[o] = swapped(keys[o ^ bits[-1]], bits[-1])
    early = [((near[by],), i) for i, by in enumerate(spans, 1)]
    sib = attend(sib_bias, sib_queries, sib_bias, early, sib, every, "sibling_second")
    own = attend(own_bias, queries, sib, early, own, every, "attend_second")
    other_bias = bias_of(2, other_queries, own)
    other_queries = gate(other_queries, other_bias)
    other_sib = swapped(other_queries, 1)
    early = [((near[by],), i) for i, by in enumerate(spans, 1)]
    other = attend(
        other_bias, other_queries, other_bias, mine + early, None, every, "other_first"
    )
    other_sib_bias = bias_of(3, other_sib, other)
    both = attend(other_sib_bias, other_sib, other, mine + early, None, every, "other_sibling_first")
    late = []
    for i, o in enumerate(far, n_near):
        late.append(((gate(keys[o], both), gate(values[o], both)), i))
    across = attend_pair(
        (other_sib_bias, other_sib, both), (sib_bias, sib_queries, sib), late, every, "attend_pair"
    )
    other = attend(other_bias, other_queries, across, late, other, every, "other_last")
    own = attend(own_bias, queries, other, late, own, every, "attend_last")
    from_core = swapped(across, 1)
    sent = join(other, [(from_core, 0)], False, own)
    got = swapped(sent, half)
    sums = row_sums(w_out, sent)
    done = join(own, [(from_core, rows + PAD), (got, 0)], True, sums)
    other_sums = from_heads([sums] * (n_head - 1))
    late = [from_head(done, k) for k in range(1, n_head)]
    partial, sum_parts, owners, received = project_early(
        place, done, w_out, sums, received, n_head
    )
    return project_last(late, received, other_sums, partial, sum_parts, owners)


def solution(mesh):
    in_specs = (
        P("frame", None),
        P(None, None, "head"),
        P(None, "head"),
        P("head", None),
        P("frame", None),
        P("frame", None),
        P(),
    )
    out_specs = (P("frame", "head"), P("frame"))
    return jax.shard_map(
        per_device, mesh=mesh, in_specs=in_specs, out_specs=out_specs, check_vma=False
    )
```

time: 58.5 us -> 56.1 us (0.959)
  waiting for transfers between devices: 20.7 us -> 18.2 us
  starting transfers between devices: 15.4 us -> 14.2 us
  Pallas kernels: 19.1 us -> 20.3 us
    ppermute x12 -> x9, starting transfers between devices: 12.3 us -> 10.6 us  [swapped(): return lax.ppermute(array, 'frame', [(i, i ^ by) for i in range(n_frame)])]
    pallas_call x5 -> x8, Pallas kernels: 6.72 us -> 5.11 us  [attend(): pl.pallas_call(functools.partial(attend_kernel, slabs, [len(c) > 1 for c,...]
    ppermute x2 -> x3, waiting for transfers between devices: 3.97 us -> 2.64 us  [from_head(): lax.ppermute(array, 'head', [(i, (i + k) % n_head) for i in range(n_head)])]
    pallas_call x2 -> x4, Pallas kernels: 1.57 us -> 2.84 us  [biases(): pl.pallas_call(functools.partial(bias_kernel, side, n_slabs, n_blocks), i...]
    ppermute x12 -> x9, waiting for transfers between devices: 16.7 us -> 15.5 us  [swapped(): return lax.ppermute(array, 'frame', [(i, i ^ by) for i in range(n_frame)])]
    pallas_call x10 -> x13, Pallas kernels: 9.66 us -> 10.5 us  [the longest x1 6.46 us: project(): pl.pallas_call(functools.partial(project_kernel, steps, n_head), in_specs...]
    pallas_call x1, Pallas kernels: 1.13 us -> 1.92 us  [project_early(): pl.pallas_call(functools.partial(early_kernel, n_head), in_specs=[IN_SMEM...]
    ppermute x2 -> x3, starting transfers between devices: 3.11 us -> 3.6 us  [from_head(): lax.ppermute(array, 'head', [(i, (i + k) % n_head) for i in range(n_head)])]
  transfers between devices with their start and end apart: 14 -> 12, of which waited for: 6 -> 7; matrix products, arithmetic and copies ran while one was open for 0% -> 2% of each run, Pallas kernels for 20% -> 22%
where the time goes in v3:
time: 56.1 us; the launch traced here: 55.9 us
  Pallas kernels  20.3 us (36%)
  waiting for transfers between devices  18.2 us (32%)
  starting transfers between devices  14.2 us (25%)
  local copies, waits for them, and re-layouts  2.28 us (4%)
  between operations  0.83 us (1%)
    ppermute x9, waiting for transfers between devices, swapped(): return lax.ppermute(array, 'frame', [(i, i ^ by) for i in range(n_frame)])  15.5 us
    ppermute x9, starting transfers between devices, swapped(): return lax.ppermute(array, 'frame', [(i, i ^ by) for i in range(n_frame)])  10.6 us
    pallas_call x1, Pallas kernels, project(): pl.pallas_call(functools.partial(project_kernel, steps, n_head), in_specs...  6.46 us
    pallas_call x8, Pallas kernels, attend(): pl.pallas_call(functools.partial(attend_kernel, slabs, [len(c) > 1 for c,...  5.11 us
    ppermute x3, starting transfers between devices, from_head(): lax.ppermute(array, 'head', [(i, (i + k) % n_head) for i in range(n_head)])  3.6 us
    pallas_call x4, Pallas kernels, biases(): pl.pallas_call(functools.partial(bias_kernel, side, n_slabs, n_blocks), i...  2.84 us
    ppermute x3, waiting for transfers between devices, from_head(): lax.ppermute(array, 'head', [(i, (i + k) % n_head) for i in range(n_head)])  2.64 us
    unnamed x11, local copies, waits for them, and re-layouts  2.15 us
  transfers between devices with their start and end apart: 12, of which 7 were waited for; matrix products, arithmetic and copies ran while one was open for 2% of the time, Pallas kernels for 22%

profile of v3, /device:TPU:0, one launch (start us, length us, event | category | flops | bytes accessed | tf_op | source)
XLA Modules:
  0.0 55.9 jit_solution(17796487628613413136)
XLA Ops:
  0.6 6.5 %project.1 = (bf16[512,384]{1,0:T(8,128)(2,1)}, bf16[272,384]{1,0:T(8,128)(2,1)}, bf16[1,384,1536]{2,1,0:T(8,128)(2,1)}) custom-call(bf16[256,3072]{1,0:T(8,128)(2,1)} %tokens.1, bf16[3,3072,384]{2,1,0:T(8,128)(2,1)} %w_qkv.1, f32[2,384]{1,0:T(2,128)} %gains.1, s32[2,4]{1,0:T(2,128)} %near_mask.1, s32[2,32]{1,0:T(2,128)} %far_pattern.1, bf16[384,3072]{1,0:T(8,128)(2,1)} %w_out.5), custom_call_target="tpu_custom_call" | custom-call | tf_op jit(solution)/shard_map/project/pallas_call | solution.py:121
  7.1 3.0 %collective-permute-start.3 = (bf16[512,384]{1,0:T(8,128)(2,1)}, bf16[512,384]{1,0:T(8,128)(2,1)S(1)}, u32[]{:S(2)}, u32[]{:S(2)}) collective-permute-start(bf16[512,384]{1,0:T(8,128)(2,1)} %get-tuple-element.12.refs_0_), channel_id=1, source_target_pairs={{0,4},{2,6},{4,0},{6,2},{8,12},{10,14},{12,8},{14,10},{16,20},{18,... | collective-permute-start | bytes 1179656 | tf_op jit(solution)/shard_map/ppermute | solution.py:483
  10.2 1.6 %collective-permute-start.2 = (bf16[512,384]{1,0:T(8,128)(2,1)}, bf16[512,384]{1,0:T(8,128)(2,1)S(1)}, u32[]{:S(2)}, u32[]{:S(2)}) collective-permute-start(bf16[512,384]{1,0:T(8,128)(2,1)} %get-tuple-element.12.refs_0_), channel_id=1, source_target_pairs={{0,8},{2,10},{4,12},{6,14},{8,0},{10,2},{12,4},{14,6},{16,24},{18,... | collective-permute-start | bytes 1179656 | tf_op jit(solution)/shard_map/ppermute | solution.py:483
  11.7 0.9 %copy.16.array = bf16[272,384]{1,0:T(8,128)(2,1)S(1)} copy(bf16[272,384]{1,0:T(8,128)(2,1)} %get-tuple-element.11.queries._) | data formatting | bytes 417792
  12.8 0.9 %copy-done.1 = bf16[272,384]{1,0:T(8,128)(2,1)S(1)} copy-done((bf16[272,384]{1,0:T(8,128)(2,1)S(1)}, bf16[272,384]{1,0:T(8,128)(2,1)}, u32[]{:S(2)}) %copy-start.1) | copy-done | bytes 208920
  13.7 0.7 %biases.4.bias._ = f32[4,256,256]{2,1,0:T(8,128)S(1)} custom-call(s32[8]{0:T(128)S(1)} %stack.32.ids, s32[16]{0:T(128)S(1)} %copy-done.4, bf16[272,384]{1,0:T(8,128)(2,1)S(1)} %copy-done.1, bf16[272,384]{1,0:T(8,128)(2,1)S(1)} %copy-done.1), custom_call_target="tpu_custom_call" | custom-call | tf_op jit(solution)/shard_map/biases/pallas_call | solution.py:208
  14.7 0.5 attend_first.1._.refs_2_
  15.2 2.7 %collective-permute-start = (bf16[272,384]{1,0:T(8,128)(2,1)S(1)}, bf16[272,384]{1,0:T(8,128)(2,1)S(1)}, u32[]{:S(2)}, u32[]{:S(2)}) collective-permute-start(bf16[272,384]{1,0:T(8,128)(2,1)S(1)} %gate.7), channel_id=1, source_target_pairs={{0,16},{2,18},{4,20},{6,22},{8,24},{10,26},{12,28},{14,30},{16,0},... | collective-permute-start | bytes 626696 | tf_op jit(solution)/shard_map/ppermute | solution.py:483
  17.8 1.5 %collective-permute-start.10 = (bf16[1,384,1536]{2,1,0:T(8,128)(2,1)}, bf16[1,384,1536]{2,1,0:T(8,128)(2,1)}, u32[]{:S(2)}, u32[]{:S(2)}) collective-permute-start(bf16[1,384,1536]{2,1,0:T(8,128)(2,1)} %gate.13), channel_id=1, source_target_pairs={{0,1},{1,0},{2,3},{3,2},{4,5},{5,4},{6,7},{7,6},{8,9},{9,8},{10,11... | collective-permute-start | bytes 3538952 | tf_op jit(solution)/shard_map/ppermute | solution.py:486
  19.3 0.7 %biases.5.bias._.second_bias = f32[4,256,256]{2,1,0:T(8,128)S(1)} custom-call(s32[8]{0:T(128)S(1)} %stack.32.ids, s32[16]{0:T(128)S(1)} %copy-done.4, bf16[272,384]{1,0:T(8,128)(2,1)S(1)} %collective-permute-done.1.queries.second, f32[3,256,256]{2,1,0:T(8,128)S(1)} %attend_first.1._.refs_2_), custom_call_target="tpu_custom_call" | custom-call | tf_op jit(solution)/shard_map/biases/pallas_call | solution.py:208
  20.0 0.5 sibling_first.1._.refs_2_
  20.6 0.8 %collective-permute-start.6 = (bf16[288,384]{1,0:T(8,128)(2,1)S(1)}, bf16[288,384]{1,0:T(8,128)(2,1)S(1)}, u32[]{:S(2)}, u32[]{:S(2)}) collective-permute-start(bf16[288,384]{1,0:T(8,128)(2,1)S(1)} %slice.9), channel_id=1, source_target_pairs={{0,8},{2,10},{4,12},{6,14},{8,0},{10,2},{12,4},{14,6},{16,24},{18,... | collective-permute-start | bytes 663560 | tf_op jit(solution)/shard_map/ppermute | solution.py:483
  21.4 4.1 %collective-permute-done.2.array = bf16[512,384]{1,0:T(8,128)(2,1)S(1)} collective-permute-done((bf16[512,384]{1,0:T(8,128)(2,1)}, bf16[512,384]{1,0:T(8,128)(2,1)S(1)}, u32[]{:S(2)}, u32[]{:S(2)}) %collective-permute-start.2) | collective-permute-done | bytes 393248 | tf_op jit(solution)/shard_map/ppermute | solution.py:483
  25.8 0.7 %sibling_second.1._.refs_3_ = f32[3,256,256]{2,1,0:T(8,128)S(1)} custom-call(f32[4,256,256]{2,1,0:T(8,128)S(1)} %biases.5.bias._.second_bias, bf16[272,384]{1,0:T(8,128)(2,1)S(1)} %collective-permute-done.1.queries.second, f32[4,256,256]{2,1,0:T(8,128)S(1)} %biases.5.bias._.second_bias, bf16[512,384]{1,0:T(8,128)(2,1)S(1)} %gate.9.refs_0_.refs_1_, ...), custom_call_target="tpu_custom_call" | custom-call | tf_op jit(solution)/shard_map/sibling_second/pallas_call | solution.py:303
  26.5 0.7 %attend_second.1._.refs_2_ = f32[3,256,256]{2,1,0:T(8,128)S(1)} custom-call(f32[4,256,256]{2,1,0:T(8,128)S(1)} %biases.4.bias._, bf16[272,384]{1,0:T(8,128)(2,1)S(1)} %copy-done.2, f32[3,256,256]{2,1,0:T(8,128)S(1)} %sibling_second.1._.refs_3_, bf16[512,384]{1,0:T(8,128)(2,1)S(1)} %gate.9.refs_0_.refs_1_, bf16[512,384]{1,0:T(8,128)(2,1)S(1)} %gate.8._.refs_1_.refs_2_, ...), custom_call_target="tpu_custom_call" | custom-call | tf_op jit(solution)/shard_map/attend_second/pallas_call | solution.py:303
  27.5 0.7 %biases.6._.bias = f32[4,256,256]{2,1,0:T(8,128)S(1)} custom-call(s32[8]{0:T(128)S(1)} %stack.32.ids, s32[16]{0:T(128)S(1)} %copy-done.4, bf16[272,384]{1,0:T(8,128)(2,1)S(1)} %collective-permute-done.queries.array, f32[3,256,256]{2,1,0:T(8,128)S(1)} %attend_second.1._.refs_2_), custom_call_target="tpu_custom_call" | custom-call | tf_op jit(solution)/shard_map/biases/pallas_call | solution.py:208
  28.3 0.9 %other_first.1._.refs_2_ = f32[3,256,256]{2,1,0:T(8,128)S(1)} custom-call(f32[4,256,256]{2,1,0:T(8,128)S(1)} %biases.6._.bias, bf16[272,384]{1,0:T(8,128)(2,1)S(1)} %gate.10.queries, f32[4,256,256]{2,1,0:T(8,128)S(1)} %biases.6._.bias, bf16[512,384]{1,0:T(8,128)(2,1)S(1)} %copy-done.3, bf16[512,384]{1,0:T(8,128)(2,1)S(1)} %gate.9.refs_0_.refs_1_, ...), custom_call_target="tpu_custom_call" | custom-call | tf_op jit(solution)/shard_map/other_first/pallas_call | solution.py:303
  29.2 0.5 collective-permute-done.4.queries.first
  29.8 0.7 %biases.7.bias.first_bias = f32[4,256,256]{2,1,0:T(8,128)S(1)} custom-call(s32[8]{0:T(128)S(1)} %stack.32.ids, s32[16]{0:T(128)S(1)} %copy-done.4, bf16[272,384]{1,0:T(8,128)(2,1)S(1)} %collective-permute-done.4.queries.first, f32[3,256,256]{2,1,0:T(8,128)S(1)} %other_first.1._.refs_2_), custom_call_target="tpu_custom_call" | custom-call | tf_op jit(solution)/shard_map/biases/pallas_call | solution.py:208
  30.5 0.9 %other_sibling_first.1._.refs_2_ = f32[3,256,256]{2,1,0:T(8,128)S(1)} custom-call(f32[4,256,256]{2,1,0:T(8,128)S(1)} %biases.7.bias.first_bias, bf16[272,384]{1,0:T(8,128)(2,1)S(1)} %collective-permute-done.4.queries.first, f32[3,256,256]{2,1,0:T(8,128)S(1)} %other_first.1._.refs_2_, bf16[512,384]{1,0:T(8,128)(2,1)S(1)} %copy-done.3, ...), custom_call_target="tpu_custom_call" | custom-call | tf_op jit(solution)/shard_map/other_sibling_first/pallas_call | solution.py:303
  31.5 0.8 %attend_pair.1._ = bf16[544,384]{1,0:T(8,128)(2,1)S(1)} custom-call(f32[4,256,256]{2,1,0:T(8,128)S(1)} %biases.7.bias.first_bias, bf16[272,384]{1,0:T(8,128)(2,1)S(1)} %collective-permute-done.4.queries.first, f32[4,256,256]{2,1,0:T(8,128)S(1)} %biases.5.bias._.second_bias, bf16[272,384]{1,0:T(8,128)(2,1)S(1)} %collective-permute-done.1.queries.second, ...), custom_call_target="tpu_custom_call" | custom-call | tf_op jit(solution)/shard_map/attend_pair/pallas_call | solution.py:282
  32.4 0.5 other_last.1._.kept
  32.9 0.5 attend_last.1.refs_1_.kept
  33.4 0.7 %collective-permute-done.7.refs_0_ = bf16[544,384]{1,0:T(8,128)(2,1)S(1)} collective-permute-done((bf16[544,384]{1,0:T(8,128)(2,1)S(1)}, bf16[544,384]{1,0:T(8,128)(2,1)S(1)}, u32[]{:S(2)}, u32[]{:S(2)}) %collective-permute-start.7) | collective-permute-done | bytes 417824 | tf_op jit(solution)/shard_map/ppermute | solution.py:483
  34.0 0.4 join.1._
  34.4 2.1 %collective-permute-start.8 = (bf16[272,384]{1,0:T(8,128)(2,1)S(1)}, bf16[272,384]{1,0:T(8,128)(2,1)S(1)}, u32[]{:S(2)}, u32[]{:S(2)}) collective-permute-start(bf16[272,384]{1,0:T(8,128)(2,1)S(1)} %join.1._), channel_id=1, source_target_pairs={{0,16},{2,18},{4,20},{6,22},{8,24},{10,26},{12,28},{14,30},{16,0},... | collective-permute-start | bytes 626696 | tf_op jit(solution)/shard_map/ppermute | solution.py:483
  36.5 0.7 %row_sums.1.refs_2_.sums = bf16[16,384]{1,0:T(8,128)(2,1)S(1)} custom-call(bf16[384,3072]{1,0:T(8,128)(2,1)S(1)} %copy-done, bf16[272,384]{1,0:T(8,128)(2,1)S(1)} %join.1._), custom_call_target="tpu_custom_call" | custom-call | tf_op jit(solution)/shard_map/row_sums/pallas_call | solution.py:166
  37.3 9.8 %collective-permute-done.8.refs_1_ = bf16[272,384]{1,0:T(8,128)(2,1)S(1)} collective-permute-done((bf16[272,384]{1,0:T(8,128)(2,1)S(1)}, bf16[272,384]{1,0:T(8,128)(2,1)S(1)}, u32[]{:S(2)}, u32[]{:S(2)}) %collective-permute-start.8) | collective-permute-done | bytes 208928 | tf_op jit(solution)/shard_map/ppermute | solution.py:483
  47.3 2.0 %collective-permute-start.9 = (bf16[256,384]{1,0:T(8,128)(2,1)S(1)}, bf16[256,384]{1,0:T(8,128)(2,1)S(1)}, u32[]{:S(2)}, u32[]{:S(2)}) collective-permute-start(bf16[256,384]{1,0:T(8,128)(2,1)S(1)} %finish.1.own), channel_id=1, source_target_pairs={{0,1},{1,0},{2,3},{3,2},{4,5},{5,4},{6,7},{7,6},{8,9},{9,8},{10,11... | collective-permute-start | bytes 589832 | tf_op jit(solution)/shard_map/ppermute | solution.py:486
  49.4 1.9 %project_early.1 = (f32[256,1536]{1,0:T(8,128)S(1)}, f32[8,256]{1,0:T(8,128)S(1)}, f32[1,8,256]{2,1,0:T(8,128)S(1)}, bf16[1,384,1536]{2,1,0:T(8,128)(2,1)S(1)}) custom-call(s32[1]{0:T(128)} %bitcast.7.place, bf16[256,384]{1,0:T(8,128)(2,1)S(1)} %finish.1.own, bf16[384,3072]{1,0:T(8,128)(2,1)S(1)} %copy-done, bf16[16,384]{1,0:T(8,128)(2,1)S(1)} %row_sums.1.refs_2_.sums, ...), custom_call_target="tpu_custom_call" | custom-call | tf_op jit(solution)/shard_map/project_early/pallas_call | solution.py:404
  51.4 2.6 %collective-permute-done.11.refs_2_ = bf16[16,384]{1,0:T(8,128)(2,1)S(1)} collective-permute-done((bf16[16,384]{1,0:T(8,128)(2,1)S(1)}, bf16[16,384]{1,0:T(8,128)(2,1)S(1)}, u32[]{:S(2)}, u32[]{:S(2)}) %collective-permute-start.11) | collective-permute-done | bytes 12320 | tf_op jit(solution)/shard_map/ppermute | solution.py:486
  54.0 1.9 %project_last.1 = (bf16[256,1536]{1,0:T(8,128)(2,1)}, f32[1,256]{1,0:T(1,128)}) custom-call(bf16[256,384]{1,0:T(8,128)(2,1)S(1)} %collective-permute-done.9.refs_0_, bf16[1,384,1536]{2,1,0:T(8,128)(2,1)S(1)} %get-tuple-element.14.refs_1_, bf16[16,384]{1,0:T(8,128)(2,1)S(1)} %collective-permute-done.11.refs_2_, f32[256,1536]{1,0:T(8,128)S(1)} %get-tuple-element.15.refs_3_, ...), custom_call_target="tpu_custom_call" | custom-call | tf_op jit(solution)/shard_map/project_last/pallas_call | solution.py:456
  (32 shorter events, 1.7 us)
Async XLA Ops:
  0.6 12.1 %copy-start.4 = (s32[16]{0:T(128)S(1)}, s32[16]{0:T(128)}, u32[]{:S(2)}) copy-start(s32[16]{0:T(128)} %window.7) | copy-start | bytes 196
  7.1 7.3 %copy-start.2 = (bf16[272,384]{1,0:T(8,128)(2,1)S(1)}, bf16[272,384]{1,0:T(8,128)(2,1)}, u32[]{:S(2)}) copy-start(bf16[272,384]{1,0:T(8,128)(2,1)} %get-tuple-element.11.queries._) | copy-start | bytes 626692
  7.1 13.4 %collective-permute-start.3 = (bf16[512,384]{1,0:T(8,128)(2,1)}, bf16[512,384]{1,0:T(8,128)(2,1)S(1)}, u32[]{:S(2)}, u32[]{:S(2)}) collective-permute-start(bf16[512,384]{1,0:T(8,128)(2,1)} %get-tuple-element.12.refs_0_), channel_id=1, source_target_pairs={{0,4},{2,6},{4,0},{6,2},{8,12},{10,14},{12,8},{14,10},{16,20},{18,... | collective-permute-start | bytes 1179656 | tf_op jit(solution)/shard_map/ppermute | solution.py:483
  10.2 15.3 %collective-permute-start.2 = (bf16[512,384]{1,0:T(8,128)(2,1)}, bf16[512,384]{1,0:T(8,128)(2,1)S(1)}, u32[]{:S(2)}, u32[]{:S(2)}) collective-permute-start(bf16[512,384]{1,0:T(8,128)(2,1)} %get-tuple-element.12.refs_0_), channel_id=1, source_target_pairs={{0,8},{2,10},{4,12},{6,14},{8,0},{10,2},{12,4},{14,6},{16,24},{18,... | collective-permute-start | bytes 1179656 | tf_op jit(solution)/shard_map/ppermute | solution.py:483
  11.7 7.6 %collective-permute-start.1 = (bf16[272,384]{1,0:T(8,128)(2,1)}, bf16[272,384]{1,0:T(8,128)(2,1)S(1)}, u32[]{:S(2)}, u32[]{:S(2)}) collective-permute-start(bf16[272,384]{1,0:T(8,128)(2,1)} %get-tuple-element.11.queries._), channel_id=1, source_target_pairs={{0,2},{2,0},{4,6},{6,4},{8,10},{10,8},{12,14},{14,12},{16,18},{18,... | collective-permute-start | bytes 626696 | tf_op jit(solution)/shard_map/ppermute | solution.py:483
  12.8 0.9 %copy-start.1 = (bf16[272,384]{1,0:T(8,128)(2,1)S(1)}, bf16[272,384]{1,0:T(8,128)(2,1)}, u32[]{:S(2)}) copy-start(bf16[272,384]{1,0:T(8,128)(2,1)} %get-tuple-element.11.queries._) | copy-start | bytes 626692
  13.7 1.0 %copy-start.3 = (bf16[512,384]{1,0:T(8,128)(2,1)S(1)}, bf16[512,384]{1,0:T(8,128)(2,1)}, u32[]{:S(2)}) copy-start(bf16[512,384]{1,0:T(8,128)(2,1)} %get-tuple-element.12.refs_0_) | copy-start | bytes 1179652
  15.2 12.3 %collective-permute-start = (bf16[272,384]{1,0:T(8,128)(2,1)S(1)}, bf16[272,384]{1,0:T(8,128)(2,1)S(1)}, u32[]{:S(2)}, u32[]{:S(2)}) collective-permute-start(bf16[272,384]{1,0:T(8,128)(2,1)S(1)} %gate.7), channel_id=1, source_target_pairs={{0,16},{2,18},{4,20},{6,22},{8,24},{10,26},{12,28},{14,30},{16,0},... | collective-permute-start | bytes 626696 | tf_op jit(solution)/shard_map/ppermute | solution.py:483
  17.8 31.6 %collective-permute-start.10 = (bf16[1,384,1536]{2,1,0:T(8,128)(2,1)}, bf16[1,384,1536]{2,1,0:T(8,128)(2,1)}, u32[]{:S(2)}, u32[]{:S(2)}) collective-permute-start(bf16[1,384,1536]{2,1,0:T(8,128)(2,1)} %gate.13), channel_id=1, source_target_pairs={{0,1},{1,0},{2,3},{3,2},{4,5},{5,4},{6,7},{7,6},{8,9},{9,8},{10,11... | collective-permute-start | bytes 3538952 | tf_op jit(solution)/shard_map/ppermute | solution.py:486
  20.6 10.8 %collective-permute-start.6 = (bf16[288,384]{1,0:T(8,128)(2,1)S(1)}, bf16[288,384]{1,0:T(8,128)(2,1)S(1)}, u32[]{:S(2)}, u32[]{:S(2)}) collective-permute-start(bf16[288,384]{1,0:T(8,128)(2,1)S(1)} %slice.9), channel_id=1, source_target_pairs={{0,8},{2,10},{4,12},{6,14},{8,0},{10,2},{12,4},{14,6},{16,24},{18,... | collective-permute-start | bytes 663560 | tf_op jit(solution)/shard_map/ppermute | solution.py:483
  25.5 6.0 %collective-permute-start.5 = (bf16[288,384]{1,0:T(8,128)(2,1)S(1)}, bf16[288,384]{1,0:T(8,128)(2,1)S(1)}, u32[]{:S(2)}, u32[]{:S(2)}) collective-permute-start(bf16[288,384]{1,0:T(8,128)(2,1)S(1)} %slice.8), channel_id=1, source_target_pairs={{0,4},{2,6},{4,0},{6,2},{8,12},{10,14},{12,8},{14,10},{16,20},{18,... | collective-permute-start | bytes 663560 | tf_op jit(solution)/shard_map/ppermute | solution.py:483
  28.3 1.5 %collective-permute-start.4 = (bf16[272,384]{1,0:T(8,128)(2,1)S(1)}, bf16[272,384]{1,0:T(8,128)(2,1)S(1)}, u32[]{:S(2)}, u32[]{:S(2)}) collective-permute-start(bf16[272,384]{1,0:T(8,128)(2,1)S(1)} %gate.10.queries), channel_id=1, source_target_pairs={{0,2},{2,0},{4,6},{6,4},{8,10},{10,8},{12,14},{14,12},{16,18},{18,... | collective-permute-start | bytes 626696 | tf_op jit(solution)/shard_map/ppermute | solution.py:483
  32.2 1.8 %collective-permute-start.7 = (bf16[544,384]{1,0:T(8,128)(2,1)S(1)}, bf16[544,384]{1,0:T(8,128)(2,1)S(1)}, u32[]{:S(2)}, u32[]{:S(2)}) collective-permute-start(bf16[544,384]{1,0:T(8,128)(2,1)S(1)} %attend_pair.1._), channel_id=1, source_target_pairs={{0,2},{2,0},{4,6},{6,4},{8,10},{10,8},{12,14},{14,12},{16,18},{18,... | collective-permute-start | bytes 1253384 | tf_op jit(solution)/shard_map/ppermute | solution.py:483
  32.9 3.7 %copy-start = (bf16[384,3072]{1,0:T(8,128)(2,1)S(1)}, bf16[384,3072]{1,0:T(8,128)(2,1)}, u32[]{:S(2)}) copy-start(bf16[384,3072]{1,0:T(8,128)(2,1)} %w_out.5) | copy-start | bytes 7077892
  34.4 12.6 %collective-permute-start.8 = (bf16[272,384]{1,0:T(8,128)(2,1)S(1)}, bf16[272,384]{1,0:T(8,128)(2,1)S(1)}, u32[]{:S(2)}, u32[]{:S(2)}) collective-permute-start(bf16[272,384]{1,0:T(8,128)(2,1)S(1)} %join.1._), channel_id=1, source_target_pairs={{0,16},{2,18},{4,20},{6,22},{8,24},{10,26},{12,28},{14,30},{16,0},... | collective-permute-start | bytes 626696 | tf_op jit(solution)/shard_map/ppermute | solution.py:483
  47.3 6.7 %collective-permute-start.9 = (bf16[256,384]{1,0:T(8,128)(2,1)S(1)}, bf16[256,384]{1,0:T(8,128)(2,1)S(1)}, u32[]{:S(2)}, u32[]{:S(2)}) collective-permute-start(bf16[256,384]{1,0:T(8,128)(2,1)S(1)} %finish.1.own), channel_id=1, source_target_pairs={{0,1},{1,0},{2,3},{3,2},{4,5},{5,4},{6,7},{7,6},{8,9},{9,8},{10,11... | collective-permute-start | bytes 589832 | tf_op jit(solution)/shard_map/ppermute | solution.py:486
  49.4 4.6 %collective-permute-start.11 = (bf16[16,384]{1,0:T(8,128)(2,1)S(1)}, bf16[16,384]{1,0:T(8,128)(2,1)S(1)}, u32[]{:S(2)}, u32[]{:S(2)}) collective-permute-start(bf16[16,384]{1,0:T(8,128)(2,1)S(1)} %row_sums.1.refs_2_.sums), channel_id=1, source_target_pairs={{0,1},{1,0},{2,3},{3,2},{4,5},{5,4},{6,7},{7,6},{8,9},{9,8},{10,11... | collective-permute-start | bytes 36872 | tf_op jit(solution)/shard_map/ppermute | solution.py:486

commit v4 on v3

--- a/solution.py
+++ b/solution.py
@@ -43,9 +43,8 @@
     return jnp.concatenate(parts, axis=1)
 
 
-def project_kernel(steps, n_head, tokens, w_qkv, gains, near_mask, far_pattern, w_out, *refs):
-    kv, queries, payload = refs[:3]
-    token_buf, w_buf, gain_buf, near_buf, far_buf, total, out_buf, sems, small_sems, out_sems = refs[3:]
+def project_kernel(steps, tokens, w_qkv, gains, near_mask, far_pattern, kv, queries, *scratch):
+    token_buf, w_buf, gain_buf, near_buf, far_buf, total, sems, small_sems = scratch
     rows, width = tokens.shape
     count, _, cols = w_qkv.shape
     deep = width // steps
@@ -70,21 +69,6 @@
     ]
     for copy in small:
         copy.start()
-    out_cols = payload.shape[2]
-    place = lax.axis_index("head")
-    columns = []
-    for k in range(1, n_head):
-        first = pl.multiple_of(lax.rem(place + k, n_head) * out_cols, HD)
-        columns.append(
-            (
-                pltpu.make_async_copy(
-                    w_out.at[:, pl.ds(first, out_cols)], out_buf.at[k - 1], out_sems.at[0, k - 1]
-                ),
-                pltpu.make_async_copy(out_buf.at[k - 1], payload.at[k - 1], out_sems.at[1, k - 1]),
-            )
-        )
-    for load, _ in columns:
-        load.start()
     for s in range(steps):
         for copy in copies[s]:
             copy.wait()
@@ -95,9 +79,6 @@
         elif s < steps - 1:
             total[...] += part
     part = total[...] + part
-    for load, store in columns:
-        load.wait()
-        store.start()
     for copy in small:
         copy.wait()
     query, key, value = (part[:, j * cols : (j + 1) * cols] for j in range(count))
@@ -110,22 +91,19 @@
     queries[rows : rows + n_blocks, HD : HD + far_pattern.shape[1]] = (
         far_buf[...].astype(F32).astype(BF16)
     )
-    for _, store in columns:
-        store.wait()
-
-
-def project(tokens, w_qkv, gains, near_mask, far_pattern, w_out, n_head):
+
+
+def project(tokens, w_qkv, gains, near_mask, far_pattern):
     rows, width = tokens.shape
     count, _, cols = w_qkv.shape
     steps = 4
     return pl.pallas_call(
-        functools.partial(project_kernel, steps, n_head),
-        in_specs=[ANYWHERE] * 6,
-        out_specs=[IN_VMEM] * 2 + [ANYWHERE],
+        functools.partial(project_kernel, steps),
+        in_specs=[ANYWHERE] * 5,
+        out_specs=[IN_VMEM] * 2,
         out_shape=[
             jax.ShapeDtypeStruct((2 * rows, cols), BF16),
             jax.ShapeDtypeStruct((rows + PAD, cols), BF16),
-            jax.ShapeDtypeStruct((n_head - 1, w_out.shape[0], w_out.shape[1] // n_head), BF16),
         ],
         scratch_shapes=[
             VMEM((rows, width), BF16),
@@ -134,21 +112,48 @@
             VMEM(near_mask.shape, jnp.int32),
             VMEM(far_pattern.shape, jnp.int32),
             VMEM((rows, count * cols), F32),
-            VMEM((n_head - 1, w_out.shape[0], w_out.shape[1] // n_head), BF16),
             pltpu.SemaphoreType.DMA((1 + count, steps)),
             pltpu.SemaphoreType.DMA((3,)),
-            pltpu.SemaphoreType.DMA((2, n_head - 1)),
         ],
         compiler_params=params(56),
         cost_estimate=cost(5.0),
         name="project",
-    )(tokens, w_qkv, gains, near_mask, far_pattern, w_out)
+    )(tokens, w_qkv, gains, near_mask, far_pattern)
 
 
 def split_sum(values):
     high = values.astype(BF16).astype(F32)
     mid = (values - high).astype(BF16).astype(F32)
     return high, mid, values - high - mid
+
+
+def columns_kernel(n_head, w_out, _, payload, sems):
+    cols = payload.shape[2]
+    place = lax.axis_index("head")
+    copies = []
+    for k in range(1, n_head):
+        first = pl.multiple_of(lax.rem(place + k, n_head) * cols, HD)
+        copies.append(
+            pltpu.make_async_copy(w_out.at[:, pl.ds(first, cols)], payload.at[k - 1], sems.at[k - 1])
+        )
+    for copy in copies:
+        copy.start()
+    for copy in copies:
+        copy.wait()
+
+
+def columns_of(w_out, n_head, before):
+    rows, width = w_out.shape
+    return pl.pallas_call(
+        functools.partial(columns_kernel, n_head),
+        in_specs=[ANYWHERE, IN_VMEM],
+        out_specs=IN_VMEM,
+        out_shape=jax.ShapeDtypeStruct((n_head - 1, rows, width // n_head), BF16),
+        scratch_shapes=[pltpu.SemaphoreType.DMA((n_head - 1,))],
+        compiler_params=params(16),
+        cost_estimate=cost(1.0),
+        name="columns",
+    )(w_out, before)
 
 
 def sums_kernel(w_out, _, sums):
@@ -200,6 +205,69 @@
                 out[c, i * BLK : (i + 1) * BLK, j * BLK : (j + 1) * BLK] = jnp.where(
                     gaps[i - j] < here, 0.0, BARRED
                 )
+
+
+def table_kernel(sides, n_slabs, n_blocks, ids, window, _, *tables):
+    for side, table in zip(sides, tables):
+        lanes, cols = table.shape
+        lane = lax.broadcasted_iota(jnp.int32, (lanes, cols), 0)
+        col = lax.broadcasted_iota(jnp.int32, (lanes, cols), 1)
+        value = jnp.zeros((lanes, cols), F32)
+        query_slab = ids[side]
+        for c in range(n_slabs):
+            key_slab = ids[4 + c]
+            distance = jnp.abs(key_slab - query_slab)
+            before = jnp.where(key_slab < query_slab, 0, 1)
+            first = jnp.where(distance == 1, before * n_blocks, HD + key_slab * n_blocks)
+            reach = window[distance].astype(F32)
+            here = (lane - first == col - c * n_blocks) & (col // n_blocks == c)
+            value = jnp.where(here, reach, value)
+        table[...] = value.astype(BF16)
+
+
+def tables(sides, ids, window, lanes, n_blocks, before):
+    n_slabs = ids.shape[0] - 4
+    return pl.pallas_call(
+        functools.partial(table_kernel, sides, n_slabs, n_blocks),
+        in_specs=[IN_SMEM] * 2 + [IN_VMEM],
+        out_specs=[IN_VMEM] * len(sides),
+        out_shape=[jax.ShapeDtypeStruct((lanes, HD), BF16) for _ in sides],
+        compiler_params=params(16),
+        cost_estimate=cost(0.5),
+        name="tables",
+    )(ids, window, before)
+
+
+def late_bias_kernel(n_slabs, n_blocks, table, queries, _, out):
+    rows = n_blocks * BLK
+    limits = jnp.dot(queries[rows : rows + PAD, :], table[...], preferred_element_type=F32)
+    shifted = lax.broadcasted_iota(jnp.int32, (BLK, BLK), 0) - lax.broadcasted_iota(
+        jnp.int32, (BLK, BLK), 1
+    )
+    gaps = {
+        by: jnp.abs(shifted + by * BLK).astype(F32) for by in range(1 - n_blocks, n_blocks)
+    }
+    for c in range(n_slabs):
+        for i in range(n_blocks):
+            for j in range(n_blocks):
+                at = c * n_blocks + j
+                here = jnp.broadcast_to(limits[i : i + 1, at : at + 1], (BLK, BLK))
+                out[c, i * BLK : (i + 1) * BLK, j * BLK : (j + 1) * BLK] = jnp.where(
+                    gaps[i - j] < here, 0.0, BARRED
+                )
+
+
+def late_biases(table, queries, n_slabs, n_blocks, before):
+    rows = n_blocks * BLK
+    return pl.pallas_call(
+        functools.partial(late_bias_kernel, n_slabs, n_blocks),
+        in_specs=[IN_VMEM] * 3,
+        out_specs=IN_VMEM,
+        out_shape=jax.ShapeDtypeStruct((n_slabs, rows, rows), F32),
+        compiler_params=params(16),
+        cost_estimate=cost(0.3),
+        name="late_biases",
+    )(table, queries, before)
 
 
 def biases(side, ids, window, queries, n_blocks, before):
@@ -364,11 +432,27 @@
     pass
 
 
+def copy_kernel(array, _, out):
+    out[...] = array[...]
+
+
+def copied(array, before):
+    return pl.pallas_call(
+        copy_kernel,
+        in_specs=[IN_VMEM] * 2,
+        out_specs=IN_VMEM,
+        out_shape=jax.ShapeDtypeStruct(array.shape, array.dtype),
+        compiler_params=params(16),
+        cost_estimate=cost(0.1),
+        name="copied",
+    )(array, before)
+
+
 def gate(array, before):
     return pl.pallas_call(
         gate_kernel,
-        in_specs=[ANYWHERE, IN_VMEM],
-        out_specs=ANYWHERE,
+        in_specs=[IN_VMEM] * 2,
+        out_specs=IN_VMEM,
         out_shape=jax.ShapeDtypeStruct(array.shape, array.dtype),
         input_output_aliases={0: 0},
         compiler_params=params(16),
@@ -498,9 +582,7 @@
     slabs = [0] + spans + far
     n_near = 1 + len(spans)
 
-    kv, queries, payload = project(
-        tokens, w_qkv, norm_gains, near_mask, far_pattern, w_out, n_head
-    )
+    kv, queries = project(tokens, w_qkv, norm_gains, near_mask, far_pattern)
     near = {by: swapped(kv, by) for by in spans}
     sib_queries = swapped(queries, 1)
     ids = jnp.stack([frame ^ o for o in [0, 1, half, half ^ 1] + slabs])
@@ -511,16 +593,18 @@
     mine = [((kv,), 0)]
     own_bias = bias_of(0, queries, queries)
     own = attend(own_bias, queries, own_bias, mine, None, every, "attend_first")
-    other_queries = swapped(gate(queries, own), half)
-    payload = gate(payload, own)
+    other_queries = swapped(copied(queries, own), half)
+    payload = columns_of(w_out, n_head, own)
     received = from_heads([payload[k - 1 : k] for k in range(1, n_head)])
-    sib_bias = bias_of(1, sib_queries, own)
+    other_table, other_sib_table = tables(
+        (2, 3), ids, window, queries.shape[1], n_blocks, own
+    )
+    sib_bias = bias_of(1, sib_queries, other_sib_table)
     sib = attend(sib_bias, sib_queries, sib_bias, mine, None, every, "sibling_first")
 
-    low = spans[-1]
-    near[low] = gate(near[low], sib)
-    for by in spans[:-1]:
-        near[by] = gate(near[by], near[low])
+    before = sib
+    for by in spans:
+        near[by] = before = gate(near[by], before)
     margin = 2 * PAD
     keys = {by: near[by][: rows + margin] for by in spans}
     values = {by: near[by][rows - margin :] for by in spans}
@@ -531,14 +615,14 @@
     early = [((near[by],), i) for i, by in enumerate(spans, 1)]
     sib = attend(sib_bias, sib_queries, sib_bias, early, sib, every, "sibling_second")
     own = attend(own_bias, queries, sib, early, own, every, "attend_second")
-    other_bias = bias_of(2, other_queries, own)
+    other_bias = late_biases(other_table, other_queries, len(slabs), n_blocks, own)
     other_queries = gate(other_queries, other_bias)
     other_sib = swapped(other_queries, 1)
     early = [((near[by],), i) for i, by in enumerate(spans, 1)]
     other = attend(
         other_bias, other_queries, other_bias, mine + early, None, every, "other_first"
     )
-    other_sib_bias = bias_of(3, other_sib, other)
+    other_sib_bias = late_biases(other_sib_table, other_sib, len(slabs), n_blocks, other)
     both = attend(other_sib_bias, other_sib, other, mine + early, None, every, "other_sibling_first")
     late = []
     for i, o in enumerate(far, n_near):

time: 56.1 us -> 54.3 us (0.968)
  waiting for transfers between devices: 18.2 us -> 14.2 us
  starting transfers between devices: 14.2 us -> 16.9 us
  local copies, waits for them, and re-layouts: 2.28 us -> 1.46 us
    ppermute x9, waiting for transfers between devices: 15.5 us -> 11.7 us  [swapped(): return lax.ppermute(array, 'frame', [(i, i ^ by) for i in range(n_frame)])]
    ppermute x9, starting transfers between devices: 10.6 us -> 13.2 us  [swapped(): return lax.ppermute(array, 'frame', [(i, i ^ by) for i in range(n_frame)])]
    pallas_call x8 -> x11, Pallas kernels: 6.47 us -> 8.23 us  [the longest x1 5.7 us: project(): pl.pallas_call(functools.partial(project_kernel, steps), in_specs=[ANYWHE...]
    pallas_call x4 -> x2, Pallas kernels: 2.84 us -> 1.42 us  [biases(): pl.pallas_call(functools.partial(bias_kernel, side, n_slabs, n_blocks), i...]
    unnamed x11 -> x10, local copies, waits for them, and re-layouts: 2.15 us -> 1.33 us
  transfers between devices with their start and end apart: 12 -> 12, of which waited for: 7 -> 6; matrix products, arithmetic and copies ran while one was open for 2% -> 0% of each run, Pallas kernels for 22% -> 24%
where the time goes in v4:
time: 54.3 us; the launch traced here: 54.1 us
  Pallas kernels  20.7 us (38%)
  starting transfers between devices  16.9 us (31%)
  waiting for transfers between devices  14.2 us (26%)
  local copies, waits for them, and re-layouts  1.46 us (3%)
  between operations  0.85 us (2%)
    ppermute x9, starting transfers between devices, swapped(): return lax.ppermute(array, 'frame', [(i, i ^ by) for i in range(n_frame)])  13.2 us
    ppermute x9, waiting for transfers between devices, swapped(): return lax.ppermute(array, 'frame', [(i, i ^ by) for i in range(n_frame)])  11.7 us
    pallas_call x1, Pallas kernels, project(): pl.pallas_call(functools.partial(project_kernel, steps), in_specs=[ANYWHE...  5.7 us
    pallas_call x8, Pallas kernels, attend(): pl.pallas_call(functools.partial(attend_kernel, slabs, [len(c) > 1 for c,...  5.11 us
    ppermute x3, starting transfers between devices, from_head(): lax.ppermute(array, 'head', [(i, (i + k) % n_head) for i in range(n_head)])  3.65 us
    ppermute x3, waiting for transfers between devices, from_head(): lax.ppermute(array, 'head', [(i, (i + k) % n_head) for i in range(n_head)])  2.46 us
    pallas_call x1, Pallas kernels, project_early(): pl.pallas_call(functools.partial(early_kernel, n_head), in_specs=[IN_SMEM...  1.92 us
    pallas_call x1, Pallas kernels, project_last(): pl.pallas_call(functools.partial(last_kernel, n_head), in_specs=[IN_VMEM]...  1.87 us
  transfers between devices with their start and end apart: 12, of which 6 were waited for; matrix products, arithmetic and copies ran while one was open for 0% of the time, Pallas kernels for 24%

profile of v4, /device:TPU:0, one launch (start us, length us, event | category | flops | bytes accessed | tf_op | source)
XLA Modules:
  0.0 54.1 jit_solution(12179267897227319594)
XLA Ops:
  0.6 5.7 %project.1 = (bf16[512,384]{1,0:T(8,128)(2,1)}, bf16[272,384]{1,0:T(8,128)(2,1)}) custom-call(bf16[256,3072]{1,0:T(8,128)(2,1)} %tokens.1, bf16[3,3072,384]{2,1,0:T(8,128)(2,1)} %w_qkv.1, f32[2,384]{1,0:T(2,128)} %gains.1, s32[2,4]{1,0:T(2,128)} %near_mask.1, s32[2,32]{1,0:T(2,128)} %far_pattern.1), custom_call_target="tpu_custom_call" | custom-call | tf_op jit(solution)/shard_map/project/pallas_call | solution.py:100
  6.3 3.1 %collective-permute-start.2 = (bf16[512,384]{1,0:T(8,128)(2,1)}, bf16[512,384]{1,0:T(8,128)(2,1)S(1)}, u32[]{:S(2)}, u32[]{:S(2)}) collective-permute-start(bf16[512,384]{1,0:T(8,128)(2,1)} %get-tuple-element.13.refs_0_), channel_id=1, source_target_pairs={{0,8},{2,10},{4,12},{6,14},{8,0},{10,2},{12,4},{14,6},{16,24},{18,... | collective-permute-start | bytes 1179656 | tf_op jit(solution)/shard_map/ppermute | solution.py:567
  9.4 1.5 %collective-permute-start.3 = (bf16[512,384]{1,0:T(8,128)(2,1)}, bf16[512,384]{1,0:T(8,128)(2,1)S(1)}, u32[]{:S(2)}, u32[]{:S(2)}) collective-permute-start(bf16[512,384]{1,0:T(8,128)(2,1)} %get-tuple-element.13.refs_0_), channel_id=1, source_target_pairs={{0,4},{2,6},{4,0},{6,2},{8,12},{10,14},{12,8},{14,10},{16,20},{18,... | collective-permute-start | bytes 1179656 | tf_op jit(solution)/shard_map/ppermute | solution.py:567
  11.1 0.9 %copy-done.1 = bf16[272,384]{1,0:T(8,128)(2,1)S(1)} copy-done((bf16[272,384]{1,0:T(8,128)(2,1)S(1)}, bf16[272,384]{1,0:T(8,128)(2,1)}, u32[]{:S(2)}) %copy-start.1) | copy-done | bytes 208920
  12.0 0.7 %biases.2.bias._ = f32[4,256,256]{2,1,0:T(8,128)S(1)} custom-call(s32[8]{0:T(128)S(1)} %stack.32.ids, s32[16]{0:T(128)S(1)} %copy-done.4, bf16[272,384]{1,0:T(8,128)(2,1)S(1)} %copy-done.1, bf16[272,384]{1,0:T(8,128)(2,1)S(1)} %copy-done.1), custom_call_target="tpu_custom_call" | custom-call | tf_op jit(solution)/shard_map/biases/pallas_call | solution.py:276
  13.1 0.5 attend_first.1._.refs_2_
  13.6 2.7 %collective-permute-start = (bf16[272,384]{1,0:T(8,128)(2,1)S(1)}, bf16[272,384]{1,0:T(8,128)(2,1)S(1)}, u32[]{:S(2)}, u32[]{:S(2)}) collective-permute-start(bf16[272,384]{1,0:T(8,128)(2,1)S(1)} %copied.1), channel_id=1, source_target_pairs={{0,16},{2,18},{4,20},{6,22},{8,24},{10,26},{12,28},{14,30},{16,0},... | collective-permute-start | bytes 626696 | tf_op jit(solution)/shard_map/ppermute | solution.py:567
  16.3 1.1 %columns.1 = bf16[1,384,1536]{2,1,0:T(8,128)(2,1)} custom-call(bf16[384,3072]{1,0:T(8,128)(2,1)S(1)} %copy-done, f32[3,256,256]{2,1,0:T(8,128)S(1)} %attend_first.1._.refs_2_), custom_call_target="tpu_custom_call" | custom-call | tf_op jit(solution)/shard_map/columns/pallas_call | solution.py:147
  17.4 1.6 %collective-permute-start.10 = (bf16[1,384,1536]{2,1,0:T(8,128)(2,1)}, bf16[1,384,1536]{2,1,0:T(8,128)(2,1)}, u32[]{:S(2)}, u32[]{:S(2)}) collective-permute-start(bf16[1,384,1536]{2,1,0:T(8,128)(2,1)} %columns.1), channel_id=1, source_target_pairs={{0,1},{1,0},{2,3},{3,2},{4,5},{5,4},{6,7},{7,6},{8,9},{9,8},{10,11... | collective-permute-start | bytes 3538952 | tf_op jit(solution)/shard_map/ppermute | solution.py:570
  19.0 0.8 %tables.1 = (bf16[384,128]{1,0:T(8,128)(2,1)S(1)}, bf16[384,128]{1,0:T(8,128)(2,1)S(1)}) custom-call(s32[8]{0:T(128)S(1)} %stack.32.ids, s32[16]{0:T(128)S(1)} %copy-done.4, f32[3,256,256]{2,1,0:T(8,128)S(1)} %attend_first.1._.refs_2_), custom_call_target="tpu_custom_call" | custom-call | tf_op jit(solution)/shard_map/tables/pallas_call | solution.py:230
  19.7 0.7 %biases.3.bias._.second_bias = f32[4,256,256]{2,1,0:T(8,128)S(1)} custom-call(s32[8]{0:T(128)S(1)} %stack.32.ids, s32[16]{0:T(128)S(1)} %copy-done.4, bf16[272,384]{1,0:T(8,128)(2,1)S(1)} %collective-permute-done.1.queries.second, bf16[384,128]{1,0:T(8,128)(2,1)S(1)} %get-tuple-element.15._.table), custom_call_target="tpu_custom_call" | custom-call | tf_op jit(solution)/shard_map/biases/pallas_call | solution.py:276
  20.5 0.5 sibling_first.1._.refs_2_
  20.9 1.0 %collective-permute-done.2.array = bf16[512,384]{1,0:T(8,128)(2,1)S(1)} collective-permute-done((bf16[512,384]{1,0:T(8,128)(2,1)}, bf16[512,384]{1,0:T(8,128)(2,1)S(1)}, u32[]{:S(2)}, u32[]{:S(2)}) %collective-permute-start.2) | collective-permute-done | bytes 393248 | tf_op jit(solution)/shard_map/ppermute | solution.py:567
  22.1 3.0 %collective-permute-start.5 = (bf16[288,384]{1,0:T(8,128)(2,1)S(1)}, bf16[288,384]{1,0:T(8,128)(2,1)S(1)}, u32[]{:S(2)}, u32[]{:S(2)}) collective-permute-start(bf16[288,384]{1,0:T(8,128)(2,1)S(1)} %slice.8), channel_id=1, source_target_pairs={{0,4},{2,6},{4,0},{6,2},{8,12},{10,14},{12,8},{14,10},{16,20},{18,... | collective-permute-start | bytes 663560 | tf_op jit(solution)/shard_map/ppermute | solution.py:567
  25.0 0.7 %sibling_second.1._.refs_3_ = f32[3,256,256]{2,1,0:T(8,128)S(1)} custom-call(f32[4,256,256]{2,1,0:T(8,128)S(1)} %biases.3.bias._.second_bias, bf16[272,384]{1,0:T(8,128)(2,1)S(1)} %collective-permute-done.1.queries.second, f32[4,256,256]{2,1,0:T(8,128)S(1)} %biases.3.bias._.second_bias, bf16[512,384]{1,0:T(8,128)(2,1)S(1)} %gate.5._.refs_0_.refs_1_, ...), custom_call_target="tpu_custom_call" | custom-call | tf_op jit(solution)/shard_map/sibling_second/pallas_call | solution.py:371
  25.7 0.7 %attend_second.1._.refs_2_ = f32[3,256,256]{2,1,0:T(8,128)S(1)} custom-call(f32[4,256,256]{2,1,0:T(8,128)S(1)} %biases.2.bias._, bf16[272,384]{1,0:T(8,128)(2,1)S(1)} %copy-done.2, f32[3,256,256]{2,1,0:T(8,128)S(1)} %sibling_second.1._.refs_3_, bf16[512,384]{1,0:T(8,128)(2,1)S(1)} %gate.5._.refs_0_.refs_1_, bf16[512,384]{1,0:T(8,128)(2,1)S(1)} %gate.6.refs_1_.refs_2_, ...), custom_call_target="tpu_custom_call" | custom-call | tf_op jit(solution)/shard_map/attend_second/pallas_call | solution.py:371
  27.2 0.9 %other_first.1._.refs_2_ = f32[3,256,256]{2,1,0:T(8,128)S(1)} custom-call(f32[4,256,256]{2,1,0:T(8,128)S(1)} %late_biases.2._.bias, bf16[272,384]{1,0:T(8,128)(2,1)S(1)} %gate.7.queries, f32[4,256,256]{2,1,0:T(8,128)S(1)} %late_biases.2._.bias, bf16[512,384]{1,0:T(8,128)(2,1)S(1)} %copy-done.3, bf16[512,384]{1,0:T(8,128)(2,1)S(1)} %gate.5._.refs_0_.refs_1_, ...), custom_call_target="tpu_custom_call" | custom-call | tf_op jit(solution)/shard_map/other_first/pallas_call | solution.py:371
  28.1 0.5 collective-permute-done.4.queries.first
  28.9 0.9 %other_sibling_first.1._.refs_2_ = f32[3,256,256]{2,1,0:T(8,128)S(1)} custom-call(f32[4,256,256]{2,1,0:T(8,128)S(1)} %late_biases.3.bias.first_bias, bf16[272,384]{1,0:T(8,128)(2,1)S(1)} %collective-permute-done.4.queries.first, f32[3,256,256]{2,1,0:T(8,128)S(1)} %other_first.1._.refs_2_, bf16[512,384]{1,0:T(8,128)(2,1)S(1)} %copy-done.3, ...), custom_call_target="tpu_custom_call" | custom-call | tf_op jit(solution)/shard_map/other_sibling_first/pallas_call | solution.py:371
  29.9 0.7 %attend_pair.1._ = bf16[544,384]{1,0:T(8,128)(2,1)S(1)} custom-call(f32[4,256,256]{2,1,0:T(8,128)S(1)} %late_biases.3.bias.first_bias, bf16[272,384]{1,0:T(8,128)(2,1)S(1)} %collective-permute-done.4.queries.first, f32[4,256,256]{2,1,0:T(8,128)S(1)} %biases.3.bias._.second_bias, bf16[272,384]{1,0:T(8,128)(2,1)S(1)} %collective-permute-done.1.queries.second, ...), custom_call_target="tpu_custom_call" | custom-call | tf_op jit(solution)/shard_map/attend_pair/pallas_call | solution.py:350
  30.8 0.5 other_last.1._.kept
  31.3 0.5 attend_last.1.refs_1_.kept
  31.8 0.6 %collective-permute-done.7.refs_0_ = bf16[544,384]{1,0:T(8,128)(2,1)S(1)} collective-permute-done((bf16[544,384]{1,0:T(8,128)(2,1)S(1)}, bf16[544,384]{1,0:T(8,128)(2,1)S(1)}, u32[]{:S(2)}, u32[]{:S(2)}) %collective-permute-start.7) | collective-permute-done | bytes 417824 | tf_op jit(solution)/shard_map/ppermute | solution.py:567
  32.4 0.4 join.1._
  32.8 2.7 %collective-permute-start.8 = (bf16[272,384]{1,0:T(8,128)(2,1)S(1)}, bf16[272,384]{1,0:T(8,128)(2,1)S(1)}, u32[]{:S(2)}, u32[]{:S(2)}) collective-permute-start(bf16[272,384]{1,0:T(8,128)(2,1)S(1)} %join.1._), channel_id=1, source_target_pairs={{0,16},{2,18},{4,20},{6,22},{8,24},{10,26},{12,28},{14,30},{16,0},... | collective-permute-start | bytes 626696 | tf_op jit(solution)/shard_map/ppermute | solution.py:567
  35.5 0.7 %row_sums.1.refs_2_.sums = bf16[16,384]{1,0:T(8,128)(2,1)S(1)} custom-call(bf16[384,3072]{1,0:T(8,128)(2,1)S(1)} %copy-done, bf16[272,384]{1,0:T(8,128)(2,1)S(1)} %join.1._), custom_call_target="tpu_custom_call" | custom-call | tf_op jit(solution)/shard_map/row_sums/pallas_call | solution.py:171
  36.2 9.2 %collective-permute-done.8.refs_1_ = bf16[272,384]{1,0:T(8,128)(2,1)S(1)} collective-permute-done((bf16[272,384]{1,0:T(8,128)(2,1)S(1)}, bf16[272,384]{1,0:T(8,128)(2,1)S(1)}, u32[]{:S(2)}, u32[]{:S(2)}) %collective-permute-start.8) | collective-permute-done | bytes 208928 | tf_op jit(solution)/shard_map/ppermute | solution.py:567
  45.7 1.6 %collective-permute-start.9 = (bf16[256,384]{1,0:T(8,128)(2,1)S(1)}, bf16[256,384]{1,0:T(8,128)(2,1)S(1)}, u32[]{:S(2)}, u32[]{:S(2)}) collective-permute-start(bf16[256,384]{1,0:T(8,128)(2,1)S(1)} %finish.1.own), channel_id=1, source_target_pairs={{0,1},{1,0},{2,3},{3,2},{4,5},{5,4},{6,7},{7,6},{8,9},{9,8},{10,11... | collective-permute-start | bytes 589832 | tf_op jit(solution)/shard_map/ppermute | solution.py:570
  47.3 0.5 collective-permute-start.11
  47.8 1.9 %project_early.1 = (f32[256,1536]{1,0:T(8,128)S(1)}, f32[8,256]{1,0:T(8,128)S(1)}, f32[1,8,256]{2,1,0:T(8,128)S(1)}, bf16[1,384,1536]{2,1,0:T(8,128)(2,1)S(1)}) custom-call(s32[1]{0:T(128)} %bitcast.7.place, bf16[256,384]{1,0:T(8,128)(2,1)S(1)} %finish.1.own, bf16[384,3072]{1,0:T(8,128)(2,1)S(1)} %copy-done, bf16[16,384]{1,0:T(8,128)(2,1)S(1)} %row_sums.1.refs_2_.sums, ...), custom_call_target="tpu_custom_call" | custom-call | tf_op jit(solution)/shard_map/project_early/pallas_call | solution.py:488
  49.8 2.5 %collective-permute-done.11.refs_2_ = bf16[16,384]{1,0:T(8,128)(2,1)S(1)} collective-permute-done((bf16[16,384]{1,0:T(8,128)(2,1)S(1)}, bf16[16,384]{1,0:T(8,128)(2,1)S(1)}, u32[]{:S(2)}, u32[]{:S(2)}) %collective-permute-start.11) | collective-permute-done | bytes 12320 | tf_op jit(solution)/shard_map/ppermute | solution.py:570
  52.2 1.9 %project_last.1 = (bf16[256,1536]{1,0:T(8,128)(2,1)}, f32[1,256]{1,0:T(1,128)}) custom-call(bf16[256,384]{1,0:T(8,128)(2,1)S(1)} %collective-permute-done.9.refs_0_, bf16[1,384,1536]{2,1,0:T(8,128)(2,1)S(1)} %get-tuple-element.16.refs_1_, bf16[16,384]{1,0:T(8,128)(2,1)S(1)} %collective-permute-done.11.refs_2_, f32[256,1536]{1,0:T(8,128)S(1)} %get-tuple-element.17.refs_3_, ...), custom_call_target="tpu_custom_call" | custom-call | tf_op jit(solution)/shard_map/project_last/pallas_call | solution.py:540
  (32 shorter events, 2.2 us)
Async XLA Ops:
  0.6 10.4 %copy-start.4 = (s32[16]{0:T(128)S(1)}, s32[16]{0:T(128)}, u32[]{:S(2)}) copy-start(s32[16]{0:T(128)} %window.5) | copy-start | bytes 196
  6.3 15.6 %collective-permute-start.2 = (bf16[512,384]{1,0:T(8,128)(2,1)}, bf16[512,384]{1,0:T(8,128)(2,1)S(1)}, u32[]{:S(2)}, u32[]{:S(2)}) collective-permute-start(bf16[512,384]{1,0:T(8,128)(2,1)} %get-tuple-element.13.refs_0_), channel_id=1, source_target_pairs={{0,8},{2,10},{4,12},{6,14},{8,0},{10,2},{12,4},{14,6},{16,24},{18,... | collective-permute-start | bytes 1179656 | tf_op jit(solution)/shard_map/ppermute | solution.py:567
  9.4 12.5 %collective-permute-start.3 = (bf16[512,384]{1,0:T(8,128)(2,1)}, bf16[512,384]{1,0:T(8,128)(2,1)S(1)}, u32[]{:S(2)}, u32[]{:S(2)}) collective-permute-start(bf16[512,384]{1,0:T(8,128)(2,1)} %get-tuple-element.13.refs_0_), channel_id=1, source_target_pairs={{0,4},{2,6},{4,0},{6,2},{8,12},{10,14},{12,8},{14,10},{16,20},{18,... | collective-permute-start | bytes 1179656 | tf_op jit(solution)/shard_map/ppermute | solution.py:567
  11.0 8.8 %collective-permute-start.1 = (bf16[272,384]{1,0:T(8,128)(2,1)}, bf16[272,384]{1,0:T(8,128)(2,1)S(1)}, u32[]{:S(2)}, u32[]{:S(2)}) collective-permute-start(bf16[272,384]{1,0:T(8,128)(2,1)} %get-tuple-element.12.queries._.array), channel_id=1, source_target_pairs={{0,2},{2,0},{4,6},{6,4},{8,10},{10,8},{12,14},{14,12},{16,18},{18,... | collective-permute-start | bytes 626696 | tf_op jit(solution)/shard_map/ppermute | solution.py:567
  11.0 0.9 %copy-start.1 = (bf16[272,384]{1,0:T(8,128)(2,1)S(1)}, bf16[272,384]{1,0:T(8,128)(2,1)}, u32[]{:S(2)}) copy-start(bf16[272,384]{1,0:T(8,128)(2,1)} %get-tuple-element.12.queries._.array) | copy-start | bytes 626692
  12.0 0.9 %copy-start.2 = (bf16[272,384]{1,0:T(8,128)(2,1)S(1)}, bf16[272,384]{1,0:T(8,128)(2,1)}, u32[]{:S(2)}) copy-start(bf16[272,384]{1,0:T(8,128)(2,1)} %get-tuple-element.12.queries._.array) | copy-start | bytes 626692
  12.0 1.1 %copy-start.3 = (bf16[512,384]{1,0:T(8,128)(2,1)S(1)}, bf16[512,384]{1,0:T(8,128)(2,1)}, u32[]{:S(2)}) copy-start(bf16[512,384]{1,0:T(8,128)(2,1)} %get-tuple-element.13.refs_0_) | copy-start | bytes 1179652
  13.1 3.2 %copy-start = (bf16[384,3072]{1,0:T(8,128)(2,1)S(1)}, bf16[384,3072]{1,0:T(8,128)(2,1)}, u32[]{:S(2)}) copy-start(bf16[384,3072]{1,0:T(8,128)(2,1)} %w_out.5) | copy-start | bytes 7077892
  13.6 13.2 %collective-permute-start = (bf16[272,384]{1,0:T(8,128)(2,1)S(1)}, bf16[272,384]{1,0:T(8,128)(2,1)S(1)}, u32[]{:S(2)}, u32[]{:S(2)}) collective-permute-start(bf16[272,384]{1,0:T(8,128)(2,1)S(1)} %copied.1), channel_id=1, source_target_pairs={{0,16},{2,18},{4,20},{6,22},{8,24},{10,26},{12,28},{14,30},{16,0},... | collective-permute-start | bytes 626696 | tf_op jit(solution)/shard_map/ppermute | solution.py:567
  17.4 30.4 %collective-permute-start.10 = (bf16[1,384,1536]{2,1,0:T(8,128)(2,1)}, bf16[1,384,1536]{2,1,0:T(8,128)(2,1)}, u32[]{:S(2)}, u32[]{:S(2)}) collective-permute-start(bf16[1,384,1536]{2,1,0:T(8,128)(2,1)} %columns.1), channel_id=1, source_target_pairs={{0,1},{1,0},{2,3},{3,2},{4,5},{5,4},{6,7},{7,6},{8,9},{9,8},{10,11... | collective-permute-start | bytes 3538952 | tf_op jit(solution)/shard_map/ppermute | solution.py:570
  21.9 7.9 %collective-permute-start.6 = (bf16[288,384]{1,0:T(8,128)(2,1)S(1)}, bf16[288,384]{1,0:T(8,128)(2,1)S(1)}, u32[]{:S(2)}, u32[]{:S(2)}) collective-permute-start(bf16[288,384]{1,0:T(8,128)(2,1)S(1)} %slice.9), channel_id=1, source_target_pairs={{0,8},{2,10},{4,12},{6,14},{8,0},{10,2},{12,4},{14,6},{16,24},{18,... | collective-permute-start | bytes 663560 | tf_op jit(solution)/shard_map/ppermute | solution.py:567
  22.1 7.8 %collective-permute-start.5 = (bf16[288,384]{1,0:T(8,128)(2,1)S(1)}, bf16[288,384]{1,0:T(8,128)(2,1)S(1)}, u32[]{:S(2)}, u32[]{:S(2)}) collective-permute-start(bf16[288,384]{1,0:T(8,128)(2,1)S(1)} %slice.8), channel_id=1, source_target_pairs={{0,4},{2,6},{4,0},{6,2},{8,12},{10,14},{12,8},{14,10},{16,20},{18,... | collective-permute-start | bytes 663560 | tf_op jit(solution)/shard_map/ppermute | solution.py:567
  27.1 1.5 %collective-permute-start.4 = (bf16[272,384]{1,0:T(8,128)(2,1)S(1)}, bf16[272,384]{1,0:T(8,128)(2,1)S(1)}, u32[]{:S(2)}, u32[]{:S(2)}) collective-permute-start(bf16[272,384]{1,0:T(8,128)(2,1)S(1)} %gate.7.queries), channel_id=1, source_target_pairs={{0,2},{2,0},{4,6},{6,4},{8,10},{10,8},{12,14},{14,12},{16,18},{18,... | collective-permute-start | bytes 626696 | tf_op jit(solution)/shard_map/ppermute | solution.py:567
  30.6 1.8 %collective-permute-start.7 = (bf16[544,384]{1,0:T(8,128)(2,1)S(1)}, bf16[544,384]{1,0:T(8,128)(2,1)S(1)}, u32[]{:S(2)}, u32[]{:S(2)}) collective-permute-start(bf16[544,384]{1,0:T(8,128)(2,1)S(1)} %attend_pair.1._), channel_id=1, source_target_pairs={{0,2},{2,0},{4,6},{6,4},{8,10},{10,8},{12,14},{14,12},{16,18},{18,... | collective-permute-start | bytes 1253384 | tf_op jit(solution)/shard_map/ppermute | solution.py:567
  32.8 12.6 %collective-permute-start.8 = (bf16[272,384]{1,0:T(8,128)(2,1)S(1)}, bf16[272,384]{1,0:T(8,128)(2,1)S(1)}, u32[]{:S(2)}, u32[]{:S(2)}) collective-permute-start(bf16[272,384]{1,0:T(8,128)(2,1)S(1)} %join.1._), channel_id=1, source_target_pairs={{0,16},{2,18},{4,20},{6,22},{8,24},{10,26},{12,28},{14,30},{16,0},... | collective-permute-start | bytes 626696 | tf_op jit(solution)/shard_map/ppermute | solution.py:567
  45.7 6.5 %collective-permute-start.9 = (bf16[256,384]{1,0:T(8,128)(2,1)S(1)}, bf16[256,384]{1,0:T(8,128)(2,1)S(1)}, u32[]{:S(2)}, u32[]{:S(2)}) collective-permute-start(bf16[256,384]{1,0:T(8,128)(2,1)S(1)} %finish.1.own), channel_id=1, source_target_pairs={{0,1},{1,0},{2,3},{3,2},{4,5},{5,4},{6,7},{7,6},{8,9},{9,8},{10,11... | collective-permute-start | bytes 589832 | tf_op jit(solution)/shard_map/ppermute | solution.py:570
  47.3 4.9 %collective-permute-start.11 = (bf16[16,384]{1,0:T(8,128)(2,1)S(1)}, bf16[16,384]{1,0:T(8,128)(2,1)S(1)}, u32[]{:S(2)}, u32[]{:S(2)}) collective-permute-start(bf16[16,384]{1,0:T(8,128)(2,1)S(1)} %row_sums.1.refs_2_.sums), channel_id=1, source_target_pairs={{0,1},{1,0},{2,3},{3,2},{4,5},{5,4},{6,7},{7,6},{8,9},{9,8},{10,11... | collective-permute-start | bytes 36872 | tf_op jit(solution)/shard_map/ppermute | solution.py:570

commit v5 on v4

--- a/solution.py
+++ b/solution.py
@@ -257,19 +257,6 @@
                 )
 
 
-def late_biases(table, queries, n_slabs, n_blocks, before):
-    rows = n_blocks * BLK
-    return pl.pallas_call(
-        functools.partial(late_bias_kernel, n_slabs, n_blocks),
-        in_specs=[IN_VMEM] * 3,
-        out_specs=IN_VMEM,
-        out_shape=jax.ShapeDtypeStruct((n_slabs, rows, rows), F32),
-        compiler_params=params(16),
-        cost_estimate=cost(0.3),
-        name="late_biases",
-    )(table, queries, before)
-
-
 def biases(side, ids, window, queries, n_blocks, before):
     n_slabs = ids.shape[0] - 4
     rows = n_blocks * BLK
@@ -326,6 +313,34 @@
     return chunks
 
 
+def other_kernel(slabs, lone, heads, n_blocks, table, queries, _, *refs):
+    refs = list(refs)
+    rows = n_blocks * BLK
+    chunks = taken_chunks(lone, rows, refs)
+    out, bias = refs
+    late_bias_kernel(bias.shape[0], n_blocks, table, queries, None, bias)
+    attend_body(slabs, False, heads, bias, queries, chunks, None, out)
+
+
+def attend_other(table, queries, before, parts, n_slabs, n_blocks, heads, name):
+    rows = n_blocks * BLK
+    operands = [table, queries, before] + [array for chunk, _ in parts for array in chunk]
+    return pl.pallas_call(
+        functools.partial(
+            other_kernel, [s for _, s in parts], [len(c) > 1 for c, _ in parts], heads, n_blocks
+        ),
+        in_specs=[IN_VMEM] * len(operands),
+        out_specs=[IN_VMEM] * 2,
+        out_shape=[
+            jax.ShapeDtypeStruct((heads[1] - heads[0], rows, 2 * HD), F32),
+            jax.ShapeDtypeStruct((n_slabs, rows, rows), F32),
+        ],
+        compiler_params=params(24),
+        cost_estimate=cost(1.0),
+        name=name,
+    )(*operands)
+
+
 def attend_kernel(slabs, lone, has_totals, heads, bias, queries, _, *refs):
     refs = list(refs)
     chunks = taken_chunks(lone, bias.shape[1], refs)
@@ -432,6 +447,24 @@
     pass
 
 
+def gate_all_kernel(*refs):
+    pass
+
+
+def gate_all(arrays, before):
+    n = len(arrays)
+    return pl.pallas_call(
+        gate_all_kernel,
+        in_specs=[IN_VMEM] * (n + 1),
+        out_specs=[IN_VMEM] * n,
+        out_shape=[jax.ShapeDtypeStruct(array.shape, array.dtype) for array in arrays],
+        input_output_aliases={i: i for i in range(n)},
+        compiler_params=params(16),
+        cost_estimate=cost(0.1),
+        name="gate_all",
+    )(*arrays, before)
+
+
 def copy_kernel(array, _, out):
     out[...] = array[...]
 
@@ -503,9 +536,9 @@
 
 def last_kernel(n_head, *refs):
     late, refs = refs[: n_head - 1], refs[n_head - 1 :]
-    received, sums, partial, parts, owners, layer_out, checksum, staged, sems = refs
+    received, sums, partial, parts, owners, layer_out, checksum, staged, summed, sems = refs
     rows, cols = partial.shape
-    tiles = sems.shape[0]
+    tiles = sems.shape[0] - 1
     tile = cols // tiles
     stores = []
     for t in range(tiles):
@@ -517,17 +550,22 @@
             )
         staged[:, here] = total.astype(BF16)
         there = pl.ds(t * tile, tile)
-        store = pltpu.make_async_copy(staged.at[:, there], layer_out.at[:, there], sems.at[t])
-        store.start()
-        stores.append(store)
-    every = parts[...]
-    for k in range(1, n_head):
-        dot = row_dot(sums[(k - 1) * PAD : k * PAD, :], late[k - 1][...])
-        every = every + owners[k - 1] * dot
-    sum_all = every[0:1, :]
-    for k in range(1, n_head):
-        sum_all = sum_all + every[k : k + 1, :]
-    checksum[...] = sum_all * D ** (-0.5)
+        stores.append(
+            pltpu.make_async_copy(staged.at[:, there], layer_out.at[:, there], sems.at[t])
+        )
+        stores[-1].start()
+        if t > 0:
+            continue
+        every = parts[...]
+        for k in range(1, n_head):
+            dot = row_dot(sums[(k - 1) * PAD : k * PAD, :], late[k - 1][...])
+            every = every + owners[k - 1] * dot
+        sum_all = every[0:1, :]
+        for k in range(1, n_head):
+            sum_all = sum_all + every[k : k + 1, :]
+        summed[...] = sum_all * D ** (-0.5)
+        stores.append(pltpu.make_async_copy(summed, checksum, sems.at[tiles]))
+        stores[-1].start()
     for store in stores:
         store.wait()
 
@@ -540,12 +578,16 @@
     layer_out, checksum = pl.pallas_call(
         functools.partial(last_kernel, n_head),
         in_specs=[IN_VMEM] * len(operands),
-        out_specs=[ANYWHERE, IN_VMEM],
+        out_specs=[ANYWHERE] * 2,
         out_shape=[
             jax.ShapeDtypeStruct((rows, cols), BF16),
             jax.ShapeDtypeStruct((1, rows), F32),
         ],
-        scratch_shapes=[VMEM((rows, cols), BF16), pltpu.SemaphoreType.DMA((tiles,))],
+        scratch_shapes=[
+            VMEM((rows, cols), BF16),
+            VMEM((1, rows), F32),
+            pltpu.SemaphoreType.DMA((tiles + 1,)),
+        ],
         compiler_params=params(24),
         name="project_last",
     )(*operands)
@@ -602,12 +644,9 @@
     sib_bias = bias_of(1, sib_queries, other_sib_table)
     sib = attend(sib_bias, sib_queries, sib_bias, mine, None, every, "sibling_first")
 
-    before = sib
-    for by in spans:
-        near[by] = before = gate(near[by], before)
-    margin = 2 * PAD
-    keys = {by: near[by][: rows + margin] for by in spans}
-    values = {by: near[by][rows - margin :] for by in spans}
+    near = dict(zip(spans, gate_all([near[by] for by in spans], sib)))
+    keys = {by: near[by][: rows + 2 * PAD] for by in spans}
+    values = {by: near[by][rows - 3 * PAD :] for by in spans}
     for o in far:
         bits = [by for by in spans if o & by]
         values[o] = swapped(values[o ^ bits[0]], bits[0])
@@ -615,15 +654,14 @@
     early = [((near[by],), i) for i, by in enumerate(spans, 1)]
     sib = attend(sib_bias, sib_queries, sib_bias, early, sib, every, "sibling_second")
     own = attend(own_bias, queries, sib, early, own, every, "attend_second")
-    other_bias = late_biases(other_table, other_queries, len(slabs), n_blocks, own)
-    other_queries = gate(other_queries, other_bias)
+    other_queries = gate(other_queries, own)
     other_sib = swapped(other_queries, 1)
-    early = [((near[by],), i) for i, by in enumerate(spans, 1)]
-    other = attend(
-        other_bias, other_queries, other_bias, mine + early, None, every, "other_first"
-    )
-    other_sib_bias = late_biases(other_sib_table, other_sib, len(slabs), n_blocks, other)
-    both = attend(other_sib_bias, other_sib, other, mine + early, None, every, "other_sibling_first")
+    other, other_bias = attend_other(
+        other_table, other_queries, own, mine + early, len(slabs), n_blocks, every, "other_first"
+    )
+    both, other_sib_bias = attend_other(
+        other_sib_table, other_sib, other, mine + early, len(slabs), n_blocks, every, "other_sibling_first"
+    )
     late = []
     for i, o in enumerate(far, n_near):
         late.append(((gate(keys[o], both), gate(values[o], both)), i))

time: 54.3 us -> 53.7 us (0.989)
  Pallas kernels: 20.7 us -> 19.9 us
    pallas_call x8 -> x6, Pallas kernels: 5.11 us -> 3.31 us  [attend(): pl.pallas_call(functools.partial(attend_kernel, slabs, [len(c) > 1 for c,...]
    pallas_call x2 -> x3, Pallas kernels: 0.61 us -> 2.1 us  [the longest x2 2.1 us: attend_other(): pl.pallas_call(functools.partial(other_kernel, [s for _, s in parts], [le...]
  transfers between devices with their start and end apart: 12 -> 12, of which waited for: 6 -> 8; matrix products, arithmetic and copies ran while one was open for 0% -> 0% of each run, Pallas kernels for 24% -> 24%
where the time goes in v5:
time: 53.7 us; the launch traced here: 53.5 us
  Pallas kernels  19.9 us (37%)
  starting transfers between devices  16.7 us (31%)
  waiting for transfers between devices  14.7 us (27%)
  local copies, waits for them, and re-layouts  1.47 us (3%)
  between operations  0.8 us (1%)
    ppermute x9, starting transfers between devices, swapped(): return lax.ppermute(array, 'frame', [(i, i ^ by) for i in range(n_frame)])  13.1 us
    ppermute x9, waiting for transfers between devices, swapped(): return lax.ppermute(array, 'frame', [(i, i ^ by) for i in range(n_frame)])  12.2 us
    pallas_call x1, Pallas kernels, project(): pl.pallas_call(functools.partial(project_kernel, steps), in_specs=[ANYWHE...  5.68 us
    ppermute x3, starting transfers between devices, from_head(): lax.ppermute(array, 'head', [(i, (i + k) % n_head) for i in range(n_head)])  3.65 us
    pallas_call x6, Pallas kernels, attend(): pl.pallas_call(functools.partial(attend_kernel, slabs, [len(c) > 1 for c,...  3.31 us
    ppermute x3, waiting for transfers between devices, from_head(): lax.ppermute(array, 'head', [(i, (i + k) % n_head) for i in range(n_head)])  2.5 us
    pallas_call x2, Pallas kernels, attend_other(): pl.pallas_call(functools.partial(other_kernel, [s for _, s in parts], [le...  2.1 us
    pallas_call x1, Pallas kernels, project_early(): pl.pallas_call(functools.partial(early_kernel, n_head), in_specs=[IN_SMEM...  1.92 us
  transfers between devices with their start and end apart: 12, of which 8 were waited for; matrix products, arithmetic and copies ran while one was open for 0% of the time, Pallas kernels for 24%

profile of v5, /device:TPU:0, one launch (start us, length us, event | category | flops | bytes accessed | tf_op | source)
XLA Modules:
  0.0 53.5 jit_solution(9460769969934931788)
XLA Ops:
  0.6 5.7 %project.1 = (bf16[512,384]{1,0:T(8,128)(2,1)}, bf16[272,384]{1,0:T(8,128)(2,1)}) custom-call(bf16[256,3072]{1,0:T(8,128)(2,1)} %tokens.1, bf16[3,3072,384]{2,1,0:T(8,128)(2,1)} %w_qkv.1, f32[2,384]{1,0:T(2,128)} %gains.1, s32[2,4]{1,0:T(2,128)} %near_mask.1, s32[2,32]{1,0:T(2,128)} %far_pattern.1), custom_call_target="tpu_custom_call" | custom-call | tf_op jit(solution)/shard_map/project/pallas_call | solution.py:100
  6.3 3.1 %collective-permute-start.2 = (bf16[512,384]{1,0:T(8,128)(2,1)}, bf16[512,384]{1,0:T(8,128)(2,1)S(1)}, u32[]{:S(2)}, u32[]{:S(2)}) collective-permute-start(bf16[512,384]{1,0:T(8,128)(2,1)} %get-tuple-element.19.refs_0_), channel_id=1, source_target_pairs={{0,8},{2,10},{4,12},{6,14},{8,0},{10,2},{12,4},{14,6},{16,24},{18,... | collective-permute-start | bytes 1179656 | tf_op jit(solution)/shard_map/ppermute | solution.py:609
  9.4 1.5 %collective-permute-start.3 = (bf16[512,384]{1,0:T(8,128)(2,1)}, bf16[512,384]{1,0:T(8,128)(2,1)S(1)}, u32[]{:S(2)}, u32[]{:S(2)}) collective-permute-start(bf16[512,384]{1,0:T(8,128)(2,1)} %get-tuple-element.19.refs_0_), channel_id=1, source_target_pairs={{0,4},{2,6},{4,0},{6,2},{8,12},{10,14},{12,8},{14,10},{16,20},{18,... | collective-permute-start | bytes 1179656 | tf_op jit(solution)/shard_map/ppermute | solution.py:609
  11.0 0.9 %copy-done.1 = bf16[272,384]{1,0:T(8,128)(2,1)S(1)} copy-done((bf16[272,384]{1,0:T(8,128)(2,1)S(1)}, bf16[272,384]{1,0:T(8,128)(2,1)}, u32[]{:S(2)}) %copy-start.1) | copy-done | bytes 208920
  12.0 0.7 %biases.2.bias._ = f32[4,256,256]{2,1,0:T(8,128)S(1)} custom-call(s32[8]{0:T(128)S(1)} %stack.32.ids, s32[16]{0:T(128)S(1)} %copy-done.4, bf16[272,384]{1,0:T(8,128)(2,1)S(1)} %copy-done.1, bf16[272,384]{1,0:T(8,128)(2,1)S(1)} %copy-done.1), custom_call_target="tpu_custom_call" | custom-call | tf_op jit(solution)/shard_map/biases/pallas_call | solution.py:263
  13.1 0.5 attend_first.1._.refs_2_
  13.6 2.7 %collective-permute-start = (bf16[272,384]{1,0:T(8,128)(2,1)S(1)}, bf16[272,384]{1,0:T(8,128)(2,1)S(1)}, u32[]{:S(2)}, u32[]{:S(2)}) collective-permute-start(bf16[272,384]{1,0:T(8,128)(2,1)S(1)} %copied.1), channel_id=1, source_target_pairs={{0,16},{2,18},{4,20},{6,22},{8,24},{10,26},{12,28},{14,30},{16,0},... | collective-permute-start | bytes 626696 | tf_op jit(solution)/shard_map/ppermute | solution.py:609
  16.2 1.1 %columns.1 = bf16[1,384,1536]{2,1,0:T(8,128)(2,1)} custom-call(bf16[384,3072]{1,0:T(8,128)(2,1)S(1)} %copy-done, f32[3,256,256]{2,1,0:T(8,128)S(1)} %attend_first.1._.refs_2_), custom_call_target="tpu_custom_call" | custom-call | tf_op jit(solution)/shard_map/columns/pallas_call | solution.py:147
  17.4 1.6 %collective-permute-start.10 = (bf16[1,384,1536]{2,1,0:T(8,128)(2,1)}, bf16[1,384,1536]{2,1,0:T(8,128)(2,1)}, u32[]{:S(2)}, u32[]{:S(2)}) collective-permute-start(bf16[1,384,1536]{2,1,0:T(8,128)(2,1)} %columns.1), channel_id=1, source_target_pairs={{0,1},{1,0},{2,3},{3,2},{4,5},{5,4},{6,7},{7,6},{8,9},{9,8},{10,11... | collective-permute-start | bytes 3538952 | tf_op jit(solution)/shard_map/ppermute | solution.py:612
  18.9 0.8 %tables.1 = (bf16[384,128]{1,0:T(8,128)(2,1)S(1)}, bf16[384,128]{1,0:T(8,128)(2,1)S(1)}) custom-call(s32[8]{0:T(128)S(1)} %stack.32.ids, s32[16]{0:T(128)S(1)} %copy-done.4, f32[3,256,256]{2,1,0:T(8,128)S(1)} %attend_first.1._.refs_2_), custom_call_target="tpu_custom_call" | custom-call | tf_op jit(solution)/shard_map/tables/pallas_call | solution.py:230
  19.7 0.7 %biases.3.bias._.second_bias = f32[4,256,256]{2,1,0:T(8,128)S(1)} custom-call(s32[8]{0:T(128)S(1)} %stack.32.ids, s32[16]{0:T(128)S(1)} %copy-done.4, bf16[272,384]{1,0:T(8,128)(2,1)S(1)} %collective-permute-done.1.queries.second, bf16[384,128]{1,0:T(8,128)(2,1)S(1)} %get-tuple-element.21._.table), custom_call_target="tpu_custom_call" | custom-call | tf_op jit(solution)/shard_map/biases/pallas_call | solution.py:263
  20.4 0.5 sibling_first.1.refs_2_
  20.9 1.0 %collective-permute-done.2.refs_0_ = bf16[512,384]{1,0:T(8,128)(2,1)S(1)} collective-permute-done((bf16[512,384]{1,0:T(8,128)(2,1)}, bf16[512,384]{1,0:T(8,128)(2,1)S(1)}, u32[]{:S(2)}, u32[]{:S(2)}) %collective-permute-start.2) | collective-permute-done | bytes 393248 | tf_op jit(solution)/shard_map/ppermute | solution.py:609
  22.0 3.0 %collective-permute-start.5 = (bf16[288,384]{1,0:T(8,128)(2,1)S(1)}, bf16[288,384]{1,0:T(8,128)(2,1)S(1)}, u32[]{:S(2)}, u32[]{:S(2)}) collective-permute-start(bf16[288,384]{1,0:T(8,128)(2,1)S(1)} %slice.6), channel_id=1, source_target_pairs={{0,4},{2,6},{4,0},{6,2},{8,12},{10,14},{12,8},{14,10},{16,20},{18,... | collective-permute-start | bytes 663560 | tf_op jit(solution)/shard_map/ppermute | solution.py:609
  25.0 0.7 %sibling_second.1._.refs_3_ = f32[3,256,256]{2,1,0:T(8,128)S(1)} custom-call(f32[4,256,256]{2,1,0:T(8,128)S(1)} %biases.3.bias._.second_bias, bf16[272,384]{1,0:T(8,128)(2,1)S(1)} %collective-permute-done.1.queries.second, f32[4,256,256]{2,1,0:T(8,128)S(1)} %biases.3.bias._.second_bias, bf16[512,384]{1,0:T(8,128)(2,1)S(1)} %get-tuple-element.22.refs_0_.refs_1_, ...), custom_call_target="tpu_custom_call" | custom-call | tf_op jit(solution)/shard_map/sibling_second/pallas_call | solution.py:386
  25.7 0.7 %attend_second.1._.refs_2_ = f32[3,256,256]{2,1,0:T(8,128)S(1)} custom-call(f32[4,256,256]{2,1,0:T(8,128)S(1)} %biases.2.bias._, bf16[272,384]{1,0:T(8,128)(2,1)S(1)} %copy-done.2, f32[3,256,256]{2,1,0:T(8,128)S(1)} %sibling_second.1._.refs_3_, bf16[512,384]{1,0:T(8,128)(2,1)S(1)} %get-tuple-element.22.refs_0_.refs_1_, ...), custom_call_target="tpu_custom_call" | custom-call | tf_op jit(solution)/shard_map/attend_second/pallas_call | solution.py:386
  26.8 1.1 %other_first.1 = (f32[3,256,256]{2,1,0:T(8,128)S(1)}, f32[4,256,256]{2,1,0:T(8,128)S(1)}) custom-call(bf16[384,128]{1,0:T(8,128)(2,1)S(1)} %get-tuple-element.20.table, bf16[272,384]{1,0:T(8,128)(2,1)S(1)} %gate.3.queries, f32[3,256,256]{2,1,0:T(8,128)S(1)} %attend_second.1._.refs_2_, bf16[512,384]{1,0:T(8,128)(2,1)S(1)} %copy-done.3, ...), custom_call_target="tpu_custom_call" | custom-call | tf_op jit(solution)/shard_map/other_first/pallas_call | solution.py:328
  27.8 0.4 collective-permute-done.4.queries.first
  28.2 1.0 %other_sibling_first.1 = (f32[3,256,256]{2,1,0:T(8,128)S(1)}, f32[4,256,256]{2,1,0:T(8,128)S(1)}) custom-call(bf16[384,128]{1,0:T(8,128)(2,1)S(1)} %get-tuple-element.21._.table, bf16[272,384]{1,0:T(8,128)(2,1)S(1)} %collective-permute-done.4.queries.first, f32[3,256,256]{2,1,0:T(8,128)S(1)} %get-tuple-element.25._.refs_2_, bf16[512,384]{1,0:T(8,128)(2,1)S(1)} %copy-done.3, ...), custom_call_target="tpu_custom_call" | custom-call | tf_op jit(solution)/shard_map/other_sibling_first/pallas_call | solution.py:328
  29.7 0.8 %attend_pair.1._ = bf16[544,384]{1,0:T(8,128)(2,1)S(1)} custom-call(f32[4,256,256]{2,1,0:T(8,128)S(1)} %get-tuple-element.26.first_bias, bf16[272,384]{1,0:T(8,128)(2,1)S(1)} %collective-permute-done.4.queries.first, f32[4,256,256]{2,1,0:T(8,128)S(1)} %biases.3.bias._.second_bias, bf16[272,384]{1,0:T(8,128)(2,1)S(1)} %collective-permute-done.1.queries.second, ...), custom_call_target="tpu_custom_call" | custom-call | tf_op jit(solution)/shard_map/attend_pair/pallas_call | solution.py:365
  30.5 0.5 other_last.1._.kept
  31.0 0.5 attend_last.1.refs_1_.kept
  31.5 0.8 %collective-permute-done.7.refs_0_ = bf16[544,384]{1,0:T(8,128)(2,1)S(1)} collective-permute-done((bf16[544,384]{1,0:T(8,128)(2,1)S(1)}, bf16[544,384]{1,0:T(8,128)(2,1)S(1)}, u32[]{:S(2)}, u32[]{:S(2)}) %collective-permute-start.7) | collective-permute-done | bytes 417824 | tf_op jit(solution)/shard_map/ppermute | solution.py:609
  32.3 0.4 join.1._
  32.6 2.7 %collective-permute-start.8 = (bf16[272,384]{1,0:T(8,128)(2,1)S(1)}, bf16[272,384]{1,0:T(8,128)(2,1)S(1)}, u32[]{:S(2)}, u32[]{:S(2)}) collective-permute-start(bf16[272,384]{1,0:T(8,128)(2,1)S(1)} %join.1._), channel_id=1, source_target_pairs={{0,16},{2,18},{4,20},{6,22},{8,24},{10,26},{12,28},{14,30},{16,0},... | collective-permute-start | bytes 626696 | tf_op jit(solution)/shard_map/ppermute | solution.py:609
  35.4 0.7 %row_sums.1.refs_2_.sums = bf16[16,384]{1,0:T(8,128)(2,1)S(1)} custom-call(bf16[384,3072]{1,0:T(8,128)(2,1)S(1)} %copy-done, bf16[272,384]{1,0:T(8,128)(2,1)S(1)} %join.1._), custom_call_target="tpu_custom_call" | custom-call | tf_op jit(solution)/shard_map/row_sums/pallas_call | solution.py:171
  36.1 9.2 %collective-permute-done.8.refs_1_ = bf16[272,384]{1,0:T(8,128)(2,1)S(1)} collective-permute-done((bf16[272,384]{1,0:T(8,128)(2,1)S(1)}, bf16[272,384]{1,0:T(8,128)(2,1)S(1)}, u32[]{:S(2)}, u32[]{:S(2)}) %collective-permute-start.8) | collective-permute-done | bytes 208928 | tf_op jit(solution)/shard_map/ppermute | solution.py:609
  45.6 1.6 %collective-permute-start.9 = (bf16[256,384]{1,0:T(8,128)(2,1)S(1)}, bf16[256,384]{1,0:T(8,128)(2,1)S(1)}, u32[]{:S(2)}, u32[]{:S(2)}) collective-permute-start(bf16[256,384]{1,0:T(8,128)(2,1)S(1)} %finish.1.own), channel_id=1, source_target_pairs={{0,1},{1,0},{2,3},{3,2},{4,5},{5,4},{6,7},{7,6},{8,9},{9,8},{10,11... | collective-permute-start | bytes 589832 | tf_op jit(solution)/shard_map/ppermute | solution.py:612
  47.2 0.5 collective-permute-start.11
  47.7 1.9 %project_early.1 = (f32[256,1536]{1,0:T(8,128)S(1)}, f32[8,256]{1,0:T(8,128)S(1)}, f32[1,8,256]{2,1,0:T(8,128)S(1)}, bf16[1,384,1536]{2,1,0:T(8,128)(2,1)S(1)}) custom-call(s32[1]{0:T(128)} %bitcast.7.place, bf16[256,384]{1,0:T(8,128)(2,1)S(1)} %finish.1.own, bf16[384,3072]{1,0:T(8,128)(2,1)S(1)} %copy-done, bf16[16,384]{1,0:T(8,128)(2,1)S(1)} %row_sums.1.refs_2_.sums, ...), custom_call_target="tpu_custom_call" | custom-call | tf_op jit(solution)/shard_map/project_early/pallas_call | solution.py:521
  49.6 2.5 %collective-permute-done.11.refs_2_ = bf16[16,384]{1,0:T(8,128)(2,1)S(1)} collective-permute-done((bf16[16,384]{1,0:T(8,128)(2,1)S(1)}, bf16[16,384]{1,0:T(8,128)(2,1)S(1)}, u32[]{:S(2)}, u32[]{:S(2)}) %collective-permute-start.11) | collective-permute-done | bytes 12320 | tf_op jit(solution)/shard_map/ppermute | solution.py:612
  52.1 1.4 %project_last.1 = (bf16[256,1536]{1,0:T(8,128)(2,1)}, f32[1,256]{1,0:T(1,128)}) custom-call(bf16[256,384]{1,0:T(8,128)(2,1)S(1)} %collective-permute-done.9.refs_0_, bf16[1,384,1536]{2,1,0:T(8,128)(2,1)S(1)} %get-tuple-element.28.refs_1_, bf16[16,384]{1,0:T(8,128)(2,1)S(1)} %collective-permute-done.11.refs_2_, f32[256,1536]{1,0:T(8,128)S(1)} %get-tuple-element.29.refs_3_, ...), custom_call_target="tpu_custom_call" | custom-call | tf_op jit(solution)/shard_map/project_last/pallas_call | solution.py:578
  (29 shorter events, 1.8 us)
Async XLA Ops:
  0.6 10.4 %copy-start.4 = (s32[16]{0:T(128)S(1)}, s32[16]{0:T(128)}, u32[]{:S(2)}) copy-start(s32[16]{0:T(128)} %window.5) | copy-start | bytes 196
  6.3 15.6 %collective-permute-start.2 = (bf16[512,384]{1,0:T(8,128)(2,1)}, bf16[512,384]{1,0:T(8,128)(2,1)S(1)}, u32[]{:S(2)}, u32[]{:S(2)}) collective-permute-start(bf16[512,384]{1,0:T(8,128)(2,1)} %get-tuple-element.19.refs_0_), channel_id=1, source_target_pairs={{0,8},{2,10},{4,12},{6,14},{8,0},{10,2},{12,4},{14,6},{16,24},{18,... | collective-permute-start | bytes 1179656 | tf_op jit(solution)/shard_map/ppermute | solution.py:609
  9.4 12.5 %collective-permute-start.3 = (bf16[512,384]{1,0:T(8,128)(2,1)}, bf16[512,384]{1,0:T(8,128)(2,1)S(1)}, u32[]{:S(2)}, u32[]{:S(2)}) collective-permute-start(bf16[512,384]{1,0:T(8,128)(2,1)} %get-tuple-element.19.refs_0_), channel_id=1, source_target_pairs={{0,4},{2,6},{4,0},{6,2},{8,12},{10,14},{12,8},{14,10},{16,20},{18,... | collective-permute-start | bytes 1179656 | tf_op jit(solution)/shard_map/ppermute | solution.py:609
  10.9 8.8 %collective-permute-start.1 = (bf16[272,384]{1,0:T(8,128)(2,1)}, bf16[272,384]{1,0:T(8,128)(2,1)S(1)}, u32[]{:S(2)}, u32[]{:S(2)}) collective-permute-start(bf16[272,384]{1,0:T(8,128)(2,1)} %get-tuple-element.18.queries._.array), channel_id=1, source_target_pairs={{0,2},{2,0},{4,6},{6,4},{8,10},{10,8},{12,14},{14,12},{16,18},{18,... | collective-permute-start | bytes 626696 | tf_op jit(solution)/shard_map/ppermute | solution.py:609
  11.0 0.9 %copy-start.1 = (bf16[272,384]{1,0:T(8,128)(2,1)S(1)}, bf16[272,384]{1,0:T(8,128)(2,1)}, u32[]{:S(2)}) copy-start(bf16[272,384]{1,0:T(8,128)(2,1)} %get-tuple-element.18.queries._.array) | copy-start | bytes 626692
  12.0 0.9 %copy-start.2 = (bf16[272,384]{1,0:T(8,128)(2,1)S(1)}, bf16[272,384]{1,0:T(8,128)(2,1)}, u32[]{:S(2)}) copy-start(bf16[272,384]{1,0:T(8,128)(2,1)} %get-tuple-element.18.queries._.array) | copy-start | bytes 626692
  12.0 1.1 %copy-start.3 = (bf16[512,384]{1,0:T(8,128)(2,1)S(1)}, bf16[512,384]{1,0:T(8,128)(2,1)}, u32[]{:S(2)}) copy-start(bf16[512,384]{1,0:T(8,128)(2,1)} %get-tuple-element.19.refs_0_) | copy-start | bytes 1179652
  13.1 3.2 %copy-start = (bf16[384,3072]{1,0:T(8,128)(2,1)S(1)}, bf16[384,3072]{1,0:T(8,128)(2,1)}, u32[]{:S(2)}) copy-start(bf16[384,3072]{1,0:T(8,128)(2,1)} %w_out.5) | copy-start | bytes 7077892
  13.6 13.2 %collective-permute-start = (bf16[272,384]{1,0:T(8,128)(2,1)S(1)}, bf16[272,384]{1,0:T(8,128)(2,1)S(1)}, u32[]{:S(2)}, u32[]{:S(2)}) collective-permute-start(bf16[272,384]{1,0:T(8,128)(2,1)S(1)} %copied.1), channel_id=1, source_target_pairs={{0,16},{2,18},{4,20},{6,22},{8,24},{10,26},{12,28},{14,30},{16,0},... | collective-permute-start | bytes 626696 | tf_op jit(solution)/shard_map/ppermute | solution.py:609
  17.4 30.3 %collective-permute-start.10 = (bf16[1,384,1536]{2,1,0:T(8,128)(2,1)}, bf16[1,384,1536]{2,1,0:T(8,128)(2,1)}, u32[]{:S(2)}, u32[]{:S(2)}) collective-permute-start(bf16[1,384,1536]{2,1,0:T(8,128)(2,1)} %columns.1), channel_id=1, source_target_pairs={{0,1},{1,0},{2,3},{3,2},{4,5},{5,4},{6,7},{7,6},{8,9},{9,8},{10,11... | collective-permute-start | bytes 3538952 | tf_op jit(solution)/shard_map/ppermute | solution.py:612
  21.9 7.8 %collective-permute-start.6 = (bf16[304,384]{1,0:T(8,128)(2,1)S(1)}, bf16[304,384]{1,0:T(8,128)(2,1)S(1)}, u32[]{:S(2)}, u32[]{:S(2)}) collective-permute-start(bf16[304,384]{1,0:T(8,128)(2,1)S(1)} %slice.7), channel_id=1, source_target_pairs={{0,8},{2,10},{4,12},{6,14},{8,0},{10,2},{12,4},{14,6},{16,24},{18,... | collective-permute-start | bytes 700424 | tf_op jit(solution)/shard_map/ppermute | solution.py:609
  22.0 7.4 %collective-permute-start.5 = (bf16[288,384]{1,0:T(8,128)(2,1)S(1)}, bf16[288,384]{1,0:T(8,128)(2,1)S(1)}, u32[]{:S(2)}, u32[]{:S(2)}) collective-permute-start(bf16[288,384]{1,0:T(8,128)(2,1)S(1)} %slice.6), channel_id=1, source_target_pairs={{0,4},{2,6},{4,0},{6,2},{8,12},{10,14},{12,8},{14,10},{16,20},{18,... | collective-permute-start | bytes 663560 | tf_op jit(solution)/shard_map/ppermute | solution.py:609
  26.7 1.5 %collective-permute-start.4 = (bf16[272,384]{1,0:T(8,128)(2,1)S(1)}, bf16[272,384]{1,0:T(8,128)(2,1)S(1)}, u32[]{:S(2)}, u32[]{:S(2)}) collective-permute-start(bf16[272,384]{1,0:T(8,128)(2,1)S(1)} %gate.3.queries), channel_id=1, source_target_pairs={{0,2},{2,0},{4,6},{6,4},{8,10},{10,8},{12,14},{14,12},{16,18},{18,... | collective-permute-start | bytes 626696 | tf_op jit(solution)/shard_map/ppermute | solution.py:609
  30.5 1.8 %collective-permute-start.7 = (bf16[544,384]{1,0:T(8,128)(2,1)S(1)}, bf16[544,384]{1,0:T(8,128)(2,1)S(1)}, u32[]{:S(2)}, u32[]{:S(2)}) collective-permute-start(bf16[544,384]{1,0:T(8,128)(2,1)S(1)} %attend_pair.1._), channel_id=1, source_target_pairs={{0,2},{2,0},{4,6},{6,4},{8,10},{10,8},{12,14},{14,12},{16,18},{18,... | collective-permute-start | bytes 1253384 | tf_op jit(solution)/shard_map/ppermute | solution.py:609
  32.6 12.7 %collective-permute-start.8 = (bf16[272,384]{1,0:T(8,128)(2,1)S(1)}, bf16[272,384]{1,0:T(8,128)(2,1)S(1)}, u32[]{:S(2)}, u32[]{:S(2)}) collective-permute-start(bf16[272,384]{1,0:T(8,128)(2,1)S(1)} %join.1._), channel_id=1, source_target_pairs={{0,16},{2,18},{4,20},{6,22},{8,24},{10,26},{12,28},{14,30},{16,0},... | collective-permute-start | bytes 626696 | tf_op jit(solution)/shard_map/ppermute | solution.py:609
  45.6 6.5 %collective-permute-start.9 = (bf16[256,384]{1,0:T(8,128)(2,1)S(1)}, bf16[256,384]{1,0:T(8,128)(2,1)S(1)}, u32[]{:S(2)}, u32[]{:S(2)}) collective-permute-start(bf16[256,384]{1,0:T(8,128)(2,1)S(1)} %finish.1.own), channel_id=1, source_target_pairs={{0,1},{1,0},{2,3},{3,2},{4,5},{5,4},{6,7},{7,6},{8,9},{9,8},{10,11... | collective-permute-start | bytes 589832 | tf_op jit(solution)/shard_map/ppermute | solution.py:612
  47.2 5.0 %collective-permute-start.11 = (bf16[16,384]{1,0:T(8,128)(2,1)S(1)}, bf16[16,384]{1,0:T(8,128)(2,1)S(1)}, u32[]{:S(2)}, u32[]{:S(2)}) collective-permute-start(bf16[16,384]{1,0:T(8,128)(2,1)S(1)} %row_sums.1.refs_2_.sums), channel_id=1, source_target_pairs={{0,1},{1,0},{2,3},{3,2},{4,5},{5,4},{6,7},{7,6},{8,9},{9,8},{10,11... | collective-permute-start | bytes 36872 | tf_op jit(solution)/shard_map/ppermute | solution.py:612

commit v6 on v5

--- a/solution.py
+++ b/solution.py
@@ -444,11 +444,13 @@
 
 
 def gate_kernel(array, _, out):
-    pass
+    out[...] = array[...]
 
 
 def gate_all_kernel(*refs):
-    pass
+    n = len(refs) // 2
+    for array, out in zip(refs[:n], refs[n + 1 :]):
+        out[...] = array[...]
 
 
 def gate_all(arrays, before):
@@ -664,7 +666,7 @@
     )
     late = []
     for i, o in enumerate(far, n_near):
-        late.append(((gate(keys[o], both), gate(values[o], both)), i))
+        late.append(((keys[o], values[o]), i))
     across = attend_pair(
         (other_sib_bias, other_sib, both), (sib_bias, sib_queries, sib), late, every, "attend_pair"
     )

time: 53.7 us -> 53.8 us (level)
  no operation moved by 1% of the time
where the time goes in v6:
time: 53.8 us; the launch traced here: 53.6 us
  Pallas kernels  20 us (37%)
  starting transfers between devices  16.8 us (31%)
  waiting for transfers between devices  14.5 us (27%)
  local copies, waits for them, and re-layouts  1.47 us (3%)
  between operations  0.82 us (2%)
    ppermute x9, starting transfers between devices, swapped(): return lax.ppermute(array, 'frame', [(i, i ^ by) for i in range(n_frame)])  13.1 us
    ppermute x9, waiting for transfers between devices, swapped(): return lax.ppermute(array, 'frame', [(i, i ^ by) for i in range(n_frame)])  12 us
    pallas_call x1, Pallas kernels, project(): pl.pallas_call(functools.partial(project_kernel, steps), in_specs=[ANYWHE...  5.68 us
    ppermute x3, starting transfers between devices, from_head(): lax.ppermute(array, 'head', [(i, (i + k) % n_head) for i in range(n_head)])  3.65 us
    pallas_call x6, Pallas kernels, attend(): pl.pallas_call(functools.partial(attend_kernel, slabs, [len(c) > 1 for c,...  3.31 us
    ppermute x3, waiting for transfers between devices, from_head(): lax.ppermute(array, 'head', [(i, (i + k) % n_head) for i in range(n_head)])  2.5 us
    pallas_call x2, Pallas kernels, attend_other(): pl.pallas_call(functools.partial(other_kernel, [s for _, s in parts], [le...  2.11 us
    pallas_call x1, Pallas kernels, project_early(): pl.pallas_call(functools.partial(early_kernel, n_head), in_specs=[IN_SMEM...  1.92 us
  transfers between devices with their start and end apart: 12, of which 8 were waited for; matrix products, arithmetic and copies ran while one was open for 0% of the time, Pallas kernels for 24%

profile of v6, /device:TPU:0, one launch (start us, length us, event | category | flops | bytes accessed | tf_op | source)
XLA Modules:
  0.0 53.6 jit_solution(7190756019081518845)
XLA Ops:
  0.6 5.7 %project.1 = (bf16[512,384]{1,0:T(8,128)(2,1)}, bf16[272,384]{1,0:T(8,128)(2,1)}) custom-call(bf16[256,3072]{1,0:T(8,128)(2,1)} %tokens.1, bf16[3,3072,384]{2,1,0:T(8,128)(2,1)} %w_qkv.1, f32[2,384]{1,0:T(2,128)} %gains.1, s32[2,4]{1,0:T(2,128)} %near_mask.1, s32[2,32]{1,0:T(2,128)} %far_pattern.1), custom_call_target="tpu_custom_call" | custom-call | tf_op jit(solution)/shard_map/project/pallas_call | solution.py:100
  6.3 3.1 %collective-permute-start.2 = (bf16[512,384]{1,0:T(8,128)(2,1)}, bf16[512,384]{1,0:T(8,128)(2,1)S(1)}, u32[]{:S(2)}, u32[]{:S(2)}) collective-permute-start(bf16[512,384]{1,0:T(8,128)(2,1)} %get-tuple-element.19.refs_0_), channel_id=1, source_target_pairs={{0,8},{2,10},{4,12},{6,14},{8,0},{10,2},{12,4},{14,6},{16,24},{18,... | collective-permute-start | bytes 1179656 | tf_op jit(solution)/shard_map/ppermute | solution.py:611
  9.4 1.5 %collective-permute-start.3 = (bf16[512,384]{1,0:T(8,128)(2,1)}, bf16[512,384]{1,0:T(8,128)(2,1)S(1)}, u32[]{:S(2)}, u32[]{:S(2)}) collective-permute-start(bf16[512,384]{1,0:T(8,128)(2,1)} %get-tuple-element.19.refs_0_), channel_id=1, source_target_pairs={{0,4},{2,6},{4,0},{6,2},{8,12},{10,14},{12,8},{14,10},{16,20},{18,... | collective-permute-start | bytes 1179656 | tf_op jit(solution)/shard_map/ppermute | solution.py:611
  11.0 0.9 %copy-done.1 = bf16[272,384]{1,0:T(8,128)(2,1)S(1)} copy-done((bf16[272,384]{1,0:T(8,128)(2,1)S(1)}, bf16[272,384]{1,0:T(8,128)(2,1)}, u32[]{:S(2)}) %copy-start.1) | copy-done | bytes 208920
  12.0 0.7 %biases.2.bias._ = f32[4,256,256]{2,1,0:T(8,128)S(1)} custom-call(s32[8]{0:T(128)S(1)} %stack.32.ids, s32[16]{0:T(128)S(1)} %copy-done.4, bf16[272,384]{1,0:T(8,128)(2,1)S(1)} %copy-done.1, bf16[272,384]{1,0:T(8,128)(2,1)S(1)} %copy-done.1), custom_call_target="tpu_custom_call" | custom-call | tf_op jit(solution)/shard_map/biases/pallas_call | solution.py:263
  13.1 0.5 attend_first.1._.refs_2_
  13.6 2.7 %collective-permute-start = (bf16[272,384]{1,0:T(8,128)(2,1)S(1)}, bf16[272,384]{1,0:T(8,128)(2,1)S(1)}, u32[]{:S(2)}, u32[]{:S(2)}) collective-permute-start(bf16[272,384]{1,0:T(8,128)(2,1)S(1)} %copied.1), channel_id=1, source_target_pairs={{0,16},{2,18},{4,20},{6,22},{8,24},{10,26},{12,28},{14,30},{16,0},... | collective-permute-start | bytes 626696 | tf_op jit(solution)/shard_map/ppermute | solution.py:611
  16.2 1.1 %columns.1 = bf16[1,384,1536]{2,1,0:T(8,128)(2,1)} custom-call(bf16[384,3072]{1,0:T(8,128)(2,1)S(1)} %copy-done, f32[3,256,256]{2,1,0:T(8,128)S(1)} %attend_first.1._.refs_2_), custom_call_target="tpu_custom_call" | custom-call | tf_op jit(solution)/shard_map/columns/pallas_call | solution.py:147
  17.4 1.6 %collective-permute-start.10 = (bf16[1,384,1536]{2,1,0:T(8,128)(2,1)}, bf16[1,384,1536]{2,1,0:T(8,128)(2,1)}, u32[]{:S(2)}, u32[]{:S(2)}) collective-permute-start(bf16[1,384,1536]{2,1,0:T(8,128)(2,1)} %columns.1), channel_id=1, source_target_pairs={{0,1},{1,0},{2,3},{3,2},{4,5},{5,4},{6,7},{7,6},{8,9},{9,8},{10,11... | collective-permute-start | bytes 3538952 | tf_op jit(solution)/shard_map/ppermute | solution.py:614
  18.9 0.8 %tables.1 = (bf16[384,128]{1,0:T(8,128)(2,1)S(1)}, bf16[384,128]{1,0:T(8,128)(2,1)S(1)}) custom-call(s32[8]{0:T(128)S(1)} %stack.32.ids, s32[16]{0:T(128)S(1)} %copy-done.4, f32[3,256,256]{2,1,0:T(8,128)S(1)} %attend_first.1._.refs_2_), custom_call_target="tpu_custom_call" | custom-call | tf_op jit(solution)/shard_map/tables/pallas_call | solution.py:230
  19.7 0.7 %biases.3.bias._.second_bias = f32[4,256,256]{2,1,0:T(8,128)S(1)} custom-call(s32[8]{0:T(128)S(1)} %stack.32.ids, s32[16]{0:T(128)S(1)} %copy-done.4, bf16[272,384]{1,0:T(8,128)(2,1)S(1)} %collective-permute-done.1.queries.second, bf16[384,128]{1,0:T(8,128)(2,1)S(1)} %get-tuple-element.21._.table), custom_call_target="tpu_custom_call" | custom-call | tf_op jit(solution)/shard_map/biases/pallas_call | solution.py:263
  20.4 0.5 sibling_first.1.refs_2_
  20.9 1.0 %collective-permute-done.2.refs_0_ = bf16[512,384]{1,0:T(8,128)(2,1)S(1)} collective-permute-done((bf16[512,384]{1,0:T(8,128)(2,1)}, bf16[512,384]{1,0:T(8,128)(2,1)S(1)}, u32[]{:S(2)}, u32[]{:S(2)}) %collective-permute-start.2) | collective-permute-done | bytes 393248 | tf_op jit(solution)/shard_map/ppermute | solution.py:611
  22.2 3.0 %collective-permute-start.5 = (bf16[288,384]{1,0:T(8,128)(2,1)S(1)}, bf16[288,384]{1,0:T(8,128)(2,1)S(1)}, u32[]{:S(2)}, u32[]{:S(2)}) collective-permute-start(bf16[288,384]{1,0:T(8,128)(2,1)S(1)} %slice.6), channel_id=1, source_target_pairs={{0,4},{2,6},{4,0},{6,2},{8,12},{10,14},{12,8},{14,10},{16,20},{18,... | collective-permute-start | bytes 663560 | tf_op jit(solution)/shard_map/ppermute | solution.py:611
  25.1 0.7 %sibling_second.1._.refs_3_ = f32[3,256,256]{2,1,0:T(8,128)S(1)} custom-call(f32[4,256,256]{2,1,0:T(8,128)S(1)} %biases.3.bias._.second_bias, bf16[272,384]{1,0:T(8,128)(2,1)S(1)} %collective-permute-done.1.queries.second, f32[4,256,256]{2,1,0:T(8,128)S(1)} %biases.3.bias._.second_bias, bf16[512,384]{1,0:T(8,128)(2,1)S(1)} %get-tuple-element.22.refs_0_.refs_1_, ...), custom_call_target="tpu_custom_call" | custom-call | tf_op jit(solution)/shard_map/sibling_second/pallas_call | solution.py:386
  25.8 0.7 %attend_second.1._.refs_2_ = f32[3,256,256]{2,1,0:T(8,128)S(1)} custom-call(f32[4,256,256]{2,1,0:T(8,128)S(1)} %biases.2.bias._, bf16[272,384]{1,0:T(8,128)(2,1)S(1)} %copy-done.2, f32[3,256,256]{2,1,0:T(8,128)S(1)} %sibling_second.1._.refs_3_, bf16[512,384]{1,0:T(8,128)(2,1)S(1)} %get-tuple-element.22.refs_0_.refs_1_, ...), custom_call_target="tpu_custom_call" | custom-call | tf_op jit(solution)/shard_map/attend_second/pallas_call | solution.py:386
  26.9 1.1 %other_first.1 = (f32[3,256,256]{2,1,0:T(8,128)S(1)}, f32[4,256,256]{2,1,0:T(8,128)S(1)}) custom-call(bf16[384,128]{1,0:T(8,128)(2,1)S(1)} %get-tuple-element.20.table, bf16[272,384]{1,0:T(8,128)(2,1)S(1)} %gate.1.queries, f32[3,256,256]{2,1,0:T(8,128)S(1)} %attend_second.1._.refs_2_, bf16[512,384]{1,0:T(8,128)(2,1)S(1)} %copy-done.3, ...), custom_call_target="tpu_custom_call" | custom-call | tf_op jit(solution)/shard_map/other_first/pallas_call | solution.py:328
  27.9 0.4 collective-permute-done.4.queries.first
  28.3 1.1 %other_sibling_first.1 = (f32[3,256,256]{2,1,0:T(8,128)S(1)}, f32[4,256,256]{2,1,0:T(8,128)S(1)}) custom-call(bf16[384,128]{1,0:T(8,128)(2,1)S(1)} %get-tuple-element.21._.table, bf16[272,384]{1,0:T(8,128)(2,1)S(1)} %collective-permute-done.4.queries.first, f32[3,256,256]{2,1,0:T(8,128)S(1)} %get-tuple-element.25._.refs_2_, bf16[512,384]{1,0:T(8,128)(2,1)S(1)} %copy-done.3, ...), custom_call_target="tpu_custom_call" | custom-call | tf_op jit(solution)/shard_map/other_sibling_first/pallas_call | solution.py:328
  29.8 0.8 %attend_pair.1._ = bf16[544,384]{1,0:T(8,128)(2,1)S(1)} custom-call(f32[4,256,256]{2,1,0:T(8,128)S(1)} %get-tuple-element.26.first_bias, bf16[272,384]{1,0:T(8,128)(2,1)S(1)} %collective-permute-done.4.queries.first, f32[4,256,256]{2,1,0:T(8,128)S(1)} %biases.3.bias._.second_bias, bf16[272,384]{1,0:T(8,128)(2,1)S(1)} %collective-permute-done.1.queries.second, ...), custom_call_target="tpu_custom_call" | custom-call | tf_op jit(solution)/shard_map/attend_pair/pallas_call | solution.py:365
  30.6 0.5 other_last.1._.kept
  31.1 0.5 attend_last.1.refs_1_.kept
  31.6 0.8 %collective-permute-done.7.refs_0_ = bf16[544,384]{1,0:T(8,128)(2,1)S(1)} collective-permute-done((bf16[544,384]{1,0:T(8,128)(2,1)S(1)}, bf16[544,384]{1,0:T(8,128)(2,1)S(1)}, u32[]{:S(2)}, u32[]{:S(2)}) %collective-permute-start.7) | collective-permute-done | bytes 417824 | tf_op jit(solution)/shard_map/ppermute | solution.py:611
  32.4 0.4 join.1._
  32.8 2.7 %collective-permute-start.8 = (bf16[272,384]{1,0:T(8,128)(2,1)S(1)}, bf16[272,384]{1,0:T(8,128)(2,1)S(1)}, u32[]{:S(2)}, u32[]{:S(2)}) collective-permute-start(bf16[272,384]{1,0:T(8,128)(2,1)S(1)} %join.1._), channel_id=1, source_target_pairs={{0,16},{2,18},{4,20},{6,22},{8,24},{10,26},{12,28},{14,30},{16,0},... | collective-permute-start | bytes 626696 | tf_op jit(solution)/shard_map/ppermute | solution.py:611
  35.5 0.7 %row_sums.1.refs_2_.sums = bf16[16,384]{1,0:T(8,128)(2,1)S(1)} custom-call(bf16[384,3072]{1,0:T(8,128)(2,1)S(1)} %copy-done, bf16[272,384]{1,0:T(8,128)(2,1)S(1)} %join.1._), custom_call_target="tpu_custom_call" | custom-call | tf_op jit(solution)/shard_map/row_sums/pallas_call | solution.py:171
  36.2 9.2 %collective-permute-done.8.refs_1_ = bf16[272,384]{1,0:T(8,128)(2,1)S(1)} collective-permute-done((bf16[272,384]{1,0:T(8,128)(2,1)S(1)}, bf16[272,384]{1,0:T(8,128)(2,1)S(1)}, u32[]{:S(2)}, u32[]{:S(2)}) %collective-permute-start.8) | collective-permute-done | bytes 208928 | tf_op jit(solution)/shard_map/ppermute | solution.py:611
  45.7 1.6 %collective-permute-start.9 = (bf16[256,384]{1,0:T(8,128)(2,1)S(1)}, bf16[256,384]{1,0:T(8,128)(2,1)S(1)}, u32[]{:S(2)}, u32[]{:S(2)}) collective-permute-start(bf16[256,384]{1,0:T(8,128)(2,1)S(1)} %finish.1.own), channel_id=1, source_target_pairs={{0,1},{1,0},{2,3},{3,2},{4,5},{5,4},{6,7},{7,6},{8,9},{9,8},{10,11... | collective-permute-start | bytes 589832 | tf_op jit(solution)/shard_map/ppermute | solution.py:614
  47.3 0.5 collective-permute-start.11
  47.8 1.9 %project_early.1 = (f32[256,1536]{1,0:T(8,128)S(1)}, f32[8,256]{1,0:T(8,128)S(1)}, f32[1,8,256]{2,1,0:T(8,128)S(1)}, bf16[1,384,1536]{2,1,0:T(8,128)(2,1)S(1)}) custom-call(s32[1]{0:T(128)} %bitcast.7.place, bf16[256,384]{1,0:T(8,128)(2,1)S(1)} %finish.1.own, bf16[384,3072]{1,0:T(8,128)(2,1)S(1)} %copy-done, bf16[16,384]{1,0:T(8,128)(2,1)S(1)} %row_sums.1.refs_2_.sums, ...), custom_call_target="tpu_custom_call" | custom-call | tf_op jit(solution)/shard_map/project_early/pallas_call | solution.py:523
  49.8 2.5 %collective-permute-done.11.refs_2_ = bf16[16,384]{1,0:T(8,128)(2,1)S(1)} collective-permute-done((bf16[16,384]{1,0:T(8,128)(2,1)S(1)}, bf16[16,384]{1,0:T(8,128)(2,1)S(1)}, u32[]{:S(2)}, u32[]{:S(2)}) %collective-permute-start.11) | collective-permute-done | bytes 12320 | tf_op jit(solution)/shard_map/ppermute | solution.py:614
  52.2 1.4 %project_last.1 = (bf16[256,1536]{1,0:T(8,128)(2,1)}, f32[1,256]{1,0:T(1,128)}) custom-call(bf16[256,384]{1,0:T(8,128)(2,1)S(1)} %collective-permute-done.9.refs_0_, bf16[1,384,1536]{2,1,0:T(8,128)(2,1)S(1)} %get-tuple-element.28.refs_1_, bf16[16,384]{1,0:T(8,128)(2,1)S(1)} %collective-permute-done.11.refs_2_, f32[256,1536]{1,0:T(8,128)S(1)} %get-tuple-element.29.refs_3_, ...), custom_call_target="tpu_custom_call" | custom-call | tf_op jit(solution)/shard_map/project_last/pallas_call | solution.py:580
  (27 shorter events, 1.9 us)
Async XLA Ops:
  0.6 10.4 %copy-start.4 = (s32[16]{0:T(128)S(1)}, s32[16]{0:T(128)}, u32[]{:S(2)}) copy-start(s32[16]{0:T(128)} %window.5) | copy-start | bytes 196
  6.3 15.6 %collective-permute-start.2 = (bf16[512,384]{1,0:T(8,128)(2,1)}, bf16[512,384]{1,0:T(8,128)(2,1)S(1)}, u32[]{:S(2)}, u32[]{:S(2)}) collective-permute-start(bf16[512,384]{1,0:T(8,128)(2,1)} %get-tuple-element.19.refs_0_), channel_id=1, source_target_pairs={{0,8},{2,10},{4,12},{6,14},{8,0},{10,2},{12,4},{14,6},{16,24},{18,... | collective-permute-start | bytes 1179656 | tf_op jit(solution)/shard_map/ppermute | solution.py:611
  9.4 12.5 %collective-permute-start.3 = (bf16[512,384]{1,0:T(8,128)(2,1)}, bf16[512,384]{1,0:T(8,128)(2,1)S(1)}, u32[]{:S(2)}, u32[]{:S(2)}) collective-permute-start(bf16[512,384]{1,0:T(8,128)(2,1)} %get-tuple-element.19.refs_0_), channel_id=1, source_target_pairs={{0,4},{2,6},{4,0},{6,2},{8,12},{10,14},{12,8},{14,10},{16,20},{18,... | collective-permute-start | bytes 1179656 | tf_op jit(solution)/shard_map/ppermute | solution.py:611
  10.9 8.8 %collective-permute-start.1 = (bf16[272,384]{1,0:T(8,128)(2,1)}, bf16[272,384]{1,0:T(8,128)(2,1)S(1)}, u32[]{:S(2)}, u32[]{:S(2)}) collective-permute-start(bf16[272,384]{1,0:T(8,128)(2,1)} %get-tuple-element.18.queries._.array), channel_id=1, source_target_pairs={{0,2},{2,0},{4,6},{6,4},{8,10},{10,8},{12,14},{14,12},{16,18},{18,... | collective-permute-start | bytes 626696 | tf_op jit(solution)/shard_map/ppermute | solution.py:611
  11.0 0.9 %copy-start.1 = (bf16[272,384]{1,0:T(8,128)(2,1)S(1)}, bf16[272,384]{1,0:T(8,128)(2,1)}, u32[]{:S(2)}) copy-start(bf16[272,384]{1,0:T(8,128)(2,1)} %get-tuple-element.18.queries._.array) | copy-start | bytes 626692
  12.0 0.9 %copy-start.2 = (bf16[272,384]{1,0:T(8,128)(2,1)S(1)}, bf16[272,384]{1,0:T(8,128)(2,1)}, u32[]{:S(2)}) copy-start(bf16[272,384]{1,0:T(8,128)(2,1)} %get-tuple-element.18.queries._.array) | copy-start | bytes 626692
  12.0 1.1 %copy-start.3 = (bf16[512,384]{1,0:T(8,128)(2,1)S(1)}, bf16[512,384]{1,0:T(8,128)(2,1)}, u32[]{:S(2)}) copy-start(bf16[512,384]{1,0:T(8,128)(2,1)} %get-tuple-element.19.refs_0_) | copy-start | bytes 1179652
  13.1 3.2 %copy-start = (bf16[384,3072]{1,0:T(8,128)(2,1)S(1)}, bf16[384,3072]{1,0:T(8,128)(2,1)}, u32[]{:S(2)}) copy-start(bf16[384,3072]{1,0:T(8,128)(2,1)} %w_out.5) | copy-start | bytes 7077892
  13.6 13.2 %collective-permute-start = (bf16[272,384]{1,0:T(8,128)(2,1)S(1)}, bf16[272,384]{1,0:T(8,128)(2,1)S(1)}, u32[]{:S(2)}, u32[]{:S(2)}) collective-permute-start(bf16[272,384]{1,0:T(8,128)(2,1)S(1)} %copied.1), channel_id=1, source_target_pairs={{0,16},{2,18},{4,20},{6,22},{8,24},{10,26},{12,28},{14,30},{16,0},... | collective-permute-start | bytes 626696 | tf_op jit(solution)/shard_map/ppermute | solution.py:611
  17.4 30.5 %collective-permute-start.10 = (bf16[1,384,1536]{2,1,0:T(8,128)(2,1)}, bf16[1,384,1536]{2,1,0:T(8,128)(2,1)}, u32[]{:S(2)}, u32[]{:S(2)}) collective-permute-start(bf16[1,384,1536]{2,1,0:T(8,128)(2,1)} %columns.1), channel_id=1, source_target_pairs={{0,1},{1,0},{2,3},{3,2},{4,5},{5,4},{6,7},{7,6},{8,9},{9,8},{10,11... | collective-permute-start | bytes 3538952 | tf_op jit(solution)/shard_map/ppermute | solution.py:614
  22.1 7.8 %collective-permute-start.6 = (bf16[304,384]{1,0:T(8,128)(2,1)S(1)}, bf16[304,384]{1,0:T(8,128)(2,1)S(1)}, u32[]{:S(2)}, u32[]{:S(2)}) collective-permute-start(bf16[304,384]{1,0:T(8,128)(2,1)S(1)} %slice.7), channel_id=1, source_target_pairs={{0,8},{2,10},{4,12},{6,14},{8,0},{10,2},{12,4},{14,6},{16,24},{18,... | collective-permute-start | bytes 700424 | tf_op jit(solution)/shard_map/ppermute | solution.py:611
  22.2 7.4 %collective-permute-start.5 = (bf16[288,384]{1,0:T(8,128)(2,1)S(1)}, bf16[288,384]{1,0:T(8,128)(2,1)S(1)}, u32[]{:S(2)}, u32[]{:S(2)}) collective-permute-start(bf16[288,384]{1,0:T(8,128)(2,1)S(1)} %slice.6), channel_id=1, source_target_pairs={{0,4},{2,6},{4,0},{6,2},{8,12},{10,14},{12,8},{14,10},{16,20},{18,... | collective-permute-start | bytes 663560 | tf_op jit(solution)/shard_map/ppermute | solution.py:611
  26.8 1.5 %collective-permute-start.4 = (bf16[272,384]{1,0:T(8,128)(2,1)S(1)}, bf16[272,384]{1,0:T(8,128)(2,1)S(1)}, u32[]{:S(2)}, u32[]{:S(2)}) collective-permute-start(bf16[272,384]{1,0:T(8,128)(2,1)S(1)} %gate.1.queries), channel_id=1, source_target_pairs={{0,2},{2,0},{4,6},{6,4},{8,10},{10,8},{12,14},{14,12},{16,18},{18,... | collective-permute-start | bytes 626696 | tf_op jit(solution)/shard_map/ppermute | solution.py:611
  30.6 1.8 %collective-permute-start.7 = (bf16[544,384]{1,0:T(8,128)(2,1)S(1)}, bf16[544,384]{1,0:T(8,128)(2,1)S(1)}, u32[]{:S(2)}, u32[]{:S(2)}) collective-permute-start(bf16[544,384]{1,0:T(8,128)(2,1)S(1)} %attend_pair.1._), channel_id=1, source_target_pairs={{0,2},{2,0},{4,6},{6,4},{8,10},{10,8},{12,14},{14,12},{16,18},{18,... | collective-permute-start | bytes 1253384 | tf_op jit(solution)/shard_map/ppermute | solution.py:611
  32.8 12.7 %collective-permute-start.8 = (bf16[272,384]{1,0:T(8,128)(2,1)S(1)}, bf16[272,384]{1,0:T(8,128)(2,1)S(1)}, u32[]{:S(2)}, u32[]{:S(2)}) collective-permute-start(bf16[272,384]{1,0:T(8,128)(2,1)S(1)} %join.1._), channel_id=1, source_target_pairs={{0,16},{2,18},{4,20},{6,22},{8,24},{10,26},{12,28},{14,30},{16,0},... | collective-permute-start | bytes 626696 | tf_op jit(solution)/shard_map/ppermute | solution.py:611
  45.7 6.5 %collective-permute-start.9 = (bf16[256,384]{1,0:T(8,128)(2,1)S(1)}, bf16[256,384]{1,0:T(8,128)(2,1)S(1)}, u32[]{:S(2)}, u32[]{:S(2)}) collective-permute-start(bf16[256,384]{1,0:T(8,128)(2,1)S(1)} %finish.1.own), channel_id=1, source_target_pairs={{0,1},{1,0},{2,3},{3,2},{4,5},{5,4},{6,7},{7,6},{8,9},{9,8},{10,11... | collective-permute-start | bytes 589832 | tf_op jit(solution)/shard_map/ppermute | solution.py:614
  47.3 5.0 %collective-permute-start.11 = (bf16[16,384]{1,0:T(8,128)(2,1)S(1)}, bf16[16,384]{1,0:T(8,128)(2,1)S(1)}, u32[]{:S(2)}, u32[]{:S(2)}) collective-permute-start(bf16[16,384]{1,0:T(8,128)(2,1)S(1)} %row_sums.1.refs_2_.sums), channel_id=1, source_target_pairs={{0,1},{1,0},{2,3},{3,2},{4,5},{5,4},{6,7},{7,6},{8,9},{9,8},{10,11... | collective-permute-start | bytes 36872 | tf_op jit(solution)/shard_map/ppermute | solution.py:614

commit v7 on v6

--- a/solution.py
+++ b/solution.py
@@ -43,8 +43,8 @@
     return jnp.concatenate(parts, axis=1)
 
 
-def project_kernel(steps, tokens, w_qkv, gains, near_mask, far_pattern, kv, queries, *scratch):
-    token_buf, w_buf, gain_buf, near_buf, far_buf, total, sems, small_sems = scratch
+def project_kernel(steps, tokens, w_qkv, gains, near_mask, far_pattern, kv_out, queries_out, *scratch):
+    token_buf, w_buf, gain_buf, near_buf, far_buf, total, kv, queries, sems, small_sems = scratch
     rows, width = tokens.shape
     count, _, cols = w_qkv.shape
     deep = width // steps
@@ -82,8 +82,15 @@
     for copy in small:
         copy.wait()
     query, key, value = (part[:, j * cols : (j + 1) * cols] for j in range(count))
+    stores = [
+        pltpu.make_async_copy(kv.at[pl.ds(0, rows)], kv_out.at[pl.ds(0, rows)], small_sems.at[3]),
+        pltpu.make_async_copy(kv.at[pl.ds(rows, rows)], kv_out.at[pl.ds(rows, rows)], small_sems.at[4]),
+        pltpu.make_async_copy(queries, queries_out, small_sems.at[5]),
+    ]
+    kv[rows:, :] = value.astype(BF16)
+    stores[1].start()
     kv[:rows, :] = normed(key, gain_buf[1:2, :], 1.0).astype(BF16)
-    kv[rows:, :] = value.astype(BF16)
+    stores[0].start()
     queries[:rows, :] = normed(query, gain_buf[0:1, :], HD ** (-0.5)).astype(BF16)
     n_blocks, n_near = near_mask.shape
     queries[rows:, :] = jnp.zeros((PAD, cols), BF16)
@@ -91,6 +98,9 @@
     queries[rows : rows + n_blocks, HD : HD + far_pattern.shape[1]] = (
         far_buf[...].astype(F32).astype(BF16)
     )
+    stores[2].start()
+    for store in stores:
+        store.wait()
 
 
 def project(tokens, w_qkv, gains, near_mask, far_pattern):
@@ -100,7 +110,7 @@
     return pl.pallas_call(
         functools.partial(project_kernel, steps),
         in_specs=[ANYWHERE] * 5,
-        out_specs=[IN_VMEM] * 2,
+        out_specs=[ANYWHERE] * 2,
         out_shape=[
             jax.ShapeDtypeStruct((2 * rows, cols), BF16),
             jax.ShapeDtypeStruct((rows + PAD, cols), BF16),
@@ -112,8 +122,10 @@
             VMEM(near_mask.shape, jnp.int32),
             VMEM(far_pattern.shape, jnp.int32),
             VMEM((rows, count * cols), F32),
+            VMEM((2 * rows, cols), BF16),
+            VMEM((rows + PAD, cols), BF16),
             pltpu.SemaphoreType.DMA((1 + count, steps)),
-            pltpu.SemaphoreType.DMA((3,)),
+            pltpu.SemaphoreType.DMA((6,)),
         ],
         compiler_params=params(56),
         cost_estimate=cost(5.0),
@@ -636,14 +648,14 @@
 
     mine = [((kv,), 0)]
     own_bias = bias_of(0, queries, queries)
-    own = attend(own_bias, queries, own_bias, mine, None, every, "attend_first")
+    other_table, other_sib_table = tables(
+        (2, 3), ids, window, queries.shape[1], n_blocks, own_bias
+    )
+    own = attend(own_bias, queries, other_sib_table, mine, None, every, "attend_first")
     other_queries = swapped(copied(queries, own), half)
     payload = columns_of(w_out, n_head, own)
     received = from_heads([payload[k - 1 : k] for k in range(1, n_head)])
-    other_table, other_sib_table = tables(
-        (2, 3), ids, window, queries.shape[1], n_blocks, own
-    )
-    sib_bias = bias_of(1, sib_queries, other_sib_table)
+    sib_bias = bias_of(1, sib_queries, own)
     sib = attend(sib_bias, sib_queries, sib_bias, mine, None, every, "sibling_first")
 
     near = dict(zip(spans, gate_all([near[by] for by in spans], sib)))

time: 53.8 us -> 53.6 us (level)
  transfers between devices with their start and end apart: 12 -> 12, of which waited for: 8 -> 7; matrix products, arithmetic and copies ran while one was open for 0% -> 0% of each run, Pallas kernels for 24% -> 24%
where the time goes in v7:
time: 53.6 us; the launch traced here: 53.4 us
  Pallas kernels  19.9 us (37%)
  starting transfers between devices  16.8 us (31%)
  waiting for transfers between devices  14.8 us (28%)
  local copies, waits for them, and re-layouts  1.08 us (2%)
  between operations  0.82 us (2%)
    ppermute x9, starting transfers between devices, swapped(): return lax.ppermute(array, 'frame', [(i, i ^ by) for i in range(n_frame)])  13.1 us
    ppermute x9, waiting for transfers between devices, swapped(): return lax.ppermute(array, 'frame', [(i, i ^ by) for i in range(n_frame)])  12.4 us
    pallas_call x1, Pallas kernels, project(): pl.pallas_call(functools.partial(project_kernel, steps), in_specs=[ANYWHE...  5.57 us
    ppermute x3, starting transfers between devices, from_head(): lax.ppermute(array, 'head', [(i, (i + k) % n_head) for i in range(n_head)])  3.65 us
    pallas_call x6, Pallas kernels, attend(): pl.pallas_call(functools.partial(attend_kernel, slabs, [len(c) > 1 for c,...  3.31 us
    ppermute x3, waiting for transfers between devices, from_head(): lax.ppermute(array, 'head', [(i, (i + k) % n_head) for i in range(n_head)])  2.43 us
    pallas_call x2, Pallas kernels, attend_other(): pl.pallas_call(functools.partial(other_kernel, [s for _, s in parts], [le...  2.11 us
    pallas_call x1, Pallas kernels, project_early(): pl.pallas_call(functools.partial(early_kernel, n_head), in_specs=[IN_SMEM...  1.92 us
  transfers between devices with their start and end apart: 12, of which 7 were waited for; matrix products, arithmetic and copies ran while one was open for 0% of the time, Pallas kernels for 24%

profile of v7, /device:TPU:0, one launch (start us, length us, event | category | flops | bytes accessed | tf_op | source)
XLA Modules:
  0.0 53.4 jit_solution(3567011565380036919)
XLA Ops:
  0.6 5.6 %project.1 = (bf16[512,384]{1,0:T(8,128)(2,1)}, bf16[272,384]{1,0:T(8,128)(2,1)}) custom-call(bf16[256,3072]{1,0:T(8,128)(2,1)} %tokens.1, bf16[3,3072,384]{2,1,0:T(8,128)(2,1)} %w_qkv.1, f32[2,384]{1,0:T(2,128)} %gains.1, s32[2,4]{1,0:T(2,128)} %near_mask.1, s32[2,32]{1,0:T(2,128)} %far_pattern.1), custom_call_target="tpu_custom_call" | custom-call | tf_op jit(solution)/shard_map/project/pallas_call | solution.py:110
  6.2 3.1 %collective-permute-start.2 = (bf16[512,384]{1,0:T(8,128)(2,1)}, bf16[512,384]{1,0:T(8,128)(2,1)S(1)}, u32[]{:S(2)}, u32[]{:S(2)}) collective-permute-start(bf16[512,384]{1,0:T(8,128)(2,1)} %get-tuple-element.21.refs_0_), channel_id=1, source_target_pairs={{0,8},{2,10},{4,12},{6,14},{8,0},{10,2},{12,4},{14,6},{16,24},{18,... | collective-permute-start | bytes 1179656 | tf_op jit(solution)/shard_map/ppermute | solution.py:623
  9.3 1.5 %collective-permute-start.3 = (bf16[512,384]{1,0:T(8,128)(2,1)}, bf16[512,384]{1,0:T(8,128)(2,1)S(1)}, u32[]{:S(2)}, u32[]{:S(2)}) collective-permute-start(bf16[512,384]{1,0:T(8,128)(2,1)} %get-tuple-element.21.refs_0_), channel_id=1, source_target_pairs={{0,4},{2,6},{4,0},{6,2},{8,12},{10,14},{12,8},{14,10},{16,20},{18,... | collective-permute-start | bytes 1179656 | tf_op jit(solution)/shard_map/ppermute | solution.py:623
  10.9 0.9 %copy-done.1 = bf16[272,384]{1,0:T(8,128)(2,1)S(1)} copy-done((bf16[272,384]{1,0:T(8,128)(2,1)S(1)}, bf16[272,384]{1,0:T(8,128)(2,1)}, u32[]{:S(2)}) %copy-start.1) | copy-done | bytes 208920
  11.9 0.7 %biases.2._.bias = f32[4,256,256]{2,1,0:T(8,128)S(1)} custom-call(s32[8]{0:T(128)S(1)} %stack.32.ids, s32[16]{0:T(128)S(1)} %copy-done.4, bf16[272,384]{1,0:T(8,128)(2,1)S(1)} %copy-done.1, bf16[272,384]{1,0:T(8,128)(2,1)S(1)} %copy-done.1), custom_call_target="tpu_custom_call" | custom-call | tf_op jit(solution)/shard_map/biases/pallas_call | solution.py:275
  12.6 0.8 %tables.1 = (bf16[384,128]{1,0:T(8,128)(2,1)S(1)}, bf16[384,128]{1,0:T(8,128)(2,1)S(1)}) custom-call(s32[8]{0:T(128)S(1)} %stack.32.ids, s32[16]{0:T(128)S(1)} %copy-done.4, f32[4,256,256]{2,1,0:T(8,128)S(1)} %biases.2._.bias), custom_call_target="tpu_custom_call" | custom-call | tf_op jit(solution)/shard_map/tables/pallas_call | solution.py:242
  13.4 0.5 attend_first.1._.refs_2_
  13.9 2.7 %collective-permute-start = (bf16[272,384]{1,0:T(8,128)(2,1)S(1)}, bf16[272,384]{1,0:T(8,128)(2,1)S(1)}, u32[]{:S(2)}, u32[]{:S(2)}) collective-permute-start(bf16[272,384]{1,0:T(8,128)(2,1)S(1)} %copied.1), channel_id=1, source_target_pairs={{0,16},{2,18},{4,20},{6,22},{8,24},{10,26},{12,28},{14,30},{16,0},... | collective-permute-start | bytes 626696 | tf_op jit(solution)/shard_map/ppermute | solution.py:623
  16.5 1.1 %columns.1 = bf16[1,384,1536]{2,1,0:T(8,128)(2,1)} custom-call(bf16[384,3072]{1,0:T(8,128)(2,1)S(1)} %copy-done, f32[3,256,256]{2,1,0:T(8,128)S(1)} %attend_first.1._.refs_2_), custom_call_target="tpu_custom_call" | custom-call | tf_op jit(solution)/shard_map/columns/pallas_call | solution.py:159
  17.7 1.6 %collective-permute-start.10 = (bf16[1,384,1536]{2,1,0:T(8,128)(2,1)}, bf16[1,384,1536]{2,1,0:T(8,128)(2,1)}, u32[]{:S(2)}, u32[]{:S(2)}) collective-permute-start(bf16[1,384,1536]{2,1,0:T(8,128)(2,1)} %columns.1), channel_id=1, source_target_pairs={{0,1},{1,0},{2,3},{3,2},{4,5},{5,4},{6,7},{7,6},{8,9},{9,8},{10,11... | collective-permute-start | bytes 3538952 | tf_op jit(solution)/shard_map/ppermute | solution.py:626
  19.2 0.7 %biases.3.bias._.second_bias = f32[4,256,256]{2,1,0:T(8,128)S(1)} custom-call(s32[8]{0:T(128)S(1)} %stack.32.ids, s32[16]{0:T(128)S(1)} %copy-done.4, bf16[272,384]{1,0:T(8,128)(2,1)S(1)} %collective-permute-done.1.queries.second, f32[3,256,256]{2,1,0:T(8,128)S(1)} %attend_first.1._.refs_2_), custom_call_target="tpu_custom_call" | custom-call | tf_op jit(solution)/shard_map/biases/pallas_call | solution.py:275
  19.9 0.5 sibling_first.1.refs_2_
  20.4 0.5 collective-permute-done.2.refs_0_
  21.3 3.3 %collective-permute-start.5 = (bf16[288,384]{1,0:T(8,128)(2,1)S(1)}, bf16[288,384]{1,0:T(8,128)(2,1)S(1)}, u32[]{:S(2)}, u32[]{:S(2)}) collective-permute-start(bf16[288,384]{1,0:T(8,128)(2,1)S(1)} %slice.6), channel_id=1, source_target_pairs={{0,4},{2,6},{4,0},{6,2},{8,12},{10,14},{12,8},{14,10},{16,20},{18,... | collective-permute-start | bytes 663560 | tf_op jit(solution)/shard_map/ppermute | solution.py:623
  24.6 0.7 %sibling_second.1._.refs_3_ = f32[3,256,256]{2,1,0:T(8,128)S(1)} custom-call(f32[4,256,256]{2,1,0:T(8,128)S(1)} %biases.3.bias._.second_bias, bf16[272,384]{1,0:T(8,128)(2,1)S(1)} %collective-permute-done.1.queries.second, f32[4,256,256]{2,1,0:T(8,128)S(1)} %biases.3.bias._.second_bias, bf16[512,384]{1,0:T(8,128)(2,1)S(1)} %get-tuple-element.22.refs_0_.refs_1_, ...), custom_call_target="tpu_custom_call" | custom-call | tf_op jit(solution)/shard_map/sibling_second/pallas_call | solution.py:398
  25.3 0.7 %attend_second.1._.refs_2_ = f32[3,256,256]{2,1,0:T(8,128)S(1)} custom-call(f32[4,256,256]{2,1,0:T(8,128)S(1)} %biases.2._.bias, bf16[272,384]{1,0:T(8,128)(2,1)S(1)} %copy-done.2, f32[3,256,256]{2,1,0:T(8,128)S(1)} %sibling_second.1._.refs_3_, bf16[512,384]{1,0:T(8,128)(2,1)S(1)} %get-tuple-element.22.refs_0_.refs_1_, ...), custom_call_target="tpu_custom_call" | custom-call | tf_op jit(solution)/shard_map/attend_second/pallas_call | solution.py:398
  26.0 1.1 %collective-permute-done.array = bf16[272,384]{1,0:T(8,128)(2,1)S(1)} collective-permute-done((bf16[272,384]{1,0:T(8,128)(2,1)S(1)}, bf16[272,384]{1,0:T(8,128)(2,1)S(1)}, u32[]{:S(2)}, u32[]{:S(2)}) %collective-permute-start) | collective-permute-done | bytes 208928 | tf_op jit(solution)/shard_map/ppermute | solution.py:623
  27.2 1.1 %other_first.1 = (f32[3,256,256]{2,1,0:T(8,128)S(1)}, f32[4,256,256]{2,1,0:T(8,128)S(1)}) custom-call(bf16[384,128]{1,0:T(8,128)(2,1)S(1)} %get-tuple-element.19.table, bf16[272,384]{1,0:T(8,128)(2,1)S(1)} %gate.1.queries, f32[3,256,256]{2,1,0:T(8,128)S(1)} %attend_second.1._.refs_2_, bf16[512,384]{1,0:T(8,128)(2,1)S(1)} %copy-done.3, ...), custom_call_target="tpu_custom_call" | custom-call | tf_op jit(solution)/shard_map/other_first/pallas_call | solution.py:340
  28.2 0.4 collective-permute-done.4.queries.first
  28.6 1.1 %other_sibling_first.1 = (f32[3,256,256]{2,1,0:T(8,128)S(1)}, f32[4,256,256]{2,1,0:T(8,128)S(1)}) custom-call(bf16[384,128]{1,0:T(8,128)(2,1)S(1)} %get-tuple-element.20._.table, bf16[272,384]{1,0:T(8,128)(2,1)S(1)} %collective-permute-done.4.queries.first, f32[3,256,256]{2,1,0:T(8,128)S(1)} %get-tuple-element.25._.refs_2_, bf16[512,384]{1,0:T(8,128)(2,1)S(1)} %copy-done.3, ...), custom_call_target="tpu_custom_call" | custom-call | tf_op jit(solution)/shard_map/other_sibling_first/pallas_call | solution.py:340
  29.8 0.8 %attend_pair.1._ = bf16[544,384]{1,0:T(8,128)(2,1)S(1)} custom-call(f32[4,256,256]{2,1,0:T(8,128)S(1)} %get-tuple-element.26.first_bias, bf16[272,384]{1,0:T(8,128)(2,1)S(1)} %collective-permute-done.4.queries.first, f32[4,256,256]{2,1,0:T(8,128)S(1)} %biases.3.bias._.second_bias, bf16[272,384]{1,0:T(8,128)(2,1)S(1)} %collective-permute-done.1.queries.second, ...), custom_call_target="tpu_custom_call" | custom-call | tf_op jit(solution)/shard_map/attend_pair/pallas_call | solution.py:377
  30.6 0.5 other_last.1._.kept
  31.1 0.5 attend_last.1.refs_1_.kept
  31.6 0.7 %collective-permute-done.7.refs_0_ = bf16[544,384]{1,0:T(8,128)(2,1)S(1)} collective-permute-done((bf16[544,384]{1,0:T(8,128)(2,1)S(1)}, bf16[544,384]{1,0:T(8,128)(2,1)S(1)}, u32[]{:S(2)}, u32[]{:S(2)}) %collective-permute-start.7) | collective-permute-done | bytes 417824 | tf_op jit(solution)/shard_map/ppermute | solution.py:623
  32.7 2.3 %collective-permute-start.8 = (bf16[272,384]{1,0:T(8,128)(2,1)S(1)}, bf16[272,384]{1,0:T(8,128)(2,1)S(1)}, u32[]{:S(2)}, u32[]{:S(2)}) collective-permute-start(bf16[272,384]{1,0:T(8,128)(2,1)S(1)} %join.1._), channel_id=1, source_target_pairs={{0,16},{2,18},{4,20},{6,22},{8,24},{10,26},{12,28},{14,30},{16,0},... | collective-permute-start | bytes 626696 | tf_op jit(solution)/shard_map/ppermute | solution.py:623
  35.0 0.7 %row_sums.1.refs_2_.sums = bf16[16,384]{1,0:T(8,128)(2,1)S(1)} custom-call(bf16[384,3072]{1,0:T(8,128)(2,1)S(1)} %copy-done, bf16[272,384]{1,0:T(8,128)(2,1)S(1)} %join.1._), custom_call_target="tpu_custom_call" | custom-call | tf_op jit(solution)/shard_map/row_sums/pallas_call | solution.py:183
  35.7 9.6 %collective-permute-done.8.refs_1_ = bf16[272,384]{1,0:T(8,128)(2,1)S(1)} collective-permute-done((bf16[272,384]{1,0:T(8,128)(2,1)S(1)}, bf16[272,384]{1,0:T(8,128)(2,1)S(1)}, u32[]{:S(2)}, u32[]{:S(2)}) %collective-permute-start.8) | collective-permute-done | bytes 208928 | tf_op jit(solution)/shard_map/ppermute | solution.py:623
  45.6 1.5 %collective-permute-start.9 = (bf16[256,384]{1,0:T(8,128)(2,1)S(1)}, bf16[256,384]{1,0:T(8,128)(2,1)S(1)}, u32[]{:S(2)}, u32[]{:S(2)}) collective-permute-start(bf16[256,384]{1,0:T(8,128)(2,1)S(1)} %finish.1.own), channel_id=1, source_target_pairs={{0,1},{1,0},{2,3},{3,2},{4,5},{5,4},{6,7},{7,6},{8,9},{9,8},{10,11... | collective-permute-start | bytes 589832 | tf_op jit(solution)/shard_map/ppermute | solution.py:626
  47.1 0.6 %collective-permute-start.11 = (bf16[16,384]{1,0:T(8,128)(2,1)S(1)}, bf16[16,384]{1,0:T(8,128)(2,1)S(1)}, u32[]{:S(2)}, u32[]{:S(2)}) collective-permute-start(bf16[16,384]{1,0:T(8,128)(2,1)S(1)} %row_sums.1.refs_2_.sums), channel_id=1, source_target_pairs={{0,1},{1,0},{2,3},{3,2},{4,5},{5,4},{6,7},{7,6},{8,9},{9,8},{10,11... | collective-permute-start | bytes 36872 | tf_op jit(solution)/shard_map/ppermute | solution.py:626
  47.7 1.9 %project_early.1 = (f32[256,1536]{1,0:T(8,128)S(1)}, f32[8,256]{1,0:T(8,128)S(1)}, f32[1,8,256]{2,1,0:T(8,128)S(1)}, bf16[1,384,1536]{2,1,0:T(8,128)(2,1)S(1)}) custom-call(s32[1]{0:T(128)} %bitcast.7.place, bf16[256,384]{1,0:T(8,128)(2,1)S(1)} %finish.1.own, bf16[384,3072]{1,0:T(8,128)(2,1)S(1)} %copy-done, bf16[16,384]{1,0:T(8,128)(2,1)S(1)} %row_sums.1.refs_2_.sums, ...), custom_call_target="tpu_custom_call" | custom-call | tf_op jit(solution)/shard_map/project_early/pallas_call | solution.py:535
  49.6 2.4 %collective-permute-done.11.refs_2_ = bf16[16,384]{1,0:T(8,128)(2,1)S(1)} collective-permute-done((bf16[16,384]{1,0:T(8,128)(2,1)S(1)}, bf16[16,384]{1,0:T(8,128)(2,1)S(1)}, u32[]{:S(2)}, u32[]{:S(2)}) %collective-permute-start.11) | collective-permute-done | bytes 12320 | tf_op jit(solution)/shard_map/ppermute | solution.py:626
  52.1 1.4 %project_last.1 = (bf16[256,1536]{1,0:T(8,128)(2,1)}, f32[1,256]{1,0:T(1,128)}) custom-call(bf16[256,384]{1,0:T(8,128)(2,1)S(1)} %collective-permute-done.9.refs_0_, bf16[1,384,1536]{2,1,0:T(8,128)(2,1)S(1)} %get-tuple-element.28.refs_1_, bf16[16,384]{1,0:T(8,128)(2,1)S(1)} %collective-permute-done.11.refs_2_, f32[256,1536]{1,0:T(8,128)S(1)} %get-tuple-element.29.refs_3_, ...), custom_call_target="tpu_custom_call" | custom-call | tf_op jit(solution)/shard_map/project_last/pallas_call | solution.py:592
  (27 shorter events, 1.4 us)
Async XLA Ops:
  0.6 10.3 %copy-start.4 = (s32[16]{0:T(128)S(1)}, s32[16]{0:T(128)}, u32[]{:S(2)}) copy-start(s32[16]{0:T(128)} %window.5) | copy-start | bytes 196
  6.2 14.7 %collective-permute-start.2 = (bf16[512,384]{1,0:T(8,128)(2,1)}, bf16[512,384]{1,0:T(8,128)(2,1)S(1)}, u32[]{:S(2)}, u32[]{:S(2)}) collective-permute-start(bf16[512,384]{1,0:T(8,128)(2,1)} %get-tuple-element.21.refs_0_), channel_id=1, source_target_pairs={{0,8},{2,10},{4,12},{6,14},{8,0},{10,2},{12,4},{14,6},{16,24},{18,... | collective-permute-start | bytes 1179656 | tf_op jit(solution)/shard_map/ppermute | solution.py:623
  9.3 11.6 %collective-permute-start.3 = (bf16[512,384]{1,0:T(8,128)(2,1)}, bf16[512,384]{1,0:T(8,128)(2,1)S(1)}, u32[]{:S(2)}, u32[]{:S(2)}) collective-permute-start(bf16[512,384]{1,0:T(8,128)(2,1)} %get-tuple-element.21.refs_0_), channel_id=1, source_target_pairs={{0,4},{2,6},{4,0},{6,2},{8,12},{10,14},{12,8},{14,10},{16,20},{18,... | collective-permute-start | bytes 1179656 | tf_op jit(solution)/shard_map/ppermute | solution.py:623
  10.8 8.4 %collective-permute-start.1 = (bf16[272,384]{1,0:T(8,128)(2,1)}, bf16[272,384]{1,0:T(8,128)(2,1)S(1)}, u32[]{:S(2)}, u32[]{:S(2)}) collective-permute-start(bf16[272,384]{1,0:T(8,128)(2,1)} %get-tuple-element.18.queries._.array), channel_id=1, source_target_pairs={{0,2},{2,0},{4,6},{6,4},{8,10},{10,8},{12,14},{14,12},{16,18},{18,... | collective-permute-start | bytes 626696 | tf_op jit(solution)/shard_map/ppermute | solution.py:623
  10.9 0.9 %copy-start.1 = (bf16[272,384]{1,0:T(8,128)(2,1)S(1)}, bf16[272,384]{1,0:T(8,128)(2,1)}, u32[]{:S(2)}) copy-start(bf16[272,384]{1,0:T(8,128)(2,1)} %get-tuple-element.18.queries._.array) | copy-start | bytes 626692
  11.9 1.5 %copy-start.2 = (bf16[272,384]{1,0:T(8,128)(2,1)S(1)}, bf16[272,384]{1,0:T(8,128)(2,1)}, u32[]{:S(2)}) copy-start(bf16[272,384]{1,0:T(8,128)(2,1)} %get-tuple-element.18.queries._.array) | copy-start | bytes 626692
  11.9 1.5 %copy-start.3 = (bf16[512,384]{1,0:T(8,128)(2,1)S(1)}, bf16[512,384]{1,0:T(8,128)(2,1)}, u32[]{:S(2)}) copy-start(bf16[512,384]{1,0:T(8,128)(2,1)} %get-tuple-element.21.refs_0_) | copy-start | bytes 1179652
  13.4 3.2 %copy-start = (bf16[384,3072]{1,0:T(8,128)(2,1)S(1)}, bf16[384,3072]{1,0:T(8,128)(2,1)}, u32[]{:S(2)}) copy-start(bf16[384,3072]{1,0:T(8,128)(2,1)} %w_out.5) | copy-start | bytes 7077892
  13.9 13.2 %collective-permute-start = (bf16[272,384]{1,0:T(8,128)(2,1)S(1)}, bf16[272,384]{1,0:T(8,128)(2,1)S(1)}, u32[]{:S(2)}, u32[]{:S(2)}) collective-permute-start(bf16[272,384]{1,0:T(8,128)(2,1)S(1)} %copied.1), channel_id=1, source_target_pairs={{0,16},{2,18},{4,20},{6,22},{8,24},{10,26},{12,28},{14,30},{16,0},... | collective-permute-start | bytes 626696 | tf_op jit(solution)/shard_map/ppermute | solution.py:623
  17.7 30.0 %collective-permute-start.10 = (bf16[1,384,1536]{2,1,0:T(8,128)(2,1)}, bf16[1,384,1536]{2,1,0:T(8,128)(2,1)}, u32[]{:S(2)}, u32[]{:S(2)}) collective-permute-start(bf16[1,384,1536]{2,1,0:T(8,128)(2,1)} %columns.1), channel_id=1, source_target_pairs={{0,1},{1,0},{2,3},{3,2},{4,5},{5,4},{6,7},{7,6},{8,9},{9,8},{10,11... | collective-permute-start | bytes 3538952 | tf_op jit(solution)/shard_map/ppermute | solution.py:626
  21.1 8.7 %collective-permute-start.6 = (bf16[304,384]{1,0:T(8,128)(2,1)S(1)}, bf16[304,384]{1,0:T(8,128)(2,1)S(1)}, u32[]{:S(2)}, u32[]{:S(2)}) collective-permute-start(bf16[304,384]{1,0:T(8,128)(2,1)S(1)} %slice.7), channel_id=1, source_target_pairs={{0,8},{2,10},{4,12},{6,14},{8,0},{10,2},{12,4},{14,6},{16,24},{18,... | collective-permute-start | bytes 700424 | tf_op jit(solution)/shard_map/ppermute | solution.py:623
  21.3 8.4 %collective-permute-start.5 = (bf16[288,384]{1,0:T(8,128)(2,1)S(1)}, bf16[288,384]{1,0:T(8,128)(2,1)S(1)}, u32[]{:S(2)}, u32[]{:S(2)}) collective-permute-start(bf16[288,384]{1,0:T(8,128)(2,1)S(1)} %slice.6), channel_id=1, source_target_pairs={{0,4},{2,6},{4,0},{6,2},{8,12},{10,14},{12,8},{14,10},{16,20},{18,... | collective-permute-start | bytes 663560 | tf_op jit(solution)/shard_map/ppermute | solution.py:623
  27.1 1.5 %collective-permute-start.4 = (bf16[272,384]{1,0:T(8,128)(2,1)S(1)}, bf16[272,384]{1,0:T(8,128)(2,1)S(1)}, u32[]{:S(2)}, u32[]{:S(2)}) collective-permute-start(bf16[272,384]{1,0:T(8,128)(2,1)S(1)} %gate.1.queries), channel_id=1, source_target_pairs={{0,2},{2,0},{4,6},{6,4},{8,10},{10,8},{12,14},{14,12},{16,18},{18,... | collective-permute-start | bytes 626696 | tf_op jit(solution)/shard_map/ppermute | solution.py:623
  30.5 1.8 %collective-permute-start.7 = (bf16[544,384]{1,0:T(8,128)(2,1)S(1)}, bf16[544,384]{1,0:T(8,128)(2,1)S(1)}, u32[]{:S(2)}, u32[]{:S(2)}) collective-permute-start(bf16[544,384]{1,0:T(8,128)(2,1)S(1)} %attend_pair.1._), channel_id=1, source_target_pairs={{0,2},{2,0},{4,6},{6,4},{8,10},{10,8},{12,14},{14,12},{16,18},{18,... | collective-permute-start | bytes 1253384 | tf_op jit(solution)/shard_map/ppermute | solution.py:623
  32.7 12.6 %collective-permute-start.8 = (bf16[272,384]{1,0:T(8,128)(2,1)S(1)}, bf16[272,384]{1,0:T(8,128)(2,1)S(1)}, u32[]{:S(2)}, u32[]{:S(2)}) collective-permute-start(bf16[272,384]{1,0:T(8,128)(2,1)S(1)} %join.1._), channel_id=1, source_target_pairs={{0,16},{2,18},{4,20},{6,22},{8,24},{10,26},{12,28},{14,30},{16,0},... | collective-permute-start | bytes 626696 | tf_op jit(solution)/shard_map/ppermute | solution.py:623
  45.6 6.4 %collective-permute-start.9 = (bf16[256,384]{1,0:T(8,128)(2,1)S(1)}, bf16[256,384]{1,0:T(8,128)(2,1)S(1)}, u32[]{:S(2)}, u32[]{:S(2)}) collective-permute-start(bf16[256,384]{1,0:T(8,128)(2,1)S(1)} %finish.1.own), channel_id=1, source_target_pairs={{0,1},{1,0},{2,3},{3,2},{4,5},{5,4},{6,7},{7,6},{8,9},{9,8},{10,11... | collective-permute-start | bytes 589832 | tf_op jit(solution)/shard_map/ppermute | solution.py:626
  47.1 5.0 %collective-permute-start.11 = (bf16[16,384]{1,0:T(8,128)(2,1)S(1)}, bf16[16,384]{1,0:T(8,128)(2,1)S(1)}, u32[]{:S(2)}, u32[]{:S(2)}) collective-permute-start(bf16[16,384]{1,0:T(8,128)(2,1)S(1)} %row_sums.1.refs_2_.sums), channel_id=1, source_target_pairs={{0,1},{1,0},{2,3},{3,2},{4,5},{5,4},{6,7},{7,6},{8,9},{9,8},{10,11... | collective-permute-start | bytes 36872 | tf_op jit(solution)/shard_map/ppermute | solution.py:626
